TPU v7x, 32 devices: a whole 2x2x4 slice. The times are simulated.
32 devices in a mesh: chain: 2 (over y), dp: 8 (over z, x), rep: 2 (over core).
Axes of the slice: x: 2, y: 2, z: 4, core: 2. Of those that a mesh axis runs over, the one named last changes fastest.
Arguments:
- descriptors: float32 [2, 32, 128, 256], P(None, ('dp', 'rep')), may hold values from -6 to 6
- counts: int32 [2, 32], P(None, ('dp', 'rep')), may hold values from 0 to 128, as said below
- struct_ids: int32 [2, 32, 128], P(None, ('dp', 'rep')), may hold values from 0 to 31
- ref_energy: float32 [512], P(('dp', 'rep')), may hold values from -9 to 9
- first_layer: float32 [4, 131072], P('chain', ('dp', 'rep')), parts along dimension 0, may hold values from -0.375 to 0.375
- second_layer: float32 [4, 262144], P('chain', ('dp', 'rep')), parts along dimension 0, may hold values from -0.25 to 0.25
- vectors: float32 [4, 3, 512], P('chain'), parts along dimension 0, may hold values from -0.6 to 0.6
- first_momentum: float32 [4, 131072], P('chain', ('dp', 'rep')), parts along dimension 0, may hold values from -6 to 6
- second_momentum: float32 [4, 262144], P('chain', ('dp', 'rep')), parts along dimension 0, may hold values from -6 to 6
- vector_momentum: float32 [4, 3, 512], P('chain'), parts along dimension 0, may hold values from -6 to 6
Outputs:
- new_first: float32 [4, 131072], P('chain', ('dp', 'rep')), parts along dimension 0
- new_second: float32 [4, 262144], P('chain', ('dp', 'rep')), parts along dimension 0
- new_vectors: float32 [4, 3, 512], P('chain'), parts along dimension 0
- new_first_mom: float32 [4, 131072], P('chain', ('dp', 'rep')), parts along dimension 0
- new_second_mom: float32 [4, 262144], P('chain', ('dp', 'rep')), parts along dimension 0
- new_vector_mom: float32 [4, 3, 512], P('chain'), parts along dimension 0
- potential: float32 [2], P('chain'), parts along dimension 0
- force_partials: float32 [4, 32, 128, 256], P('chain', ('dp', 'rep')), parts along dimension 0
There are 2 independent parts, one for each index of `chain`. A program takes and returns all parts, laid end to end along the dimension named above; an argument that names none is the same for every part. Nothing has to cross between parts.
Inputs may be any that keep to these rules, and one draw needn't show every extreme that they name: `counts`: in each element, the 2 block slots of one device hold their blocks with atoms first; each such block but the last holds 128 atoms, the later slots hold 0. For each element and each device d below 8 along dp+rep, devices d and d + 8 hold at most 2 blocks with atoms together, and this is reached by some pair in every draw.
All inputs are finite; a program needn't handle non-finite values.
Results may differ from a plain program's by a relative error of at most 0.0003.
Values sent between devices are 32-bit elements; how exact they have to be, the bound alone decides.
No kernel may reach another device: no remote copies, remote signals or barrier semaphores. Data moves between devices by JAX's collectives and lax.ppermute only.
A program may use at most 192 MiB of HBM per device.

v0:
```python
import jax
import jax.numpy as jnp
from jax import lax
from jax.sharding import PartitionSpec as P

NOISE_VAR = 0.1
STEP_SIZE = 0.01
HIGH = lax.Precision.HIGHEST


def element_energies(first, second, vectors, desc):
    lower = jnp.einsum("erf,efj->erj", desc, first, precision=HIGH) + vectors[:, 0][:, None, :]
    hidden = jnp.tanh(lower)
    upper = jnp.einsum("erj,ejk->erk", hidden, second, precision=HIGH) + vectors[:, 1][:, None, :]
    top = jnp.tanh(upper)
    return jnp.einsum("erk,ek->er", top, vectors[:, 2], precision=HIGH)


def structure_terms(energies, live, ids, refs):
    member = (
        ids[..., None] == jnp.arange(refs.shape[0], dtype=jnp.int32)[None, None, None, :]
    ).astype(jnp.float32)
    total = jnp.einsum("ebas,eba->s", member, energies, precision=HIGH)
    count = jnp.maximum(jnp.einsum("ebas,eba->s", member, live, precision=HIGH), 1.0)
    error = total / count - refs
    potential_part = jnp.sum(error * error) / (2.0 * NOISE_VAR)
    scale = error / count / NOISE_VAR
    adjoint = jnp.einsum("ebas,s->eba", member, scale, precision=HIGH) * live
    return (potential_part, adjoint)


def on_device(
    descriptors,
    counts,
    struct_ids,
    ref_energy,
    first_layer,
    second_layer,
    vectors,
    first_momentum,
    second_momentum,
    vector_momentum,
):
    nelem, slots, atoms, width = descriptors.shape
    hidden_width = vectors.shape[2]
    flat_first, flat_second = (
        lax.all_gather(first_layer, ("dp", "rep"), axis=1, tiled=True),
        lax.all_gather(second_layer, ("dp", "rep"), axis=1, tiled=True),
    )
    params = (
        flat_first.reshape(nelem, width, hidden_width),
        flat_second.reshape(nelem, hidden_width, hidden_width),
        vectors,
    )
    positions = jnp.arange(atoms, dtype=jnp.int32)
    live = (positions[None, None, :] < counts[:, :, None]).astype(jnp.float32)

    def forward(block):
        number = block.shape[1]

        def energy_fn(weights, pieces):
            flat = pieces.reshape(nelem, number * atoms, width)
            return element_energies(weights[0], weights[1], weights[2], flat).reshape(
                nelem, number, atoms
            )

        return jax.vjp(energy_fn, params, block)

    raw, pull = forward(descriptors)
    potential_part, adjoint = structure_terms(raw * live, live, struct_ids, ref_energy)
    grads, force_partials = pull(adjoint)
    grad_first = grads[0].reshape(nelem, width * hidden_width)
    grad_second = grads[1].reshape(nelem, hidden_width * hidden_width)
    sum_first, sum_second, grad_vectors, potential_sum = lax.psum(
        (grad_first, grad_second, grads[2], potential_part), ("dp", "rep")
    )
    position = lax.axis_index(("dp", "rep"))
    share_first = lax.dynamic_slice_in_dim(
        sum_first, position * first_layer.shape[1], first_layer.shape[1], 1
    )
    share_second = lax.dynamic_slice_in_dim(
        sum_second, position * second_layer.shape[1], second_layer.shape[1], 1
    )
    new_first_mom = first_momentum - STEP_SIZE * share_first
    new_second_mom = second_momentum - STEP_SIZE * share_second
    new_vector_mom = vector_momentum - STEP_SIZE * grad_vectors
    new_first = first_layer + STEP_SIZE * new_first_mom
    new_second = second_layer + STEP_SIZE * new_second_mom
    new_vectors = vectors + STEP_SIZE * new_vector_mom
    potential = (potential_sum / (ref_energy.shape[0] * lax.axis_size(("dp", "rep")))).reshape(1)
    return (
        new_first,
        new_second,
        new_vectors,
        new_first_mom,
        new_second_mom,
        new_vector_mom,
        potential,
        force_partials,
    )


def solution(mesh):
    placed = (
        P(None, ("dp", "rep"), None, None),
        P(None, ("dp", "rep")),
        P(None, ("dp", "rep"), None),
        P(("dp", "rep")),
        P("chain", ("dp", "rep")),
        P("chain", ("dp", "rep")),
        P("chain", None, None),
        P("chain", ("dp", "rep")),
        P("chain", ("dp", "rep")),
        P("chain", None, None),
    )
    return jax.shard_map(
        on_device,
        mesh=mesh,
        in_specs=placed,
        out_specs=(
            P("chain", ("dp", "rep")),
            P("chain", ("dp", "rep")),
            P("chain", None, None),
            P("chain", ("dp", "rep")),
            P("chain", ("dp", "rep")),
            P("chain", None, None),
            P("chain"),
            P("chain", ("dp", "rep"), None, None),
        ),
        check_vma=False,
    )
```

profile of v0, /device:TPU:0, one launch (start us, length us, event | category | flops | bytes accessed | tf_op | source)
XLA Modules:
  0.0 228.9 jit_solution(13092734360983376674)
XLA Ops:
  7.2 0.0 copy-start
  7.2 0.0 all-gather.3.cloned.1.call-start
  7.2 0.7 all-gather.3.cloned.1.call-update
  7.9 0.0 all-gather.5.cloned.1.call-start
  8.0 0.7 all-gather.5.cloned.1.call-update
  8.7 0.0 all-reduce.7.cloned.1.call-start
  8.7 0.8 fusion.32
  9.5 0.9 fusion.18
  10.4 0.7 slice_bitcast_fusion.2
  11.1 39.7 %all-gather.3.cloned.1.call-done = f32[2,131072]{1,0:T(2,128)} async-done(((f32[2,8192]{1,0:T(2,128)}), f32[2,131072]{1,0:T(2,128)}) %all-gather.3.cloned.1.call-update) | async-done | bytes 1048592 | tf_op jit(solution)/shard_map/all_gather | solution.py:47
  50.8 0.0 copy-done
  50.8 2.4 %fusion.15 = f32[2,256,512]{2,1,0:T(8,128)S(1)} fusion(f32[2,256,256]{2,1,0:T(8,128)S(1)} %bitcast.84, f32[1,2,256,512]{3,1,2,0:T(2,128)} %bitcast.89, f32[2,512]{1,0:T(2,128)S(1)} %get-tuple-element.20), kind=kOutput, calls=%fused_computation.11 | convolution fusion | flops 805568512 | bytes 2625536 | tf_op jit(solution)/shard_map/jvp(erf,efj->erj)/dot_general | solution.py:12
  53.3 40.1 %all-gather.5.cloned.1.call-done = f32[2,262144]{1,0:T(2,128)} async-done(((f32[2,16384]{1,0:T(2,128)}), f32[2,262144]{1,0:T(2,128)}) %all-gather.5.cloned.1.call-update) | async-done | bytes 2097168 | tf_op jit(solution)/shard_map/all_gather | solution.py:48
  93.4 0.0 copy-start.8
  93.4 0.0 copy-start.10
  93.4 0.0 copy-start.11
  93.4 3.8 %fusion.9 = f32[2,256,512]{2,1,0:T(8,128)S(1)} fusion(f32[2,256,512]{2,1,0:T(8,128)S(1)} %fusion.15, f32[1,2,512,512]{3,1,2,0:T(2,128)} %bitcast.86, f32[2,512]{1,0:T(2,128)S(1)} %get-tuple-element.19), kind=kOutput, calls=%fused_computation.8 | convolution fusion | flops 1610874880 | bytes 4198400 | tf_op jit(solution)/shard_map/jvp(erj,ejk->erk)/dot_general | solution.py:14
  97.2 1.0 fusion.28
  98.2 0.0 copy-done.8
  98.2 0.1 select_bitcast_fusion
  98.3 0.0 copy-done.10
  98.3 0.0 copy-done.11
  98.3 0.9 multiply_reduce_fusion
  99.2 0.3 fusion.30
  99.5 0.1 fusion.52
  99.5 3.9 %fusion.41 = (f32[2,512]{1,0:T(2,128)S(1)}, f32[2,256,512]{2,1,0:T(8,128)S(1)}) fusion(f32[2,256,512]{2,1,0:T(8,128)S(1)} %fusion.15, f32[1,2,512,512]{3,1,2,0:T(2,128)} %bitcast.87, f32[2,256,512]{2,1,0:T(8,128)S(1)} %fusion.9, f32[2,512]{1,0:T(2,128)S(1)} %get-tuple-element.21, f32[2,256]{1,0:T(2,128)S(1)} %bitcast.94), kind=kOutput, calls=%fused_computation.58 | convolution fusion | flops 1613233152 | bytes 5253120 | tf_op jit(solution)/shard_map/transpose(jvp(erj,ejk->erk))/dot_general | solution.py:14
  103.4 0.0 copy-start.1
  103.4 2.2 convolution_bitcast_fusion
  105.6 3.0 %copy.40 = f32[1,2,512,512]{3,1,2,0:T(2,128)} copy(f32[1,2,512,512]{3,2,1,0:T(8,128)S(1)} %convolution_bitcast_fusion) | data formatting | bytes 4194304
  108.6 0.0 copy-done.1
  108.6 3.0 %convolution_bitcast_fusion.1 = f32[2,256,512]{1,2,0:T(8,128)} fusion(f32[2,256,512]{2,1,0:T(8,128)S(1)} %get-tuple-element.23, f32[2,256,256]{2,1,0:T(8,128)S(1)} %bitcast.85), kind=kOutput, calls=%fused_computation.12 | convolution fusion | flops 805306368 | bytes 2621440 | tf_op jit(solution)/shard_map/transpose(jvp(erf,efj->erj))/dot_general | solution.py:12
  111.6 1.6 copy.21
  113.2 1.8 copy.39
  115.0 0.0 copy-start.7
  115.0 0.0 copy-start.9
  115.0 0.0 copy-start.2
  115.0 0.0 all-reduce.7.cloned.1.call-update
  115.1 0.1 fusion.31
  115.1 0.6 fusion.42
  115.7 0.0 copy-start.4
  115.7 0.0 copy-start.6
  115.7 0.0 copy-start.3
  115.8 0.0 copy-start.5
  116.5 0.2 fusion.24
  116.7 60.3 %all-reduce.3 = (f32[2,3,512]{2,0,1:T(2,128)S(1)}, f32[]{:T(128)}) all-reduce(f32[2,3,512]{2,0,1:T(2,128)S(1)} %pad_add_fusion, f32[]{:T(128)S(6)} %div.22), channel_id=1, replica_groups=mesh['chain'=2,'dp'=8,'rep'=2] {'dp','rep'}, use_global_device_ids=true, to_apply=%region_4.0 | all-reduce | flops 3073 | bytes 24584 | tf_op jit(solution)/shard_map/psum | solution.py:74
  177.7 0.0 copy-done.7
  177.7 0.0 copy-done.9
  177.7 0.6 multiply_add_fusion.2
  178.3 0.0 copy-done.2
  178.3 3.3 %fusion.19 = f32[2,256,256]{2,1,0:T(8,128)} fusion(f32[2,256,512]{2,1,0:T(8,128)S(1)} %copy-done.2, f32[1,2,256,512]{3,1,2,0:T(2,128)} %bitcast.90), kind=kOutput, calls=%fused_computation.18 | convolution fusion | flops 805306368 | bytes 2621440 | tf_op jit(solution)/shard_map/transpose(jvp(erf,efj->erj))/dot_general | solution.py:12
  181.6 36.3 %all-reduce.7.cloned.1.call-done = (f32[2,131072]{1,0:T(2,128)}, f32[2,262144]{1,0:T(2,128)}) async-done(((f32[2,131072]{1,0:T(2,128)}, f32[2,262144]{1,0:T(2,128)}), (f32[2,131072]{1,0:T(2,128)}, f32[2,262144]{1,0:T(2,128)})) %all-reduce.7.cloned.1.call-update) | async-done | bytes 3145744 | tf_op jit(solution)/shard_map/psum | solution.py:74
  217.9 0.0 copy-done.4
  217.9 0.0 copy-done.6
  217.9 1.6 multiply_add_fusion.1
  219.5 0.0 copy-done.3
  219.5 0.0 copy-done.5
  219.5 1.8 multiply_add_fusion
  (5 shorter events, 0.0 us)
Async XLA Ops:
  7.2 43.7 %copy-start = (f32[2,2,128,256]{3,2,1,0:T(8,128)S(1)}, f32[2,2,128,256]{3,2,1,0:T(8,128)}, u32[]{:S(2)}) copy-start(f32[2,2,128,256]{3,2,1,0:T(8,128)} %param.10) | copy-start | bytes 1572868
  7.2 43.7 %all-gather.3.cloned.1.call-start = ((), (), s32[]{:S(2)}) async-start(), calls=%async_computation | async-start | bytes 1114112 | tf_op jit(solution)/shard_map/all_gather | solution.py:47
  7.9 85.4 %all-gather.5.cloned.1.call-start = ((), (), s32[]{:S(2)}) async-start(), calls=%async_computation.1 | async-start | bytes 2228224 | tf_op jit(solution)/shard_map/all_gather | solution.py:48
  8.7 209.3 %all-reduce.7.cloned.1.call-start = ((), (), s32[]{:S(2)}) async-start(), calls=%async_computation.2 | async-start | bytes 6291456 | tf_op jit(solution)/shard_map/psum | solution.py:74
  93.4 4.8 %copy-start.8 = (s32[2,2]{1,0:T(2,128)S(1)}, s32[2,2]{1,0:T(2,128)}, u32[]{:S(2)}) copy-start(s32[2,2]{1,0:T(2,128)} %param.11) | copy-start | bytes 52
  93.4 4.9 %copy-start.10 = (s32[2,2,128]{2,1,0:T(2,128)S(1)}, s32[2,2,128]{2,1,0:T(2,128)}, u32[]{:S(2)}) copy-start(s32[2,2,128]{2,1,0:T(2,128)} %param.12) | copy-start | bytes 6148
  93.4 4.9 %copy-start.11 = (f32[32]{0:T(128)S(1)}, f32[32]{0:T(128)}, u32[]{:S(2)}) copy-start(f32[32]{0:T(128)} %param.13) | copy-start | bytes 388
  103.4 5.2 %copy-start.1 = (f32[2,256,512]{2,1,0:T(8,128)}, f32[2,256,512]{2,1,0:T(8,128)S(1)}, u32[]{:S(2)}) copy-start(f32[2,256,512]{2,1,0:T(8,128)S(1)} %get-tuple-element.23) | copy-start | bytes 3145732
  115.0 62.7 %copy-start.7 = (f32[2,3,512]{2,0,1:T(2,128)S(1)}, f32[2,3,512]{2,0,1:T(2,128)}, u32[]{:S(2)}) copy-start(f32[2,3,512]{2,0,1:T(2,128)} %param.16) | copy-start | bytes 36868
  115.0 62.7 %copy-start.9 = (f32[2,3,512]{2,0,1:T(2,128)S(1)}, f32[2,3,512]{2,0,1:T(2,128)}, u32[]{:S(2)}) copy-start(f32[2,3,512]{2,0,1:T(2,128)} %param.19) | copy-start | bytes 36868
  115.0 63.3 %copy-start.2 = (f32[2,256,512]{2,1,0:T(8,128)S(1)}, f32[2,256,512]{2,1,0:T(8,128)}, u32[]{:S(2)}) copy-start(f32[2,256,512]{2,1,0:T(8,128)} %copy-done.1) | copy-start | bytes 3145732
  115.7 102.2 %copy-start.4 = (f32[2,8192]{1,0:T(2,128)S(1)}, f32[2,8192]{1,0:T(2,128)}, u32[]{:S(2)}) copy-start(f32[2,8192]{1,0:T(2,128)} %param.14) | copy-start | bytes 196612
  115.7 102.2 %copy-start.6 = (f32[2,8192]{1,0:T(2,128)S(1)}, f32[2,8192]{1,0:T(2,128)}, u32[]{:S(2)}) copy-start(f32[2,8192]{1,0:T(2,128)} %param.17) | copy-start | bytes 196612
  115.7 103.8 %copy-start.3 = (f32[2,16384]{1,0:T(2,128)S(1)}, f32[2,16384]{1,0:T(2,128)}, u32[]{:S(2)}) copy-start(f32[2,16384]{1,0:T(2,128)} %param.15) | copy-start | bytes 393220
  115.8 103.8 %copy-start.5 = (f32[2,16384]{1,0:T(2,128)S(1)}, f32[2,16384]{1,0:T(2,128)}, u32[]{:S(2)}) copy-start(f32[2,16384]{1,0:T(2,128)} %param.18) | copy-start | bytes 393220
Sparse Core Ops, SparseCore 0:
  10.2 40.6 all-gather.2
  53.0 40.3 all-gather.4
  115.2 102.7 all-reduce.6
where the time goes:
time: 229 us
  waiting for transfers between devices  117 us (51%)
  blocking collectives  60.3 us (26%)
  matrix products  22.3 us (10%)
  between operations  16.4 us (7%)
  local copies, waits for them, and re-layouts  7.15 us (3%)
  other arithmetic  5.17 us (2%)
    psum x1, blocking collectives, on_device(): lax.psum((grad_first, grad_second, grads[2], potential_part), ('dp', 'rep'))  60.3 us
    all_gather x1, waiting for transfers between devices, on_device(): lax.all_gather(second_layer, ('dp', 'rep'), axis=1, tiled=True)  40.1 us
    all_gather x1, waiting for transfers between devices, on_device(): lax.all_gather(first_layer, ('dp', 'rep'), axis=1, tiled=True)  39.7 us
    psum x1, waiting for transfers between devices, on_device(): lax.psum((grad_first, grad_second, grads[2], potential_part), ('dp', 'rep'))  36.3 us
    dot_general x3, matrix products, element_energies(): jnp.einsum('erj,ejk->erk', hidden, second, precision=HIGH)  9.84 us
    dot_general x3, matrix products, element_energies(): jnp.einsum('erf,efj->erj', desc, first, precision=HIGH)  8.74 us
    unnamed x27, local copies, waits for them, and re-layouts  4.84 us
  transfers between devices with their start and end apart: 3, of which 3 were waited for; matrix products, arithmetic and copies ran while one was open for 4% of the time, Pallas kernels for 0%

commit v1 on v0

--- a/solution.py
+++ b/solution.py
@@ -1,11 +1,299 @@
 import jax
 import jax.numpy as jnp
 from jax import lax
+from jax.experimental import pallas as pl
+from jax.experimental.pallas import tpu as pltpu
 from jax.sharding import PartitionSpec as P
 
 NOISE_VAR = 0.1
 STEP_SIZE = 0.01
 HIGH = lax.Precision.HIGHEST
+F32 = jnp.float32
+BF16 = jnp.bfloat16
+VMEM = pltpu.VMEM
+LIMIT = 32 * 1024 * 1024
+
+NT = (((1,), (1,)), ((), ()))
+TN = (((0,), (0,)), ((), ()))
+NN = (((1,), (0,)), ((), ()))
+
+
+def split(x):
+    high = x.astype(BF16)
+    return high, (x - high.astype(F32)).astype(BF16)
+
+
+def product(left, right, dims):
+    one = lambda a, b: lax.dot_general(a, b, dims, preferred_element_type=F32)
+    return one(left[0], right[0]) + (one(left[0], right[1]) + one(left[1], right[0]))
+
+
+def call(kernel, outs, args, scratch=(), flops=0, size=0, name=None):
+    return pl.pallas_call(
+        kernel,
+        out_shape=[jax.ShapeDtypeStruct(shape, F32) for shape in outs],
+        in_specs=[pl.BlockSpec(memory_space=VMEM)] * len(args),
+        out_specs=[pl.BlockSpec(memory_space=VMEM)] * len(outs),
+        scratch_shapes=list(scratch),
+        compiler_params=pltpu.CompilerParams(vmem_limit_bytes=LIMIT),
+        cost_estimate=pl.CostEstimate(flops=flops, bytes_accessed=size, transcendentals=0),
+        name=name,
+    )(*args)
+
+
+def place():
+    spot = lax.axis_index("dp")
+    return spot, lax.axis_index("rep"), spot // 4, lax.axis_index("chain")
+
+
+def forward_kernel(
+    desc_ref, meta_ref, first_far, second_far, far_meta, vec_ref,
+    own0, own1, rec0, rec1,
+    h1_ref, h2_ref, g2_ref, g1_ref, f_ref, x_ref, member_ref, sums_ref,
+    w1h, w1l, w2h, w2l,
+):
+    spot, core, half, chain = place()
+    width = w1h.shape[1]
+    rows1 = w1h.shape[0] // 16
+    rows2 = w2h.shape[0] // 16
+    rows = rows1 + rows2
+    for far in range(2):
+        for other in range(2):
+            block = ((own0, own1), (rec0, rec1))[far][other]
+            for delta in range(4):
+                owner = ((spot ^ (delta + 4 * far)) * 2 + (core ^ other))
+                piece = block[delta * rows : delta * rows + rows1, :]
+                high, low = split(piece)
+                at = pl.ds(pl.multiple_of(owner * rows1, rows1), rows1)
+                w1h[at, :] = high
+                w1l[at, :] = low
+                piece = block[delta * rows + rows1 : (delta + 1) * rows, :]
+                high, low = split(piece)
+                at = pl.ds(pl.multiple_of(owner * rows2, rows2), rows2)
+                w2h[at, :] = high
+                w2l[at, :] = low
+    atoms = desc_ref.shape[2]
+    near = meta_ref[...]
+    away = far_meta[...]
+    n_near = [near[1:2, 0:1], near[1:2, 1:2]]
+    n_far = [away[1:2, 0:1], away[1:2, 1:2]]
+    choose = lambda number, yes, no: jnp.where(jnp.broadcast_to(number, yes.shape) > 0.5, yes, no)
+    own_desc = [desc_ref[half, 0], desc_ref[half, 1]]
+    direct = first_far[...]
+    shared = second_far[...]
+    even = chain == 0
+    far_desc = [jnp.where(even, direct, shared), jnp.where(even, shared, direct)]
+    first = lambda own, far: choose(n_near[0], own[0], far[0])
+    second = lambda own, far: choose(n_near[1], own[1], choose(n_near[0], far[0], far[1]))
+    x0, x1 = first(own_desc, far_desc), second(own_desc, far_desc)
+    n0, n1 = first(n_near, n_far), second(n_near, n_far)
+    near_ids = near[0:1, :]
+    far_ids = away[0:1, :] + 32.0
+    pair = lambda row: [row[:, :atoms], row[:, atoms:]]
+    id0, id1 = first(pair(near_ids), pair(far_ids)), second(pair(near_ids), pair(far_ids))
+    ids = jnp.broadcast_to(jnp.concatenate([id0, id1], axis=1), (128, 2 * atoms)).T[:, 0:128]
+    spots = lax.broadcasted_iota(jnp.int32, (atoms, 128), 0).astype(F32)
+    live = jnp.concatenate([(spots < n0).astype(F32), (spots < n1).astype(F32)], axis=0)
+    lanes = lax.broadcasted_iota(jnp.int32, (2 * atoms, 128), 1).astype(F32)
+    member = jnp.where(ids == lanes, live, 0.0)
+    member_ref[...] = member
+
+    x = jnp.concatenate([x0, x1], axis=0)
+    x_ref[...] = x
+    vec = vec_ref[half]
+    c1, c2, w3 = vec[0:1, :], vec[1:2, :], vec[2:3, :]
+    w1 = (w1h[...], w1l[...])
+    w2 = (w2h[...], w2l[...])
+    h1 = jnp.tanh(product(split(x), w1, NN) + c1)
+    h1_ref[...] = h1
+    h2 = jnp.tanh(product(split(h1), w2, NN) + c2)
+    h2_ref[...] = h2
+    energy = jnp.sum(h2 * w3, axis=1, keepdims=True)
+    sums_ref[0:1, :] = jnp.sum(member * energy, axis=0, keepdims=True)
+    sums_ref[1:2, :] = jnp.sum(member, axis=0, keepdims=True)
+    sums_ref[2:8, :] = jnp.zeros((6, 128), F32)
+    g2 = w3 * (1.0 - h2 * h2)
+    g2_ref[...] = g2
+    g1 = product(split(g2), w2, NT) * (1.0 - h1 * h1)
+    g1_ref[...] = g1
+    f_ref[...] = product(split(g1), w1, NT)
+
+
+def force_kernel(mine, theirs, refs, near, member, f_ref, force_near, force_far, adj_ref, pot_ref):
+    other = theirs[...]
+    lane = lax.broadcasted_iota(jnp.int32, other.shape, 1)
+    other = jnp.where(lane < 32, pltpu.roll(other, 96, 1), pltpu.roll(other, 32, 1))
+    total = mine[0:1, :] + other[0:1, :]
+    count = jnp.maximum(mine[1:2, :] + other[1:2, :], 1.0)
+    error = total / count - refs[0:1, :]
+    inside = lax.broadcasted_iota(jnp.int32, (1, 128), 1) < 64
+    error = jnp.where(inside, error, 0.0)
+    square = error * error
+    low = jnp.sum(square[:, 0:32], axis=1, keepdims=True)
+    high = jnp.sum(square[:, 32:64], axis=1, keepdims=True)
+    pot_ref[...] = jnp.broadcast_to((low + high) / (2.0 * NOISE_VAR), (8, 128))
+    scale = error / count / NOISE_VAR
+    adj = jnp.sum(member[...] * scale, axis=1, keepdims=True)
+    adj_ref[...] = jnp.broadcast_to(adj, adj_ref.shape)
+    force = adj * f_ref[...]
+    atoms = force.shape[0] // 2
+    f0, f1 = force[:atoms], force[atoms:]
+    has0 = jnp.broadcast_to(near[1:2, 0:1], f0.shape) > 0.5
+    has1 = jnp.broadcast_to(near[1:2, 1:2], f0.shape) > 0.5
+    force_near[0] = jnp.where(has0, f0, 0.0)
+    force_near[1] = jnp.where(has1, f1, 0.0)
+    force_far[0] = jnp.where(has0, jnp.where(has1, 0.0, f1), f0)
+    force_far[1] = jnp.where(has0, 0.0, f1)
+
+
+def gradient_kernel(adj_ref, pot_ref, h1_ref, h2_ref, g2_ref, g1_ref, x_ref, keep, give, dw1, dw2):
+    spot, core, half, chain = place()
+    adj = adj_ref[...][:, 0:1]
+    g2 = adj * g2_ref[...]
+    g1 = adj * g1_ref[...]
+    dw2[...] = product(split(h1_ref[...]), split(g2), TN)
+    dw1[...] = product(split(x_ref[...]), split(g1), TN)
+    rows1 = dw1.shape[0] // 16
+    rows2 = dw2.shape[0] // 16
+    rows = rows1 + rows2
+    for delta in range(8):
+        for out, holder in ((keep, core), (give, 1 - core)):
+            owner = (spot ^ delta) * 2 + holder
+            base = delta * rows
+            at = pl.ds(pl.multiple_of(owner * rows1, rows1), rows1)
+            out[base : base + rows1, :] = dw1[at, :]
+            at = pl.ds(pl.multiple_of(owner * rows2, rows2), rows2)
+            out[base + rows1 : base + rows, :] = dw2[at, :]
+    base = 8 * rows
+    width = g2.shape[1]
+    vec = [
+        jnp.sum(g1, axis=0, keepdims=True),
+        jnp.sum(g2, axis=0, keepdims=True),
+        jnp.sum(adj * h2_ref[...], axis=0, keepdims=True),
+        jnp.broadcast_to(pot_ref[0:1, 0:1], (1, width)),
+    ]
+    tail = jnp.concatenate(vec + [jnp.zeros((4, width), F32)], axis=0)
+    keep[base : base + 8, :] = tail
+    give[base : base + 8, :] = tail
+
+
+def core_sum_kernel(keep, came, s0, s1, s2, s3, o0, o1, o2, o3):
+    rows = s0.shape[0]
+    for delta, out in enumerate((s0, s1, s2, s3, o0, o1, o2, o3)):
+        at = slice(delta * rows, (delta + 1) * rows)
+        out[0:rows, :] = keep[at, :] + came[at, :]
+        if delta >= 4:
+            at = slice(8 * rows, 8 * rows + 8)
+            out[rows : rows + 8, :] = keep[at, :] + came[at, :]
+
+
+def four_sum_kernel(a, b, c, d, out):
+    out[...] = (a[...] + b[...]) + (c[...] + d[...])
+
+
+def flip(axis, delta, size):
+    return lambda x: lax.ppermute(x, axis, [(i, i ^ delta) for i in range(size)])
+
+
+def halves(
+    descriptors, counts, struct_ids, ref_energy, first_layer, second_layer, vectors,
+    first_momentum, second_momentum, vector_momentum,
+):
+    nelem, slots, atoms, width = descriptors.shape
+    hidden = vectors.shape[2]
+    structs = ref_energy.shape[0]
+    spot, core, half, chain = place()
+    to = [None] + [flip("dp", delta, 8) for delta in range(1, 8)]
+    to_core = flip("rep", 1, 2)
+    to_chain = flip("chain", 1, 2)
+    rows1 = first_layer.shape[1] // hidden
+    rows2 = second_layer.shape[1] // hidden
+    rows = rows1 + rows2
+    shards = jnp.concatenate(
+        [first_layer.reshape(nelem, rows1, hidden), second_layer.reshape(nelem, rows2, hidden)], axis=1
+    )
+    pick = lambda x, at: lax.dynamic_index_in_dim(x, at, 0, keepdims=False)
+    own = pick(shards, half)
+    got = to[4](pick(shards, 1 - half))
+
+    def meta_of(at):
+        ids = pick(struct_ids, at).astype(F32).reshape(1, slots * atoms)
+        number = jnp.pad(pick(counts, at).astype(F32).reshape(1, slots), ((0, 0), (0, slots * atoms - slots)))
+        refs = jnp.pad(ref_energy.reshape(1, structs), ((0, 0), (0, slots * atoms - structs)))
+        return jnp.concatenate([ids, number, refs, jnp.zeros((5, slots * atoms), F32)], axis=0)
+
+    meta = meta_of(half)
+    sent_desc = lax.dynamic_slice(descriptors, (1 - half, chain, 0, 0), (1, 1, atoms, width)).reshape(atoms, width)
+    message = to[4](jnp.concatenate([sent_desc, meta_of(1 - half)], axis=0))
+    direct = message[:atoms]
+    far_meta = message[atoms:]
+    shared = to_chain(direct)
+    own_set = jnp.concatenate([own] + [to[delta](own) for delta in (1, 2, 3)], axis=0)
+    own_across = to_core(own_set)
+    got_set = jnp.concatenate([got] + [to[delta](got) for delta in (1, 2, 3)], axis=0)
+    got_across = to_core(got_set)
+
+    work = slots * atoms
+    h1, h2, g2, g1, f, x, member, sums = call(
+        forward_kernel,
+        [(work, hidden)] * 4 + [(work, width)] * 2 + [(work, 128), (8, 128)],
+        (descriptors, meta, direct, shared, far_meta, vectors, own_set, own_across, got_set, got_across),
+        scratch=[pltpu.VMEM((width, hidden), BF16)] * 2 + [pltpu.VMEM((hidden, hidden), BF16)] * 2,
+        flops=12 * work * hidden * (width + hidden),
+        size=8 * 1024 * 1024,
+        name="forward",
+    )
+    refs = jnp.concatenate([meta[2:3, 0:structs], far_meta[2:3, 0:structs], jnp.zeros((1, 128 - 2 * structs), F32)], axis=1)
+    force_near, force_far, adj, pot = call(
+        force_kernel,
+        [(slots, atoms, width)] * 2 + [(work, 128), (8, 128)],
+        (sums, to[4](sums), refs, meta, member, f),
+        size=2 * 1024 * 1024,
+        name="force",
+    )
+    force_came = to[4](force_far)
+    total_rows = 8 * rows + 8
+    keep, give = call(
+        gradient_kernel,
+        [(total_rows, hidden)] * 2,
+        (adj, pot, h1, h2, g2, g1, x),
+        scratch=[pltpu.VMEM((width, hidden), F32), pltpu.VMEM((hidden, hidden), F32)],
+        flops=6 * work * hidden * (width + hidden),
+        size=4 * 1024 * 1024,
+        name="gradient",
+    )
+    parts = call(
+        core_sum_kernel,
+        [(rows, hidden)] * 4 + [(rows + 8, hidden)] * 4,
+        (keep, to_core(give)),
+        size=3 * 1024 * 1024,
+        name="core_sum",
+    )
+    beyond = [parts[4]] + [to[delta](parts[4 + delta]) for delta in (1, 2, 3)]
+    (beyond_sum,) = call(four_sum_kernel, [(rows + 8, hidden)], beyond, size=500 * 1024, name="beyond_sum")
+    came = to[4](beyond_sum)
+    mine = [parts[0]] + [to[delta](parts[delta]) for delta in (1, 2, 3)]
+    (mine_sum,) = call(four_sum_kernel, [(rows, hidden)], mine, size=500 * 1024, name="mine_sum")
+
+    low = half == 0
+    order = lambda a, b: jnp.where(low, jnp.stack([a, b]), jnp.stack([b, a]))
+    grads = order(mine_sum, came[:rows])
+    tails = order(beyond_sum[rows:], came[rows:])
+    share_first = grads[:, :rows1].reshape(nelem, rows1 * hidden)
+    share_second = grads[:, rows1:].reshape(nelem, rows2 * hidden)
+    grad_vectors = tails[:, 0:3, :]
+    potential_sum = beyond_sum[rows + 3, 0:1]
+    force_partials = order(force_near, force_came)
+    new_first_mom = first_momentum - STEP_SIZE * share_first
+    new_second_mom = second_momentum - STEP_SIZE * share_second
+    new_vector_mom = vector_momentum - STEP_SIZE * grad_vectors
+    new_first = first_layer + STEP_SIZE * new_first_mom
+    new_second = second_layer + STEP_SIZE * new_second_mom
+    new_vectors = vectors + STEP_SIZE * new_vector_mom
+    potential = potential_sum / (structs * 16)
+    return (
+        new_first, new_second, new_vectors, new_first_mom, new_second_mom, new_vector_mom, potential, force_partials,
+    )
 
 
 def element_energies(first, second, vectors, desc):
@@ -113,8 +401,9 @@
         P("chain", ("dp", "rep")),
         P("chain", None, None),
     )
+    split_by_half = (mesh.shape["chain"], mesh.shape["dp"], mesh.shape["rep"]) == (2, 8, 2)
     return jax.shard_map(
-        on_device,
+        halves if split_by_half else on_device,
         mesh=mesh,
         in_specs=placed,
         out_specs=(

time: 229 us -> 82.1 us (0.36)
  waiting for transfers between devices: 117 us -> 45.7 us
  blocking collectives: 60.3 us -> 0 us
  matrix products: 22.3 us -> 0 us
  starting transfers between devices: 0.11 us -> 21.3 us
  between operations: 16.4 us -> 2.82 us
  Pallas kernels: 0 us -> 3.56 us
  other arithmetic: 5.17 us -> 2.57 us
    all_gather x2 -> x0, waiting for transfers between devices: 79.8 us -> none  [the longest x1 40.1 us: on_device(): lax.all_gather(second_layer, ('dp', 'rep'), axis=1, tiled=True)]
    psum x1 -> x0, blocking collectives: 60.3 us -> none  [on_device(): lax.psum((grad_first, grad_second, grads[2], potential_part), ('dp', 'rep'))]
    ppermute x0 -> x21, waiting for transfers between devices: none -> 45.7 us  [flip(): lax.ppermute(x, axis, [(i, i ^ delta) for i in range(size)])]
    psum x1 -> x0, waiting for transfers between devices: 36.3 us -> none  [on_device(): lax.psum((grad_first, grad_second, grads[2], potential_part), ('dp', 'rep'))]
    dot_general x11 -> x0, matrix products: 22.3 us -> none  [the longest x3 9.84 us: element_energies(): jnp.einsum('erj,ejk->erk', hidden, second, precision=HIGH)]
    ppermute x0 -> x21, starting transfers between devices: none -> 21.3 us  [flip(): lax.ppermute(x, axis, [(i, i ^ delta) for i in range(size)])]
    pallas_call x0 -> x6, Pallas kernels: none -> 3.56 us  [call(): pl.pallas_call(kernel, out_shape=[jax.ShapeDtypeStruct(shape, F32) for sh...]
    add x3, other arithmetic: 3.95 us -> 1.57 us  [the longest x1 0.83 us: halves(): new_second = second_layer + STEP_SIZE * new_second_mom]
  transfers between devices with their start and end apart: 3 -> 21, of which waited for: 3 -> 10; matrix products, arithmetic and copies ran while one was open for 4% -> 1% of each run, Pallas kernels for 0% -> 0%
where the time goes in v1:
time: 82.1 us; the launch traced here: 81.8 us
  waiting for transfers between devices  45.7 us (56%)
  starting transfers between devices  21.3 us (26%)
  local copies, waits for them, and re-layouts  5.87 us (7%)
  Pallas kernels  3.56 us (4%)
  between operations  2.82 us (3%)
  other arithmetic  2.57 us (3%)
    ppermute x21, waiting for transfers between devices, flip(): lax.ppermute(x, axis, [(i, i ^ delta) for i in range(size)])  45.7 us
    ppermute x21, starting transfers between devices, flip(): lax.ppermute(x, axis, [(i, i ^ delta) for i in range(size)])  21.3 us
    unnamed x29, local copies, waits for them, and re-layouts  5.2 us
    pallas_call x6, Pallas kernels, call(): pl.pallas_call(kernel, out_shape=[jax.ShapeDtypeStruct(shape, F32) for sh...  3.56 us
  transfers between devices with their start and end apart: 21, of which 10 were waited for; matrix products, arithmetic and copies ran while one was open for 1% of the time, Pallas kernels for 0%

profile of v1, /device:TPU:0, one launch (start us, length us, event | category | flops | bytes accessed | tf_op | source)
XLA Modules:
  0.0 81.8 jit_solution(17051160386579965344)
XLA Ops:
  0.7 0.9 %bitcast_dynamic-update-slice_fusion.1 = f32[2,48,512]{2,1,0:T(8,128)S(1)} fusion(f32[1,2,16,512]{3,1,2,0:T(2,128)} %bitcast.37), kind=kLoop, calls=%fused_computation.11 | loop fusion | bytes 131072
  1.6 0.0 copy-start.7
  1.7 4.0 %collective-permute-start.4 = (f32[48,512]{1,0:T(8,128)S(1)}, f32[48,512]{1,0:T(8,128)S(1)}, u32[]{:S(2)}, u32[]{:S(2)}) collective-permute-start(f32[48,512]{1,0:T(8,128)S(1)} %get-tuple-element.67), channel_id=1, source_target_pairs={{0,6},{2,4},{4,2},{6,0},{8,14},{10,12},{12,10},{14,8},{1,7},{3,5},... | collective-permute-start | bytes 294920 | tf_op jit(solution)/shard_map/ppermute | solution.py:195
  5.7 0.4 collective-permute-start.3
  6.1 0.2 collective-permute-start.2
  6.3 2.9 %collective-permute-start.6 = (f32[48,512]{1,0:T(8,128)S(1)}, f32[48,512]{1,0:T(8,128)S(1)}, u32[]{:S(2)}, u32[]{:S(2)}) collective-permute-start(f32[48,512]{1,0:T(8,128)S(1)} %get-tuple-element.66), channel_id=1, source_target_pairs={{0,8},{2,10},{4,12},{6,14},{8,0},{10,2},{12,4},{14,6},{1,9},{3,11}... | collective-permute-start | bytes 294920 | tf_op jit(solution)/shard_map/ppermute | solution.py:195
  9.3 0.0 collective-permute-done.4
  9.3 3.7 %collective-permute-done.3 = f32[48,512]{1,0:T(8,128)S(1)} collective-permute-done((f32[48,512]{1,0:T(8,128)S(1)}, f32[48,512]{1,0:T(8,128)S(1)}, u32[]{:S(2)}, u32[]{:S(2)}) %collective-permute-start.3) | collective-permute-done | bytes 98336 | tf_op jit(solution)/shard_map/ppermute | solution.py:195
  12.9 0.0 collective-permute-done.2
  13.0 0.0 copy-start
  13.0 0.1 collective-permute-start.5
  13.0 0.0 collective-permute-done.6
  13.1 2.5 %collective-permute-start.9 = (f32[48,512]{1,0:T(8,128)S(1)}, f32[48,512]{1,0:T(8,128)S(1)}, u32[]{:S(2)}, u32[]{:S(2)}) collective-permute-start(f32[48,512]{1,0:T(8,128)S(1)} %collective-permute-done.6), channel_id=1, source_target_pairs={{0,6},{2,4},{4,2},{6,0},{8,14},{10,12},{12,10},{14,8},{1,7},{3,5},... | collective-permute-start | bytes 294920 | tf_op jit(solution)/shard_map/ppermute | solution.py:195
  15.6 1.6 %collective-permute-start.8 = (f32[48,512]{1,0:T(8,128)S(1)}, f32[48,512]{1,0:T(8,128)S(1)}, u32[]{:S(2)}, u32[]{:S(2)}) collective-permute-start(f32[48,512]{1,0:T(8,128)S(1)} %collective-permute-done.6), channel_id=1, source_target_pairs={{0,4},{2,6},{4,0},{6,2},{8,12},{10,14},{12,8},{14,10},{1,5},{3,7},... | collective-permute-start | bytes 294920 | tf_op jit(solution)/shard_map/ppermute | solution.py:195
  17.2 0.0 collective-permute-start.7
  17.2 4.6 %collective-permute-done.7 = f32[48,512]{1,0:T(8,128)S(1)} collective-permute-done((f32[48,512]{1,0:T(8,128)S(1)}, f32[48,512]{1,0:T(8,128)S(1)}, u32[]{:S(2)}, u32[]{:S(2)}) %collective-permute-start.7) | collective-permute-done | bytes 98336 | tf_op jit(solution)/shard_map/ppermute | solution.py:195
  21.8 0.0 collective-permute-done.8
  21.8 0.0 copy-start.9
  21.8 0.0 collective-permute-done.9
  21.9 0.1 collective-permute-start.10
  21.9 0.6 copy-done.9
  22.5 0.6 copy-done.8
  23.3 1.4 %collective-permute-start = (f32[136,256]{1,0:T(8,128)S(1)}, f32[136,256]{1,0:T(8,128)S(1)}, u32[]{:S(2)}, u32[]{:S(2)}) collective-permute-start(f32[136,256]{1,0:T(8,128)S(1)} %concatenate.19), channel_id=1, source_target_pairs={{0,8},{2,10},{4,12},{6,14},{8,0},{10,2},{12,4},{14,6},{1,9},{3,11}... | collective-permute-start | bytes 417800 | tf_op jit(solution)/shard_map/ppermute | solution.py:195
  24.7 8.1 %collective-permute-done = f32[136,256]{1,0:T(8,128)S(1)} collective-permute-done((f32[136,256]{1,0:T(8,128)S(1)}, f32[136,256]{1,0:T(8,128)S(1)}, u32[]{:S(2)}, u32[]{:S(2)}) %collective-permute-start) | collective-permute-done | bytes 139296 | tf_op jit(solution)/shard_map/ppermute | solution.py:195
  32.8 1.6 %collective-permute-start.1 = (f32[128,256]{1,0:T(8,128)S(1)}, f32[128,256]{1,0:T(8,128)S(1)}, u32[]{:S(2)}, u32[]{:S(2)}) collective-permute-start(f32[128,256]{1,0:T(8,128)S(1)} %slice.42.first_far), channel_id=1, source_target_pairs={{0,16},{16,0},{1,17},{17,1},{2,18},{18,2},{3,19},{19,3},{4,20},{20... | collective-permute-start | bytes 393224 | tf_op jit(solution)/shard_map/ppermute | solution.py:195
  34.4 3.8 %collective-permute-done.1.second_far = f32[128,256]{1,0:T(8,128)S(1)} collective-permute-done((f32[128,256]{1,0:T(8,128)S(1)}, f32[128,256]{1,0:T(8,128)S(1)}, u32[]{:S(2)}, u32[]{:S(2)}) %collective-permute-start.1) | collective-permute-done | bytes 131104 | tf_op jit(solution)/shard_map/ppermute | solution.py:195
  38.2 2.2 %forward.1 = (f32[256,512]{1,0:T(8,128)S(1)}, f32[256,512]{1,0:T(8,128)S(1)}, f32[256,512]{1,0:T(8,128)S(1)}, f32[256,512]{1,0:T(8,128)S(1)}, f32[256,256]{1,0:T...) custom-call(f32[2,2,128,256]{3,2,1,0:T(8,128)S(1)} %copy-done, ...), custom_call_target="tpu_custom_call" | custom-call | flops 1207959552 | bytes 8388608 | tf_op jit(solution)/shard_map/forward/pallas_call | solution.py:32
  40.3 0.1 collective-permute-start.11
  40.4 0.1 bitcast_maximum_fusion.refs
  40.5 4.4 %collective-permute-done.11.theirs = f32[8,128]{1,0:T(8,128)S(1)} collective-permute-done((f32[8,128]{1,0:T(8,128)S(1)}, f32[8,128]{1,0:T(8,128)S(1)}, u32[]{:S(2)}, u32[]{:S(2)}) %collective-permute-start.11) | collective-permute-done | bytes 4128 | tf_op jit(solution)/shard_map/ppermute | solution.py:195
  44.9 0.2 force.1
  45.2 1.0 %gradient.1 = (f32[392,512]{1,0:T(8,128)S(1)}, f32[392,512]{1,0:T(8,128)S(1)}) custom-call(f32[256,128]{1,0:T(8,128)S(1)} %get-tuple-element.33.adj_ref, f32[8,128]{1,0:T(8,128)S(1)} %get-tuple-element.34.pot_ref, f32[256,512]{1,0:T(8,128)S(1)} %get-tuple-element.35.h1_ref, f32[256,512]{1,0:T(8,128)S(1)} %get-tuple-element.36.h2_ref, ...), custom_call_target="tpu_custom_call" | custom-call | flops 603979776 | bytes 4194304 | tf_op jit(solution)/shard_map/gradient/pallas_call | solution.py:32
  46.2 0.1 collective-permute-start.12
  46.3 0.1 collective-permute-start.20
  46.3 2.2 %collective-permute-done.12.came = f32[392,512]{1,0:T(8,128)S(1)} collective-permute-done((f32[392,512]{1,0:T(8,128)S(1)}, f32[392,512]{1,0:T(8,128)S(1)}, u32[]{:S(2)}, u32[]{:S(2)}) %collective-permute-start.12) | collective-permute-done | bytes 802848 | tf_op jit(solution)/shard_map/ppermute | solution.py:195
  48.6 0.1 core_sum.1
  48.6 0.2 collective-permute-start.13
  48.9 1.3 %collective-permute-start.14 = (f32[48,512]{1,0:T(8,128)S(1)}, f32[48,512]{1,0:T(8,128)S(1)}, u32[]{:S(2)}, u32[]{:S(2)}) collective-permute-start(f32[48,512]{1,0:T(8,128)S(1)} %get-tuple-element.44), channel_id=1, source_target_pairs={{0,4},{2,6},{4,0},{6,2},{8,12},{10,14},{12,8},{14,10},{1,5},{3,7},... | collective-permute-start | bytes 294920 | tf_op jit(solution)/shard_map/ppermute | solution.py:195
  50.1 2.1 %collective-permute-start.15 = (f32[48,512]{1,0:T(8,128)S(1)}, f32[48,512]{1,0:T(8,128)S(1)}, u32[]{:S(2)}, u32[]{:S(2)}) collective-permute-start(f32[48,512]{1,0:T(8,128)S(1)} %get-tuple-element.45), channel_id=1, source_target_pairs={{0,6},{2,4},{4,2},{6,0},{8,14},{10,12},{12,10},{14,8},{1,7},{3,5},... | collective-permute-start | bytes 294920 | tf_op jit(solution)/shard_map/ppermute | solution.py:195
  52.2 0.1 collective-permute-start.16
  52.3 8.9 %collective-permute-done.20 = f32[2,128,256]{2,1,0:T(8,128)S(1)} collective-permute-done((f32[2,128,256]{2,1,0:T(8,128)S(1)}, f32[2,128,256]{2,1,0:T(8,128)S(1)}, u32[]{:S(2)}, u32[]{:S(2)}) %collective-permute-start.20) | collective-permute-done | bytes 262176 | tf_op jit(solution)/shard_map/ppermute | solution.py:195
  61.3 0.0 collective-permute-start.17
  61.3 0.0 collective-permute-done.13.b
  61.3 1.9 %collective-permute-start.18 = (f32[56,512]{1,0:T(8,128)S(1)}, f32[56,512]{1,0:T(8,128)S(1)}, u32[]{:S(2)}, u32[]{:S(2)}) collective-permute-start(f32[56,512]{1,0:T(8,128)S(1)} %get-tuple-element.49), channel_id=1, source_target_pairs={{0,6},{2,4},{4,2},{6,0},{8,14},{10,12},{12,10},{14,8},{1,7},{3,5},... | collective-permute-start | bytes 344072 | tf_op jit(solution)/shard_map/ppermute | solution.py:195
  63.2 0.8 %maximum_select_fusion = f32[2,2,128,256]{3,2,1,0:T(8,128)} fusion(f32[1,2,128,256]{3,2,1,0:T(8,128)S(1)} %bitcast.39, f32[1,2,128,256]{3,2,1,0:T(8,128)S(1)} %bitcast.34, pred[]{:T(512)S(6)} %eq.3), kind=kLoop, calls=%fused_computation | loop fusion | flops 393216 | bytes 1048577 | tf_op jit(solution)/shard_map/jit(_where)/select_n | solution.py:279
  64.1 0.0 collective-permute-done.15.d
  64.1 3.2 %collective-permute-done.17.c = f32[56,512]{1,0:T(8,128)S(1)} collective-permute-done((f32[56,512]{1,0:T(8,128)S(1)}, f32[56,512]{1,0:T(8,128)S(1)}, u32[]{:S(2)}, u32[]{:S(2)}) %collective-permute-start.17) | collective-permute-done | bytes 114720 | tf_op jit(solution)/shard_map/ppermute | solution.py:195
  67.3 1.2 %collective-permute-done.18.d = f32[56,512]{1,0:T(8,128)S(1)} collective-permute-done((f32[56,512]{1,0:T(8,128)S(1)}, f32[56,512]{1,0:T(8,128)S(1)}, u32[]{:S(2)}, u32[]{:S(2)}) %collective-permute-start.18) | collective-permute-done | bytes 114720 | tf_op jit(solution)/shard_map/ppermute | solution.py:195
  68.5 0.5 slice.50
  69.0 0.6 collective-permute-start.19
  70.2 5.7 %collective-permute-done.19 = f32[56,512]{1,0:T(8,128)S(1)} collective-permute-done((f32[56,512]{1,0:T(8,128)S(1)}, f32[56,512]{1,0:T(8,128)S(1)}, u32[]{:S(2)}, u32[]{:S(2)}) %collective-permute-start.19) | collective-permute-done | bytes 114720 | tf_op jit(solution)/shard_map/ppermute | solution.py:195
  76.0 0.0 copy-start.6
  76.0 0.7 copy-done.6
  76.8 0.6 copy.21
  77.4 0.6 copy.22
  78.0 0.1 copy.26
  78.1 0.0 copy-start.2
  78.1 0.0 copy-start.4
  78.1 0.1 copy.25
  78.2 0.8 copy-done.2
  78.9 0.0 copy-done.4
  79.0 0.7 multiply_add_fusion.1
  79.7 0.2 copy-done.3
  79.9 0.8 %multiply_add_fusion = (f32[2,16384]{1,0:T(2,128)}, f32[2,16384]{1,0:T(2,128)}) fusion(f32[2,16384]{1,0:T(2,128)S(1)} %copy-done.1, f32[2,16384]{1,0:T(2,128)S(1)} %copy-done.3, f32[2,16384]{1,0:T(2,128)S(1)} %bitcast.36), kind=kLoop, calls=%fused_computation.6 | loop fusion | flops 98304 | bytes 655360 | tf_op jit(solution)/shard_map/add | solution.py:291
  (41 shorter events, 0.4 us)
Async XLA Ops:
  0.6 0.9 %copy-start.1 = (f32[2,16384]{1,0:T(2,128)S(1)}, f32[2,16384]{1,0:T(2,128)}, u32[]{:S(2)}) copy-start(f32[2,16384]{1,0:T(2,128)} %param.15) | copy-start | bytes 393220
  1.6 7.6 %copy-start.7 = (s32[2,2,128]{2,1,0:T(2,128)S(1)}, s32[2,2,128]{2,1,0:T(2,128)}, u32[]{:S(2)}) copy-start(s32[2,2,128]{2,1,0:T(2,128)} %param.12) | copy-start | bytes 6148
  1.7 7.6 %collective-permute-start.4 = (f32[48,512]{1,0:T(8,128)S(1)}, f32[48,512]{1,0:T(8,128)S(1)}, u32[]{:S(2)}, u32[]{:S(2)}) collective-permute-start(f32[48,512]{1,0:T(8,128)S(1)} %get-tuple-element.67), channel_id=1, source_target_pairs={{0,6},{2,4},{4,2},{6,0},{8,14},{10,12},{12,10},{14,8},{1,7},{3,5},... | collective-permute-start | bytes 294920 | tf_op jit(solution)/shard_map/ppermute | solution.py:195
  5.7 7.3 %collective-permute-start.3 = (f32[48,512]{1,0:T(8,128)S(1)}, f32[48,512]{1,0:T(8,128)S(1)}, u32[]{:S(2)}, u32[]{:S(2)}) collective-permute-start(f32[48,512]{1,0:T(8,128)S(1)} %get-tuple-element.67), channel_id=1, source_target_pairs={{0,4},{2,6},{4,0},{6,2},{8,12},{10,14},{12,8},{14,10},{1,5},{3,7},... | collective-permute-start | bytes 294920 | tf_op jit(solution)/shard_map/ppermute | solution.py:195
  6.1 6.8 %collective-permute-start.2 = (f32[48,512]{1,0:T(8,128)S(1)}, f32[48,512]{1,0:T(8,128)S(1)}, u32[]{:S(2)}, u32[]{:S(2)}) collective-permute-start(f32[48,512]{1,0:T(8,128)S(1)} %get-tuple-element.67), channel_id=1, source_target_pairs={{0,2},{2,0},{4,6},{6,4},{8,10},{10,8},{12,14},{14,12},{1,3},{3,1},... | collective-permute-start | bytes 294920 | tf_op jit(solution)/shard_map/ppermute | solution.py:195
  6.3 6.7 %collective-permute-start.6 = (f32[48,512]{1,0:T(8,128)S(1)}, f32[48,512]{1,0:T(8,128)S(1)}, u32[]{:S(2)}, u32[]{:S(2)}) collective-permute-start(f32[48,512]{1,0:T(8,128)S(1)} %get-tuple-element.66), channel_id=1, source_target_pairs={{0,8},{2,10},{4,12},{6,14},{8,0},{10,2},{12,4},{14,6},{1,9},{3,11}... | collective-permute-start | bytes 294920 | tf_op jit(solution)/shard_map/ppermute | solution.py:195
  13.0 10.2 %copy-start = (f32[2,2,128,256]{3,2,1,0:T(8,128)S(1)}, f32[2,2,128,256]{3,2,1,0:T(8,128)}, u32[]{:S(2)}) copy-start(f32[2,2,128,256]{3,2,1,0:T(8,128)} %desc_ref.1) | copy-start | bytes 1572868
  13.0 25.2 %collective-permute-start.5 = (f32[192,512]{1,0:T(8,128)S(1)}, f32[192,512]{1,0:T(8,128)S(1)}, u32[]{:S(2)}, u32[]{:S(2)}) collective-permute-start(f32[192,512]{1,0:T(8,128)S(1)} %pad_maximum_fusion.own0), channel_id=1, source_target_pairs={{0,1},{1,0},{2,3},{3,2},{4,5},{5,4},{6,7},{7,6},{8,9},{9,8},{10,11... | collective-permute-start | bytes 1179656 | tf_op jit(solution)/shard_map/ppermute | solution.py:195
  13.1 8.8 %collective-permute-start.9 = (f32[48,512]{1,0:T(8,128)S(1)}, f32[48,512]{1,0:T(8,128)S(1)}, u32[]{:S(2)}, u32[]{:S(2)}) collective-permute-start(f32[48,512]{1,0:T(8,128)S(1)} %collective-permute-done.6), channel_id=1, source_target_pairs={{0,6},{2,4},{4,2},{6,0},{8,14},{10,12},{12,10},{14,8},{1,7},{3,5},... | collective-permute-start | bytes 294920 | tf_op jit(solution)/shard_map/ppermute | solution.py:195
  15.6 6.2 %collective-permute-start.8 = (f32[48,512]{1,0:T(8,128)S(1)}, f32[48,512]{1,0:T(8,128)S(1)}, u32[]{:S(2)}, u32[]{:S(2)}) collective-permute-start(f32[48,512]{1,0:T(8,128)S(1)} %collective-permute-done.6), channel_id=1, source_target_pairs={{0,4},{2,6},{4,0},{6,2},{8,12},{10,14},{12,8},{14,10},{1,5},{3,7},... | collective-permute-start | bytes 294920 | tf_op jit(solution)/shard_map/ppermute | solution.py:195
  17.2 4.6 %collective-permute-start.7 = (f32[48,512]{1,0:T(8,128)S(1)}, f32[48,512]{1,0:T(8,128)S(1)}, u32[]{:S(2)}, u32[]{:S(2)}) collective-permute-start(f32[48,512]{1,0:T(8,128)S(1)} %collective-permute-done.6), channel_id=1, source_target_pairs={{0,2},{2,0},{4,6},{6,4},{8,10},{10,8},{12,14},{14,12},{1,3},{3,1},... | collective-permute-start | bytes 294920 | tf_op jit(solution)/shard_map/ppermute | solution.py:195
  21.8 0.7 copy-start.9
  21.9 16.3 %collective-permute-start.10 = (f32[192,512]{1,0:T(8,128)S(1)}, f32[192,512]{1,0:T(8,128)S(1)}, u32[]{:S(2)}, u32[]{:S(2)}) collective-permute-start(f32[192,512]{1,0:T(8,128)S(1)} %constant_dynamic-update-slice_fusion.rec0), channel_id=1, source_target_pairs={{0,1},{1,0},{2,3},{3,2},{4,5},{5,4},{6,7},{7,6},{8,9},{9,8},{10,11... | collective-permute-start | bytes 1179656 | tf_op jit(solution)/shard_map/ppermute | solution.py:195
  22.5 0.7 copy-start.8
  23.3 11.1 %copy-start.5 = (f32[2,3,512]{2,0,1:T(2,128)S(1)}, f32[2,3,512]{2,0,1:T(2,128)}, u32[]{:S(2)}) copy-start(f32[2,3,512]{2,0,1:T(2,128)} %param.16) | copy-start | bytes 36868
  23.3 9.5 %collective-permute-start = (f32[136,256]{1,0:T(8,128)S(1)}, f32[136,256]{1,0:T(8,128)S(1)}, u32[]{:S(2)}, u32[]{:S(2)}) collective-permute-start(f32[136,256]{1,0:T(8,128)S(1)} %concatenate.19), channel_id=1, source_target_pairs={{0,8},{2,10},{4,12},{6,14},{8,0},{10,2},{12,4},{14,6},{1,9},{3,11}... | collective-permute-start | bytes 417800 | tf_op jit(solution)/shard_map/ppermute | solution.py:195
  32.8 5.4 %collective-permute-start.1 = (f32[128,256]{1,0:T(8,128)S(1)}, f32[128,256]{1,0:T(8,128)S(1)}, u32[]{:S(2)}, u32[]{:S(2)}) collective-permute-start(f32[128,256]{1,0:T(8,128)S(1)} %slice.42.first_far), channel_id=1, source_target_pairs={{0,16},{16,0},{1,17},{17,1},{2,18},{18,2},{3,19},{19,3},{4,20},{20... | collective-permute-start | bytes 393224 | tf_op jit(solution)/shard_map/ppermute | solution.py:195
  40.3 4.6 %collective-permute-start.11 = (f32[8,128]{1,0:T(8,128)S(1)}, f32[8,128]{1,0:T(8,128)S(1)}, u32[]{:S(2)}, u32[]{:S(2)}) collective-permute-start(f32[8,128]{1,0:T(8,128)S(1)} %get-tuple-element.30.mine), channel_id=1, source_target_pairs={{0,8},{2,10},{4,12},{6,14},{8,0},{10,2},{12,4},{14,6},{1,9},{3,11}... | collective-permute-start | bytes 12296 | tf_op jit(solution)/shard_map/ppermute | solution.py:195
  46.2 2.4 %collective-permute-start.12 = (f32[392,512]{1,0:T(8,128)S(1)}, f32[392,512]{1,0:T(8,128)S(1)}, u32[]{:S(2)}, u32[]{:S(2)}) collective-permute-start(f32[392,512]{1,0:T(8,128)S(1)} %get-tuple-element.41), channel_id=1, source_target_pairs={{0,1},{1,0},{2,3},{3,2},{4,5},{5,4},{6,7},{7,6},{8,9},{9,8},{10,11... | collective-permute-start | bytes 2408456 | tf_op jit(solution)/shard_map/ppermute | solution.py:195
  46.3 15.0 %collective-permute-start.20 = (f32[2,128,256]{2,1,0:T(8,128)S(1)}, f32[2,128,256]{2,1,0:T(8,128)S(1)}, u32[]{:S(2)}, u32[]{:S(2)}) collective-permute-start(f32[2,128,256]{2,1,0:T(8,128)S(1)} %get-tuple-element.51), channel_id=1, source_target_pairs={{0,8},{2,10},{4,12},{6,14},{8,0},{10,2},{12,4},{14,6},{1,9},{3,11}... | collective-permute-start | bytes 786440 | tf_op jit(solution)/shard_map/ppermute | solution.py:195
  48.6 12.6 %collective-permute-start.13 = (f32[48,512]{1,0:T(8,128)S(1)}, f32[48,512]{1,0:T(8,128)S(1)}, u32[]{:S(2)}, u32[]{:S(2)}) collective-permute-start(f32[48,512]{1,0:T(8,128)S(1)} %get-tuple-element.43), channel_id=1, source_target_pairs={{0,2},{2,0},{4,6},{6,4},{8,10},{10,8},{12,14},{14,12},{1,3},{3,1},... | collective-permute-start | bytes 294920 | tf_op jit(solution)/shard_map/ppermute | solution.py:195
  48.9 15.2 %collective-permute-start.14 = (f32[48,512]{1,0:T(8,128)S(1)}, f32[48,512]{1,0:T(8,128)S(1)}, u32[]{:S(2)}, u32[]{:S(2)}) collective-permute-start(f32[48,512]{1,0:T(8,128)S(1)} %get-tuple-element.44), channel_id=1, source_target_pairs={{0,4},{2,6},{4,0},{6,2},{8,12},{10,14},{12,8},{14,10},{1,5},{3,7},... | collective-permute-start | bytes 294920 | tf_op jit(solution)/shard_map/ppermute | solution.py:195
  50.1 13.9 %collective-permute-start.15 = (f32[48,512]{1,0:T(8,128)S(1)}, f32[48,512]{1,0:T(8,128)S(1)}, u32[]{:S(2)}, u32[]{:S(2)}) collective-permute-start(f32[48,512]{1,0:T(8,128)S(1)} %get-tuple-element.45), channel_id=1, source_target_pairs={{0,6},{2,4},{4,2},{6,0},{8,14},{10,12},{12,10},{14,8},{1,7},{3,5},... | collective-permute-start | bytes 294920 | tf_op jit(solution)/shard_map/ppermute | solution.py:195
  52.2 11.9 %collective-permute-start.16 = (f32[56,512]{1,0:T(8,128)S(1)}, f32[56,512]{1,0:T(8,128)S(1)}, u32[]{:S(2)}, u32[]{:S(2)}) collective-permute-start(f32[56,512]{1,0:T(8,128)S(1)} %get-tuple-element.47), channel_id=1, source_target_pairs={{0,2},{2,0},{4,6},{6,4},{8,10},{10,8},{12,14},{14,12},{1,3},{3,1},... | collective-permute-start | bytes 344072 | tf_op jit(solution)/shard_map/ppermute | solution.py:195
  61.3 6.0 %collective-permute-start.17 = (f32[56,512]{1,0:T(8,128)S(1)}, f32[56,512]{1,0:T(8,128)S(1)}, u32[]{:S(2)}, u32[]{:S(2)}) collective-permute-start(f32[56,512]{1,0:T(8,128)S(1)} %get-tuple-element.48), channel_id=1, source_target_pairs={{0,4},{2,6},{4,0},{6,2},{8,12},{10,14},{12,8},{14,10},{1,5},{3,7},... | collective-permute-start | bytes 344072 | tf_op jit(solution)/shard_map/ppermute | solution.py:195
  61.3 7.2 %collective-permute-start.18 = (f32[56,512]{1,0:T(8,128)S(1)}, f32[56,512]{1,0:T(8,128)S(1)}, u32[]{:S(2)}, u32[]{:S(2)}) collective-permute-start(f32[56,512]{1,0:T(8,128)S(1)} %get-tuple-element.49), channel_id=1, source_target_pairs={{0,6},{2,4},{4,2},{6,0},{8,14},{10,12},{12,10},{14,8},{1,7},{3,5},... | collective-permute-start | bytes 344072 | tf_op jit(solution)/shard_map/ppermute | solution.py:195
  69.0 7.0 %collective-permute-start.19 = (f32[56,512]{1,0:T(8,128)S(1)}, f32[56,512]{1,0:T(8,128)S(1)}, u32[]{:S(2)}, u32[]{:S(2)}) collective-permute-start(f32[56,512]{1,0:T(8,128)S(1)} %beyond_sum.1), channel_id=1, source_target_pairs={{0,8},{2,10},{4,12},{6,14},{8,0},{10,2},{12,4},{14,6},{1,9},{3,11}... | collective-permute-start | bytes 344072 | tf_op jit(solution)/shard_map/ppermute | solution.py:195
  76.0 0.7 copy-start.6
  78.1 0.8 %copy-start.2 = (f32[2,8192]{1,0:T(2,128)S(1)}, f32[2,8192]{1,0:T(2,128)}, u32[]{:S(2)}) copy-start(f32[2,8192]{1,0:T(2,128)} %param.14) | copy-start | bytes 196612
  78.1 0.9 %copy-start.4 = (f32[2,8192]{1,0:T(2,128)S(1)}, f32[2,8192]{1,0:T(2,128)}, u32[]{:S(2)}) copy-start(f32[2,8192]{1,0:T(2,128)} %param.17) | copy-start | bytes 196612
  78.9 0.9 %copy-start.3 = (f32[2,16384]{1,0:T(2,128)S(1)}, f32[2,16384]{1,0:T(2,128)}, u32[]{:S(2)}) copy-start(f32[2,16384]{1,0:T(2,128)} %param.18) | copy-start | bytes 393220

commit v2 on v1

--- a/solution.py
+++ b/solution.py
@@ -31,12 +31,12 @@
 def call(kernel, outs, args, scratch=(), flops=0, size=0, name=None):
     return pl.pallas_call(
         kernel,
-        out_shape=[jax.ShapeDtypeStruct(shape, F32) for shape in outs],
+        out_shape=[jax.ShapeDtypeStruct(shape, kind) for shape, kind in ((*out, F32)[:2] for out in outs)],
         in_specs=[pl.BlockSpec(memory_space=VMEM)] * len(args),
         out_specs=[pl.BlockSpec(memory_space=VMEM)] * len(outs),
         scratch_shapes=list(scratch),
         compiler_params=pltpu.CompilerParams(vmem_limit_bytes=LIMIT),
-        cost_estimate=pl.CostEstimate(flops=flops, bytes_accessed=size, transcendentals=0),
+        cost_estimate=pl.CostEstimate(flops=1, bytes_accessed=1, transcendentals=0),
         name=name,
     )(*args)
 
@@ -49,8 +49,7 @@
 def forward_kernel(
     desc_ref, meta_ref, first_far, second_far, far_meta, vec_ref,
     own0, own1, rec0, rec1,
-    h1_ref, h2_ref, g2_ref, g1_ref, f_ref, x_ref, member_ref, sums_ref,
-    w1h, w1l, w2h, w2l,
+    h1_ref, h2_ref, x_ref, member_ref, sums_ref, w1h, w1l, w2h, w2l,
 ):
     spot, core, half, chain = place()
     width = w1h.shape[1]
@@ -100,8 +99,7 @@
 
     x = jnp.concatenate([x0, x1], axis=0)
     x_ref[...] = x
-    vec = vec_ref[half]
-    c1, c2, w3 = vec[0:1, :], vec[1:2, :], vec[2:3, :]
+    c1, c2, w3 = [vec_ref[kind, pl.ds(half, 1), :] for kind in range(3)]
     w1 = (w1h[...], w1l[...])
     w2 = (w2h[...], w2l[...])
     h1 = jnp.tanh(product(split(x), w1, NN) + c1)
@@ -112,11 +110,17 @@
     sums_ref[0:1, :] = jnp.sum(member * energy, axis=0, keepdims=True)
     sums_ref[1:2, :] = jnp.sum(member, axis=0, keepdims=True)
     sums_ref[2:8, :] = jnp.zeros((6, 128), F32)
+
+
+def backward_kernel(h1_ref, h2_ref, vec_ref, w1h, w1l, w2h, w2l, g2_ref, g1_ref, f_ref):
+    spot, core, half, chain = place()
+    w3 = vec_ref[2, pl.ds(half, 1), :]
+    h1, h2 = h1_ref[...], h2_ref[...]
     g2 = w3 * (1.0 - h2 * h2)
     g2_ref[...] = g2
-    g1 = product(split(g2), w2, NT) * (1.0 - h1 * h1)
+    g1 = product(split(g2), (w2h[...], w2l[...]), NT) * (1.0 - h1 * h1)
     g1_ref[...] = g1
-    f_ref[...] = product(split(g1), w1, NT)
+    f_ref[...] = product(split(g1), (w1h[...], w1l[...]), NT)
 
 
 def force_kernel(mine, theirs, refs, near, member, f_ref, force_near, force_far, adj_ref, pot_ref):
@@ -146,7 +150,9 @@
     force_far[1] = jnp.where(has0, 0.0, f1)
 
 
-def gradient_kernel(adj_ref, pot_ref, h1_ref, h2_ref, g2_ref, g1_ref, x_ref, keep, give, dw1, dw2):
+def gradient_kernel(
+    adj_ref, pot_ref, h1_ref, h2_ref, g2_ref, g1_ref, x_ref, keep_far, give_far, keep_near, give_near, dw1, dw2,
+):
     spot, core, half, chain = place()
     adj = adj_ref[...][:, 0:1]
     g2 = adj * g2_ref[...]
@@ -156,15 +162,16 @@
     rows1 = dw1.shape[0] // 16
     rows2 = dw2.shape[0] // 16
     rows = rows1 + rows2
-    for delta in range(8):
-        for out, holder in ((keep, core), (give, 1 - core)):
-            owner = (spot ^ delta) * 2 + holder
-            base = delta * rows
-            at = pl.ds(pl.multiple_of(owner * rows1, rows1), rows1)
-            out[base : base + rows1, :] = dw1[at, :]
-            at = pl.ds(pl.multiple_of(owner * rows2, rows2), rows2)
-            out[base + rows1 : base + rows, :] = dw2[at, :]
-    base = 8 * rows
+    for far, keep, give in ((4, keep_far, give_far), (0, keep_near, give_near)):
+        for index, delta in enumerate((0, 2, 1, 3)):
+            for out, holder in ((keep, core), (give, 1 - core)):
+                owner = (spot ^ (delta + far)) * 2 + holder
+                base = index * rows
+                at = pl.ds(pl.multiple_of(owner * rows1, rows1), rows1)
+                out[base : base + rows1, :] = dw1[at, :]
+                at = pl.ds(pl.multiple_of(owner * rows2, rows2), rows2)
+                out[base + rows1 : base + rows, :] = dw2[at, :]
+    base = 4 * rows
     width = g2.shape[1]
     vec = [
         jnp.sum(g1, axis=0, keepdims=True),
@@ -173,22 +180,95 @@
         jnp.broadcast_to(pot_ref[0:1, 0:1], (1, width)),
     ]
     tail = jnp.concatenate(vec + [jnp.zeros((4, width), F32)], axis=0)
-    keep[base : base + 8, :] = tail
-    give[base : base + 8, :] = tail
-
-
-def core_sum_kernel(keep, came, s0, s1, s2, s3, o0, o1, o2, o3):
-    rows = s0.shape[0]
-    for delta, out in enumerate((s0, s1, s2, s3, o0, o1, o2, o3)):
-        at = slice(delta * rows, (delta + 1) * rows)
-        out[0:rows, :] = keep[at, :] + came[at, :]
-        if delta >= 4:
-            at = slice(8 * rows, 8 * rows + 8)
-            out[rows : rows + 8, :] = keep[at, :] + came[at, :]
-
-
-def four_sum_kernel(a, b, c, d, out):
-    out[...] = (a[...] + b[...]) + (c[...] + d[...])
+    keep_far[base : base + 8, :] = tail
+    give_far[base : base + 8, :] = tail
+
+
+def halving_kernel(keep, came, stay, leave):
+    tail = stay.shape[0] % 48
+    rows = stay.shape[0] - tail
+    stay[0:rows, :] = keep[0:rows, :] + came[0:rows, :]
+    leave[0:rows, :] = keep[rows : 2 * rows, :] + came[rows : 2 * rows, :]
+    if tail:
+        end = keep[2 * rows :, :] + came[2 * rows :, :]
+        stay[rows:, :] = end
+        leave[rows:, :] = end
+
+
+def sum_kernel(a, b, out):
+    out[...] = a[...] + b[...]
+
+
+def message_kernel(desc_hbm, counts_hbm, ids_hbm, refs_hbm, message, near, counts, ids, refs, sems):
+    spot, core, half, chain = place()
+    atoms = message.shape[0] - 8
+    loads = [
+        pltpu.make_async_copy(source, target, sems.at[index])
+        for index, (source, target) in enumerate(
+            (
+                (counts_hbm, counts),
+                (ids_hbm, ids),
+                (refs_hbm, refs),
+                (desc_hbm.at[1 - half, chain], message.at[pl.ds(0, atoms)]),
+            )
+        )
+    ]
+    for load in loads:
+        load.start()
+    for load in loads:
+        load.wait()
+    for out, base, element in ((near, 0, half), (message, atoms, 1 - half)):
+        out[base : base + 8, :] = jnp.zeros((8, 2 * atoms), F32)
+        row = ids[element].astype(F32)
+        out[base : base + 1, 0:atoms] = row[0:1]
+        out[base : base + 1, atoms:] = row[1:2]
+        number = counts[pl.ds(element, 1), :].astype(F32)
+        out[base + 1 : base + 2, 0:2] = number
+        out[base + 2 : base + 3, 0 : refs.shape[1]] = refs[...]
+
+
+def final_kernel(
+    mine, beyond, came, first, second, vec, first_mom, second_mom, vec_mom, force_near, force_came,
+    new_first, new_second, new_vec, new_first_mom, new_second_mom, new_vec_mom, potential, forces,
+    flat_first, flat_second, sems,
+):
+    spot, core, half, chain = place()
+    near_copy = pltpu.make_async_copy(force_near, forces.at[half], sems.at[0])
+    far_copy = pltpu.make_async_copy(force_came, forces.at[1 - half], sems.at[1])
+    near_copy.start()
+    far_copy.start()
+    hidden = mine.shape[1]
+    rows1 = flat_first.shape[1] // hidden
+    rows2 = flat_second.shape[1] // hidden
+    rows = rows1 + rows2
+    for source, element in ((mine, half), (came, 1 - half)):
+        for row in range(rows1):
+            flat_first[pl.ds(element, 1), row * hidden : (row + 1) * hidden] = source[row : row + 1, :]
+        for row in range(rows2):
+            flat_second[pl.ds(element, 1), row * hidden : (row + 1) * hidden] = source[rows1 + row : rows1 + row + 1, :]
+    for grad, value, momentum, new_value, new_momentum in (
+        (flat_first, first, first_mom, new_first, new_first_mom),
+        (flat_second, second, second_mom, new_second, new_second_mom),
+    ):
+        moved = momentum[...] - STEP_SIZE * grad[...]
+        new_momentum[...] = moved
+        new_value[...] = value[...] + STEP_SIZE * moved
+    low = jnp.full((1, hidden), half, jnp.int32) == 0
+    for kind in range(3):
+        own = beyond[rows + kind : rows + kind + 1, :]
+        other = came[rows + kind : rows + kind + 1, :]
+        for element in range(2):
+            grad = jnp.where(low, own, other) if element == 0 else jnp.where(low, other, own)
+            moved = vec_mom[kind, element : element + 1, :] - STEP_SIZE * grad
+            new_vec_mom[kind, element : element + 1, :] = moved
+            new_vec[kind, element : element + 1, :] = vec[kind, element : element + 1, :] + STEP_SIZE * moved
+    potential[...] = beyond[rows + 3 : rows + 4, 0:128] * (1.0 / 512.0)
+    near_copy.wait()
+    far_copy.wait()
+
+
+def after(value, *others):
+    return lax.optimization_barrier((value,) + others)[0]
 
 
 def flip(axis, delta, size):
@@ -216,83 +296,110 @@
     own = pick(shards, half)
     got = to[4](pick(shards, 1 - half))
 
-    def meta_of(at):
-        ids = pick(struct_ids, at).astype(F32).reshape(1, slots * atoms)
-        number = jnp.pad(pick(counts, at).astype(F32).reshape(1, slots), ((0, 0), (0, slots * atoms - slots)))
-        refs = jnp.pad(ref_energy.reshape(1, structs), ((0, 0), (0, slots * atoms - structs)))
-        return jnp.concatenate([ids, number, refs, jnp.zeros((5, slots * atoms), F32)], axis=0)
-
-    meta = meta_of(half)
-    sent_desc = lax.dynamic_slice(descriptors, (1 - half, chain, 0, 0), (1, 1, atoms, width)).reshape(atoms, width)
-    message = to[4](jnp.concatenate([sent_desc, meta_of(1 - half)], axis=0))
+    any_space = pl.BlockSpec(memory_space=pl.ANY)
+    vmem = pl.BlockSpec(memory_space=VMEM)
+    message, meta = pl.pallas_call(
+        message_kernel,
+        out_shape=[jax.ShapeDtypeStruct((atoms + 8, width), F32), jax.ShapeDtypeStruct((8, width), F32)],
+        in_specs=[pl.BlockSpec(memory_space=pltpu.HBM)] * 4,
+        out_specs=[vmem] * 2,
+        scratch_shapes=[
+            pltpu.VMEM(counts.shape, jnp.int32), pltpu.VMEM(struct_ids.shape, jnp.int32), pltpu.VMEM((1, structs), F32),
+            pltpu.SemaphoreType.DMA((4,)),
+        ],
+        compiler_params=pltpu.CompilerParams(vmem_limit_bytes=60 * 1024 * 1024),
+        name="message",
+    )(descriptors, counts, struct_ids, ref_energy.reshape(1, structs))
+    message = to[4](message)
+    own_came = [to[delta](own) for delta in (1, 2, 3)]
+    got = after(got, message, *own_came)
     direct = message[:atoms]
     far_meta = message[atoms:]
     shared = to_chain(direct)
-    own_set = jnp.concatenate([own] + [to[delta](own) for delta in (1, 2, 3)], axis=0)
+    own_set = jnp.concatenate(lax.optimization_barrier((own, *own_came, got))[:4], axis=0)
     own_across = to_core(own_set)
     got_set = jnp.concatenate([got] + [to[delta](got) for delta in (1, 2, 3)], axis=0)
-    got_across = to_core(got_set)
+    got_across = to_core(after(got_set, shared))
 
     work = slots * atoms
-    h1, h2, g2, g1, f, x, member, sums = call(
+    vec = vectors.transpose(1, 0, 2)
+    h1, h2, x, member, sums, *weights = call(
         forward_kernel,
-        [(work, hidden)] * 4 + [(work, width)] * 2 + [(work, 128), (8, 128)],
-        (descriptors, meta, direct, shared, far_meta, vectors, own_set, own_across, got_set, got_across),
-        scratch=[pltpu.VMEM((width, hidden), BF16)] * 2 + [pltpu.VMEM((hidden, hidden), BF16)] * 2,
-        flops=12 * work * hidden * (width + hidden),
-        size=8 * 1024 * 1024,
+        [((work, hidden),)] * 2 + [((work, width),), ((work, 128),), ((8, 128),)]
+        + [((width, hidden), BF16)] * 2 + [((hidden, hidden), BF16)] * 2,
+        (descriptors, meta, direct, shared, far_meta, vec, own_set, own_across, got_set, got_across),
+        flops=6 * work * hidden * (width + hidden),
+        size=6 * 1024 * 1024,
         name="forward",
+    )
+    sums_came = to[4](sums)
+    g2, g1, f = call(
+        backward_kernel,
+        [((work, hidden),)] * 2 + [((work, width),)],
+        (h1, h2, vec, *weights),
+        flops=6 * work * hidden * (width + hidden),
+        size=6 * 1024 * 1024,
+        name="backward",
     )
     refs = jnp.concatenate([meta[2:3, 0:structs], far_meta[2:3, 0:structs], jnp.zeros((1, 128 - 2 * structs), F32)], axis=1)
     force_near, force_far, adj, pot = call(
         force_kernel,
-        [(slots, atoms, width)] * 2 + [(work, 128), (8, 128)],
-        (sums, to[4](sums), refs, meta, member, f),
+        [((slots, atoms, width),)] * 2 + [((work, 128),), ((8, 128),)],
+        (sums, sums_came, refs, meta, member, f),
         size=2 * 1024 * 1024,
         name="force",
     )
     force_came = to[4](force_far)
-    total_rows = 8 * rows + 8
-    keep, give = call(
+    tail = 8
+    group = 4 * rows
+    keep_far, give_far, keep_near, give_near = call(
         gradient_kernel,
-        [(total_rows, hidden)] * 2,
+        [((group + tail, hidden),)] * 2 + [((group, hidden),)] * 2,
         (adj, pot, h1, h2, g2, g1, x),
         scratch=[pltpu.VMEM((width, hidden), F32), pltpu.VMEM((hidden, hidden), F32)],
         flops=6 * work * hidden * (width + hidden),
         size=4 * 1024 * 1024,
         name="gradient",
     )
-    parts = call(
-        core_sum_kernel,
-        [(rows, hidden)] * 4 + [(rows + 8, hidden)] * 4,
-        (keep, to_core(give)),
-        size=3 * 1024 * 1024,
-        name="core_sum",
-    )
-    beyond = [parts[4]] + [to[delta](parts[4 + delta]) for delta in (1, 2, 3)]
-    (beyond_sum,) = call(four_sum_kernel, [(rows + 8, hidden)], beyond, size=500 * 1024, name="beyond_sum")
-    came = to[4](beyond_sum)
-    mine = [parts[0]] + [to[delta](parts[delta]) for delta in (1, 2, 3)]
-    (mine_sum,) = call(four_sum_kernel, [(rows, hidden)], mine, size=500 * 1024, name="mine_sum")
-
-    low = half == 0
-    order = lambda a, b: jnp.where(low, jnp.stack([a, b]), jnp.stack([b, a]))
-    grads = order(mine_sum, came[:rows])
-    tails = order(beyond_sum[rows:], came[rows:])
-    share_first = grads[:, :rows1].reshape(nelem, rows1 * hidden)
-    share_second = grads[:, rows1:].reshape(nelem, rows2 * hidden)
-    grad_vectors = tails[:, 0:3, :]
-    potential_sum = beyond_sum[rows + 3, 0:1]
-    force_partials = order(force_near, force_came)
-    new_first_mom = first_momentum - STEP_SIZE * share_first
-    new_second_mom = second_momentum - STEP_SIZE * share_second
-    new_vector_mom = vector_momentum - STEP_SIZE * grad_vectors
-    new_first = first_layer + STEP_SIZE * new_first_mom
-    new_second = second_layer + STEP_SIZE * new_second_mom
-    new_vectors = vectors + STEP_SIZE * new_vector_mom
-    potential = potential_sum / (structs * 16)
+
+    def halve(keep, came, end, name):
+        left = (keep.shape[0] - end) // 2 + end
+        return call(halving_kernel, [((left, hidden),)] * 2, (keep, came), size=4 * 4 * left * hidden, name=name)
+
+    far_stay, far_leave = halve(keep_far, to_core(give_far), tail, "far_core")
+    near_stay, near_leave = halve(keep_near, to_core(give_near), 0, "near_core")
+    far_came = to[1](far_leave)
+    far_stay, far_leave = halve(far_stay, far_came, tail, "far_x")
+    near_came = to[1](after(near_leave, far_came))
+    far_came = to[2](far_leave)
+    near_stay, near_leave = halve(near_stay, near_came, 0, "near_x")
+    (beyond_sum,) = call(sum_kernel, [((rows + tail, hidden),)], (far_stay, far_came), size=400 * 1024, name="far_z")
+    came = to[4](after(beyond_sum, force_came))
+    (mine_sum,) = call(sum_kernel, [((rows, hidden),)], (near_stay, to[2](near_leave)), size=400 * 1024, name="near_z")
+    shape = lambda x: jax.ShapeDtypeStruct(x.shape, F32)
+    vec_mom = vector_momentum.transpose(1, 0, 2)
+    (
+        new_first, new_second, new_vec, new_first_mom, new_second_mom, new_vec_mom, potential, force_partials,
+    ) = pl.pallas_call(
+        final_kernel,
+        out_shape=[
+            shape(first_layer), shape(second_layer), shape(vec), shape(first_layer), shape(second_layer), shape(vec),
+            jax.ShapeDtypeStruct((1, 128), F32), shape(descriptors),
+        ],
+        in_specs=[vmem] * 11,
+        out_specs=[vmem] * 7 + [any_space],
+        scratch_shapes=[
+            pltpu.VMEM(first_layer.shape, F32), pltpu.VMEM(second_layer.shape, F32), pltpu.SemaphoreType.DMA((2,)),
+        ],
+        compiler_params=pltpu.CompilerParams(vmem_limit_bytes=8 * 1024 * 1024),
+        name="final",
+    )(
+        mine_sum, beyond_sum, came, first_layer, second_layer, vec, first_momentum, second_momentum, vec_mom,
+        force_near, after(force_came, came, mine_sum),
+    )
     return (
-        new_first, new_second, new_vectors, new_first_mom, new_second_mom, new_vector_mom, potential, force_partials,
+        new_first, new_second, new_vec.transpose(1, 0, 2), new_first_mom, new_second_mom,
+        new_vec_mom.transpose(1, 0, 2), potential[0, 0:1], force_partials,
     )
 
 

time: 82.1 us -> 65.5 us (0.80)
  waiting for transfers between devices: 45.7 us -> 29.9 us
  starting transfers between devices: 21.3 us -> 26.3 us
  local copies, waits for them, and re-layouts: 5.87 us -> 1.06 us
  Pallas kernels: 3.56 us -> 7.11 us
  other arithmetic: 2.57 us -> 0.08 us
  between operations: 2.82 us -> 0.92 us
    ppermute x21 -> x20, waiting for transfers between devices: 45.7 us -> 29.9 us  [flip(): lax.ppermute(x, axis, [(i, i ^ delta) for i in range(size)])]
    ppermute x21 -> x20, starting transfers between devices: 21.3 us -> 26.3 us  [flip(): lax.ppermute(x, axis, [(i, i ^ delta) for i in range(size)])]
    unnamed x29 -> x23, local copies, waits for them, and re-layouts: 5.2 us -> 0.98 us
    pallas_call x6 -> x12, Pallas kernels: 3.56 us -> 7.11 us  [the longest x10 3.86 us: call(): pl.pallas_call(kernel, out_shape=[jax.ShapeDtypeStruct(shape, kind) for s...]
    add x3 -> x0, other arithmetic: 1.57 us -> none  [the longest x1 0.83 us: halves(): new_second = second_layer + STEP_SIZE * new_second_mom]
    select_n x2 -> x0, other arithmetic: 0.86 us -> none  [halves(): order = lambda a, b: jnp.where(low, jnp.stack([a, b]), jnp.stack([b, a]))]
  transfers between devices with their start and end apart: 21 -> 20, of which waited for: 10 -> 10; matrix products, arithmetic and copies ran while one was open for 1% -> 0% of each run, Pallas kernels for 0% -> 2%
where the time goes in v2:
time: 65.5 us; the launch traced here: 65.4 us
  waiting for transfers between devices  29.9 us (46%)
  starting transfers between devices  26.3 us (40%)
  Pallas kernels  7.11 us (11%)
  local copies, waits for them, and re-layouts  1.06 us (2%)
  between operations  0.92 us (1%)
    ppermute x20, waiting for transfers between devices, flip(): lax.ppermute(x, axis, [(i, i ^ delta) for i in range(size)])  29.9 us
    ppermute x20, starting transfers between devices, flip(): lax.ppermute(x, axis, [(i, i ^ delta) for i in range(size)])  26.3 us
    pallas_call x10, Pallas kernels, call(): pl.pallas_call(kernel, out_shape=[jax.ShapeDtypeStruct(shape, kind) for s...  3.86 us
    pallas_call x1, Pallas kernels, halves(): pl.pallas_call(message_kernel, out_shape=[jax.ShapeDtypeStruct((atoms + 8...  1.69 us
    pallas_call x1, Pallas kernels, halves(): pl.pallas_call(final_kernel, out_shape=[shape(first_layer), shape(second_...  1.57 us
  transfers between devices with their start and end apart: 20, of which 10 were waited for; matrix products, arithmetic and copies ran while one was open for 0% of the time, Pallas kernels for 2%

profile of v2, /device:TPU:0, one launch (start us, length us, event | category | flops | bytes accessed | tf_op | source)
XLA Modules:
  0.0 65.4 jit_solution(17546182563275258311)
XLA Ops:
  0.6 0.0 copy-start.2
  0.6 1.7 %message.1 = (f32[136,256]{1,0:T(8,128)}, f32[8,256]{1,0:T(8,128)}) custom-call(f32[2,2,128,256]{3,2,1,0:T(8,128)} %desc_ref.1, s32[2,2]{1,0:T(2,128)} %counts_hbm.1, s32[2,2,128]{2,1,0:T(2,128)} %ids_hbm.1, f32[1,32]{1,0:T(1,128)} %bitcast.25), custom_call_target="tpu_custom_call" | custom-call | tf_op jit(solution)/shard_map/message/pallas_call | solution.py:301
  2.3 0.0 copy-start.1
  2.4 4.1 %collective-permute-start = (f32[136,256]{1,0:T(8,128)}, f32[136,256]{1,0:T(8,128)S(1)}, u32[]{:S(2)}, u32[]{:S(2)}) collective-permute-start(f32[136,256]{1,0:T(8,128)} %get-tuple-element.56), channel_id=1, source_target_pairs={{0,8},{2,10},{4,12},{6,14},{8,0},{10,2},{12,4},{14,6},{1,9},{3,11}... | collective-permute-start | bytes 417800 | tf_op jit(solution)/shard_map/ppermute | solution.py:275
  6.5 0.0 copy-done.2
  6.5 0.0 copy-done.1
  6.6 0.8 %collective-permute-start.5 = (f32[48,512]{1,0:T(8,128)S(1)}, f32[48,512]{1,0:T(8,128)S(1)}, u32[]{:S(2)}, u32[]{:S(2)}) collective-permute-start(f32[48,512]{1,0:T(8,128)S(1)} %get-tuple-element.102), channel_id=1, source_target_pairs={{0,8},{2,10},{4,12},{6,14},{8,0},{10,2},{12,4},{14,6},{1,9},{3,11}... | collective-permute-start | bytes 294920 | tf_op jit(solution)/shard_map/ppermute | solution.py:275
  7.4 2.5 %collective-permute-start.4 = (f32[48,512]{1,0:T(8,128)S(1)}, f32[48,512]{1,0:T(8,128)S(1)}, u32[]{:S(2)}, u32[]{:S(2)}) collective-permute-start(f32[48,512]{1,0:T(8,128)S(1)} %get-tuple-element.58), channel_id=1, source_target_pairs={{0,6},{2,4},{4,2},{6,0},{8,14},{10,12},{12,10},{14,8},{1,7},{3,5},... | collective-permute-start | bytes 294920 | tf_op jit(solution)/shard_map/ppermute | solution.py:275
  9.9 0.4 collective-permute-start.3
  10.4 0.5 collective-permute-start.2
  10.9 6.7 %collective-permute-done.5 = f32[48,512]{1,0:T(8,128)S(1)} collective-permute-done((f32[48,512]{1,0:T(8,128)S(1)}, f32[48,512]{1,0:T(8,128)S(1)}, u32[]{:S(2)}, u32[]{:S(2)}) %collective-permute-start.5) | collective-permute-done | bytes 98336 | tf_op jit(solution)/shard_map/ppermute | solution.py:275
  17.6 0.0 collective-permute-done.4
  17.6 1.2 %collective-permute-done.3 = f32[48,512]{1,0:T(8,128)S(1)} collective-permute-done((f32[48,512]{1,0:T(8,128)S(1)}, f32[48,512]{1,0:T(8,128)S(1)}, u32[]{:S(2)}, u32[]{:S(2)}) %collective-permute-start.3) | collective-permute-done | bytes 98336 | tf_op jit(solution)/shard_map/ppermute | solution.py:275
  18.9 0.0 collective-permute-done.2
  18.9 0.0 collective-permute-done
  18.9 0.5 collective-permute-start.9
  19.4 1.5 %collective-permute-start.8 = (f32[48,512]{1,0:T(8,128)S(1)}, f32[48,512]{1,0:T(8,128)S(1)}, u32[]{:S(2)}, u32[]{:S(2)}) collective-permute-start(f32[48,512]{1,0:T(8,128)S(1)} %collective-permute-done.5), channel_id=1, source_target_pairs={{0,4},{2,6},{4,0},{6,2},{8,12},{10,14},{12,8},{14,10},{1,5},{3,7},... | collective-permute-start | bytes 294920 | tf_op jit(solution)/shard_map/ppermute | solution.py:275
  20.9 1.4 %collective-permute-start.7 = (f32[48,512]{1,0:T(8,128)S(1)}, f32[48,512]{1,0:T(8,128)S(1)}, u32[]{:S(2)}, u32[]{:S(2)}) collective-permute-start(f32[48,512]{1,0:T(8,128)S(1)} %collective-permute-done.5), channel_id=1, source_target_pairs={{0,2},{2,0},{4,6},{6,4},{8,10},{10,8},{12,14},{14,12},{1,3},{3,1},... | collective-permute-start | bytes 294920 | tf_op jit(solution)/shard_map/ppermute | solution.py:275
  22.4 1.6 %collective-permute-start.1 = (f32[128,256]{1,0:T(8,128)S(1)}, f32[128,256]{1,0:T(8,128)S(1)}, u32[]{:S(2)}, u32[]{:S(2)}) collective-permute-start(f32[128,256]{1,0:T(8,128)S(1)} %slice.21.first_far), channel_id=1, source_target_pairs={{0,16},{16,0},{1,17},{17,1},{2,18},{18,2},{3,19},{19,3},{4,20},{20... | collective-permute-start | bytes 393224 | tf_op jit(solution)/shard_map/ppermute | solution.py:275
  24.0 0.0 copy-start
  24.1 0.1 collective-permute-start.6
  24.2 1.4 %collective-permute-done.7 = f32[48,512]{1,0:T(8,128)S(1)} collective-permute-done((f32[48,512]{1,0:T(8,128)S(1)}, f32[48,512]{1,0:T(8,128)S(1)}, u32[]{:S(2)}, u32[]{:S(2)}) %collective-permute-start.7) | collective-permute-done | bytes 98336 | tf_op jit(solution)/shard_map/ppermute | solution.py:275
  25.5 0.0 collective-permute-done.8
  25.6 0.0 copy-start.6
  25.6 0.0 collective-permute-done.9
  25.6 0.0 copy-start.4
  25.6 1.8 %collective-permute-done.1.second_far = f32[128,256]{1,0:T(8,128)S(1)} collective-permute-done((f32[128,256]{1,0:T(8,128)S(1)}, f32[128,256]{1,0:T(8,128)S(1)}, u32[]{:S(2)}, u32[]{:S(2)}) %collective-permute-start.1) | collective-permute-done | bytes 131104 | tf_op jit(solution)/shard_map/ppermute | solution.py:275
  27.4 0.0 collective-permute-start.10
  27.4 0.0 copy-done.6
  27.4 0.0 collective-permute-done.6.own1
  27.5 1.7 %collective-permute-done.10.rec1 = f32[192,512]{1,0:T(8,128)S(1)} collective-permute-done((f32[192,512]{1,0:T(8,128)S(1)}, f32[192,512]{1,0:T(8,128)S(1)}, u32[]{:S(2)}, u32[]{:S(2)}) %collective-permute-start.10) | collective-permute-done | bytes 393248 | tf_op jit(solution)/shard_map/ppermute | solution.py:275
  29.1 0.0 copy-done
  29.1 0.0 copy-done.4
  29.1 1.3 %forward.1 = (f32[256,512]{1,0:T(8,128)S(1)}, f32[256,512]{1,0:T(8,128)S(1)}, f32[256,256]{1,0:T(8,128)S(1)}, f32[256,128]{1,0:T(8,128)S(1)}, f32[8,128]{1,0:T(8...) custom-call(f32[2,2,128,256]{3,2,1,0:T(8,128)S(1)} %copy-done, ...), custom_call_target="tpu_custom_call" | custom-call | flops 1 | bytes 1 | tf_op jit(solution)/shard_map/forward/pallas_call | solution.py:32
  30.4 2.3 %collective-permute-start.11 = (f32[8,128]{1,0:T(8,128)S(1)}, f32[8,128]{1,0:T(8,128)S(1)}, u32[]{:S(2)}, u32[]{:S(2)}) collective-permute-start(f32[8,128]{1,0:T(8,128)S(1)} %get-tuple-element.63.mine), channel_id=1, source_target_pairs={{0,8},{2,10},{4,12},{6,14},{8,0},{10,2},{12,4},{14,6},{1,9},{3,11}... | collective-permute-start | bytes 12296 | tf_op jit(solution)/shard_map/ppermute | solution.py:275
  32.7 0.1 bitcast_maximum_fusion.refs
  32.8 1.2 %backward.1 = (f32[256,512]{1,0:T(8,128)S(1)}, f32[256,512]{1,0:T(8,128)S(1)}, f32[256,256]{1,0:T(8,128)S(1)}) custom-call(f32[256,512]{1,0:T(8,128)S(1)} %get-tuple-element.65.h1_ref, f32[256,512]{1,0:T(8,128)S(1)} %get-tuple-element.66.h2_ref, f32[3,2,512]{2,1,0:T(2,128)S(1)} %bitcast.22, bf16[256,512]{1,0:T(8,128)(2,1)S(1)} %get-tuple-element.67.w1h, ...), custom_call_target="tpu_custom_call" | custom-call | flops 1 | bytes 1 | tf_op jit(solution)/shard_map/backward/pallas_call | solution.py:32
  34.0 1.0 %collective-permute-done.11.theirs = f32[8,128]{1,0:T(8,128)S(1)} collective-permute-done((f32[8,128]{1,0:T(8,128)S(1)}, f32[8,128]{1,0:T(8,128)S(1)}, u32[]{:S(2)}, u32[]{:S(2)}) %collective-permute-start.11) | collective-permute-done | bytes 4128 | tf_op jit(solution)/shard_map/ppermute | solution.py:275
  35.0 0.2 force.1
  35.2 1.0 %gradient.1 = (f32[200,512]{1,0:T(8,128)S(1)}, f32[200,512]{1,0:T(8,128)S(1)}, f32[192,512]{1,0:T(8,128)S(1)}, f32[192,512]{1,0:T(8,128)S(1)}) custom-call(f32[256,128]{1,0:T(8,128)S(1)} %get-tuple-element.72.adj_ref, f32[8,128]{1,0:T(8,128)S(1)} %get-tuple-element.73.pot_ref, f32[256,512]{1,0:T(8,128)S(1)} %get-tuple-element.65.h1_ref, ...), custom_call_target="tpu_custom_call" | custom-call | flops 1 | bytes 1 | tf_op jit(solution)/shard_map/gradient/pallas_call | solution.py:32
  36.2 0.1 collective-permute-start.13
  36.3 0.5 collective-permute-start.12
  36.8 1.2 %collective-permute-done.13.came = f32[200,512]{1,0:T(8,128)S(1)} collective-permute-done((f32[200,512]{1,0:T(8,128)S(1)}, f32[200,512]{1,0:T(8,128)S(1)}, u32[]{:S(2)}, u32[]{:S(2)}) %collective-permute-start.13) | collective-permute-done | bytes 409632 | tf_op jit(solution)/shard_map/ppermute | solution.py:275
  38.1 0.7 collective-permute-start.14
  38.8 2.3 %collective-permute-start.18 = (f32[2,128,256]{2,1,0:T(8,128)S(1)}, f32[2,128,256]{2,1,0:T(8,128)S(1)}, u32[]{:S(2)}, u32[]{:S(2)}) collective-permute-start(f32[2,128,256]{2,1,0:T(8,128)S(1)} %get-tuple-element.90), channel_id=1, source_target_pairs={{0,8},{2,10},{4,12},{6,14},{8,0},{10,2},{12,4},{14,6},{1,9},{3,11}... | collective-permute-start | bytes 786440 | tf_op jit(solution)/shard_map/ppermute | solution.py:275
  41.0 0.0 collective-permute-done.12.came
  41.1 4.4 %collective-permute-done.14.came = f32[104,512]{1,0:T(8,128)S(1)} collective-permute-done((f32[104,512]{1,0:T(8,128)S(1)}, f32[104,512]{1,0:T(8,128)S(1)}, u32[]{:S(2)}, u32[]{:S(2)}) %collective-permute-start.14) | collective-permute-done | bytes 213024 | tf_op jit(solution)/shard_map/ppermute | solution.py:275
  45.5 0.6 collective-permute-start.15
  46.1 1.4 %collective-permute-start.17 = (f32[56,512]{1,0:T(8,128)S(1)}, f32[56,512]{1,0:T(8,128)S(1)}, u32[]{:S(2)}, u32[]{:S(2)}) collective-permute-start(f32[56,512]{1,0:T(8,128)S(1)} %get-tuple-element.89), channel_id=1, source_target_pairs={{0,4},{2,6},{4,0},{6,2},{8,12},{10,14},{12,8},{14,10},{1,5},{3,7},... | collective-permute-start | bytes 344072 | tf_op jit(solution)/shard_map/ppermute | solution.py:275
  47.4 7.3 %collective-permute-done.17.b = f32[56,512]{1,0:T(8,128)S(1)} collective-permute-done((f32[56,512]{1,0:T(8,128)S(1)}, f32[56,512]{1,0:T(8,128)S(1)}, u32[]{:S(2)}, u32[]{:S(2)}) %collective-permute-start.17) | collective-permute-done | bytes 114720 | tf_op jit(solution)/shard_map/ppermute | solution.py:275
  54.8 0.0 collective-permute-done.18.force_came
  54.8 2.4 %collective-permute-start.19 = (f32[56,512]{1,0:T(8,128)S(1)}, f32[56,512]{1,0:T(8,128)S(1)}, u32[]{:S(2)}, u32[]{:S(2)}) collective-permute-start(f32[56,512]{1,0:T(8,128)S(1)} %far_z.1.beyond), channel_id=1, source_target_pairs={{0,8},{2,10},{4,12},{6,14},{8,0},{10,2},{12,4},{14,6},{1,9},{3,11}... | collective-permute-start | bytes 344072 | tf_op jit(solution)/shard_map/ppermute | solution.py:275
  57.2 0.0 collective-permute-done.15.came
  57.2 2.5 %collective-permute-start.16 = (f32[48,512]{1,0:T(8,128)S(1)}, f32[48,512]{1,0:T(8,128)S(1)}, u32[]{:S(2)}, u32[]{:S(2)}) collective-permute-start(f32[48,512]{1,0:T(8,128)S(1)} %get-tuple-element.86), channel_id=1, source_target_pairs={{0,4},{2,6},{4,0},{6,2},{8,12},{10,14},{12,8},{14,10},{1,5},{3,7},... | collective-permute-start | bytes 294920 | tf_op jit(solution)/shard_map/ppermute | solution.py:275
  59.7 3.2 %collective-permute-done.16.b = f32[48,512]{1,0:T(8,128)S(1)} collective-permute-done((f32[48,512]{1,0:T(8,128)S(1)}, f32[48,512]{1,0:T(8,128)S(1)}, u32[]{:S(2)}, u32[]{:S(2)}) %collective-permute-start.16) | collective-permute-done | bytes 98336 | tf_op jit(solution)/shard_map/ppermute | solution.py:275
  62.9 0.0 copy-start.3
  62.9 0.0 copy-start.5
  62.9 0.0 copy-start.7
  62.9 0.0 collective-permute-done.19.came
  62.9 0.9 %copy-done.3 = f32[2,16384]{1,0:T(2,128)S(1)} copy-done((f32[2,16384]{1,0:T(2,128)S(1)}, f32[2,16384]{1,0:T(2,128)}, u32[]{:S(2)}) %copy-start.3) | copy-done | bytes 131096
  63.8 0.0 copy-done.5
  63.8 0.0 copy-done.7
  63.8 1.6 %final.1 = (f32[2,8192]{1,0:T(2,128)}, f32[2,16384]{1,0:T(2,128)}, f32[3,2,512]{2,1,0:T(2,128)}, f32[2,8192]{1,0:T(2,128)}, f32[2,16384]{1,0:T(2,128)}, /*index=...) custom-call(f32[48,512]{1,0:T(8,128)S(1)} %near_z.1.mine, f32[56,512]{1,0:T(8,128)S(1)} %far_z.1.beyond, ...), custom_call_target="tpu_custom_call" | custom-call | tf_op jit(solution)/shard_map/final/pallas_call | solution.py:383
  (22 shorter events, 0.3 us)
Async XLA Ops:
  0.6 5.8 %copy-start.2 = (f32[2,8192]{1,0:T(2,128)S(1)}, f32[2,8192]{1,0:T(2,128)}, u32[]{:S(2)}) copy-start(f32[2,8192]{1,0:T(2,128)} %first.1) | copy-start | bytes 196612
  2.3 4.1 %copy-start.1 = (f32[2,16384]{1,0:T(2,128)S(1)}, f32[2,16384]{1,0:T(2,128)}, u32[]{:S(2)}) copy-start(f32[2,16384]{1,0:T(2,128)} %second.1) | copy-start | bytes 393220
  2.4 16.5 %collective-permute-start = (f32[136,256]{1,0:T(8,128)}, f32[136,256]{1,0:T(8,128)S(1)}, u32[]{:S(2)}, u32[]{:S(2)}) collective-permute-start(f32[136,256]{1,0:T(8,128)} %get-tuple-element.56), channel_id=1, source_target_pairs={{0,8},{2,10},{4,12},{6,14},{8,0},{10,2},{12,4},{14,6},{1,9},{3,11}... | collective-permute-start | bytes 417800 | tf_op jit(solution)/shard_map/ppermute | solution.py:275
  6.6 11.1 %collective-permute-start.5 = (f32[48,512]{1,0:T(8,128)S(1)}, f32[48,512]{1,0:T(8,128)S(1)}, u32[]{:S(2)}, u32[]{:S(2)}) collective-permute-start(f32[48,512]{1,0:T(8,128)S(1)} %get-tuple-element.102), channel_id=1, source_target_pairs={{0,8},{2,10},{4,12},{6,14},{8,0},{10,2},{12,4},{14,6},{1,9},{3,11}... | collective-permute-start | bytes 294920 | tf_op jit(solution)/shard_map/ppermute | solution.py:275
  7.4 10.2 %collective-permute-start.4 = (f32[48,512]{1,0:T(8,128)S(1)}, f32[48,512]{1,0:T(8,128)S(1)}, u32[]{:S(2)}, u32[]{:S(2)}) collective-permute-start(f32[48,512]{1,0:T(8,128)S(1)} %get-tuple-element.58), channel_id=1, source_target_pairs={{0,6},{2,4},{4,2},{6,0},{8,14},{10,12},{12,10},{14,8},{1,7},{3,5},... | collective-permute-start | bytes 294920 | tf_op jit(solution)/shard_map/ppermute | solution.py:275
  9.9 9.0 %collective-permute-start.3 = (f32[48,512]{1,0:T(8,128)S(1)}, f32[48,512]{1,0:T(8,128)S(1)}, u32[]{:S(2)}, u32[]{:S(2)}) collective-permute-start(f32[48,512]{1,0:T(8,128)S(1)} %get-tuple-element.58), channel_id=1, source_target_pairs={{0,4},{2,6},{4,0},{6,2},{8,12},{10,14},{12,8},{14,10},{1,5},{3,7},... | collective-permute-start | bytes 294920 | tf_op jit(solution)/shard_map/ppermute | solution.py:275
  10.4 8.5 %collective-permute-start.2 = (f32[48,512]{1,0:T(8,128)S(1)}, f32[48,512]{1,0:T(8,128)S(1)}, u32[]{:S(2)}, u32[]{:S(2)}) collective-permute-start(f32[48,512]{1,0:T(8,128)S(1)} %get-tuple-element.58), channel_id=1, source_target_pairs={{0,2},{2,0},{4,6},{6,4},{8,10},{10,8},{12,14},{14,12},{1,3},{3,1},... | collective-permute-start | bytes 294920 | tf_op jit(solution)/shard_map/ppermute | solution.py:275
  18.9 6.7 %collective-permute-start.9 = (f32[48,512]{1,0:T(8,128)S(1)}, f32[48,512]{1,0:T(8,128)S(1)}, u32[]{:S(2)}, u32[]{:S(2)}) collective-permute-start(f32[48,512]{1,0:T(8,128)S(1)} %collective-permute-done.5), channel_id=1, source_target_pairs={{0,6},{2,4},{4,2},{6,0},{8,14},{10,12},{12,10},{14,8},{1,7},{3,5},... | collective-permute-start | bytes 294920 | tf_op jit(solution)/shard_map/ppermute | solution.py:275
  19.4 6.2 %collective-permute-start.8 = (f32[48,512]{1,0:T(8,128)S(1)}, f32[48,512]{1,0:T(8,128)S(1)}, u32[]{:S(2)}, u32[]{:S(2)}) collective-permute-start(f32[48,512]{1,0:T(8,128)S(1)} %collective-permute-done.5), channel_id=1, source_target_pairs={{0,4},{2,6},{4,0},{6,2},{8,12},{10,14},{12,8},{14,10},{1,5},{3,7},... | collective-permute-start | bytes 294920 | tf_op jit(solution)/shard_map/ppermute | solution.py:275
  20.9 4.6 %collective-permute-start.7 = (f32[48,512]{1,0:T(8,128)S(1)}, f32[48,512]{1,0:T(8,128)S(1)}, u32[]{:S(2)}, u32[]{:S(2)}) collective-permute-start(f32[48,512]{1,0:T(8,128)S(1)} %collective-permute-done.5), channel_id=1, source_target_pairs={{0,2},{2,0},{4,6},{6,4},{8,10},{10,8},{12,14},{14,12},{1,3},{3,1},... | collective-permute-start | bytes 294920 | tf_op jit(solution)/shard_map/ppermute | solution.py:275
  22.4 5.0 %collective-permute-start.1 = (f32[128,256]{1,0:T(8,128)S(1)}, f32[128,256]{1,0:T(8,128)S(1)}, u32[]{:S(2)}, u32[]{:S(2)}) collective-permute-start(f32[128,256]{1,0:T(8,128)S(1)} %slice.21.first_far), channel_id=1, source_target_pairs={{0,16},{16,0},{1,17},{17,1},{2,18},{18,2},{3,19},{19,3},{4,20},{20... | collective-permute-start | bytes 393224 | tf_op jit(solution)/shard_map/ppermute | solution.py:275
  24.0 5.1 %copy-start = (f32[2,2,128,256]{3,2,1,0:T(8,128)S(1)}, f32[2,2,128,256]{3,2,1,0:T(8,128)}, u32[]{:S(2)}) copy-start(f32[2,2,128,256]{3,2,1,0:T(8,128)} %desc_ref.1) | copy-start | bytes 1572868
  24.1 3.4 %collective-permute-start.6 = (f32[192,512]{1,0:T(8,128)S(1)}, f32[192,512]{1,0:T(8,128)S(1)}, u32[]{:S(2)}, u32[]{:S(2)}) collective-permute-start(f32[192,512]{1,0:T(8,128)S(1)} %constant_dynamic-update-slice_fusion.own0), channel_id=1, source_target_pairs={{0,1},{1,0},{2,3},{3,2},{4,5},{5,4},{6,7},{7,6},{8,9},{9,8},{10,11... | collective-permute-start | bytes 1179656 | tf_op jit(solution)/shard_map/ppermute | solution.py:275
  25.6 1.8 %copy-start.6 = (f32[8,256]{1,0:T(8,128)S(1)}, f32[8,256]{1,0:T(8,128)}, u32[]{:S(2)}) copy-start(f32[8,256]{1,0:T(8,128)} %get-tuple-element.55.meta_ref.near) | copy-start | bytes 24580
  25.6 3.5 %copy-start.4 = (f32[2,3,512]{2,0,1:T(2,128)S(1)}, f32[2,3,512]{2,0,1:T(2,128)}, u32[]{:S(2)}) copy-start(f32[2,3,512]{2,0,1:T(2,128)} %param.16) | copy-start | bytes 36868
  27.4 1.7 %collective-permute-start.10 = (f32[192,512]{1,0:T(8,128)S(1)}, f32[192,512]{1,0:T(8,128)S(1)}, u32[]{:S(2)}, u32[]{:S(2)}) collective-permute-start(f32[192,512]{1,0:T(8,128)S(1)} %constant_dynamic-update-slice_fusion.4.rec0), channel_id=1, source_target_pairs={{0,1},{1,0},{2,3},{3,2},{4,5},{5,4},{6,7},{7,6},{8,9},{9,8},{10,11... | collective-permute-start | bytes 1179656 | tf_op jit(solution)/shard_map/ppermute | solution.py:275
  30.4 4.6 %collective-permute-start.11 = (f32[8,128]{1,0:T(8,128)S(1)}, f32[8,128]{1,0:T(8,128)S(1)}, u32[]{:S(2)}, u32[]{:S(2)}) collective-permute-start(f32[8,128]{1,0:T(8,128)S(1)} %get-tuple-element.63.mine), channel_id=1, source_target_pairs={{0,8},{2,10},{4,12},{6,14},{8,0},{10,2},{12,4},{14,6},{1,9},{3,11}... | collective-permute-start | bytes 12296 | tf_op jit(solution)/shard_map/ppermute | solution.py:275
  36.2 1.8 %collective-permute-start.13 = (f32[200,512]{1,0:T(8,128)S(1)}, f32[200,512]{1,0:T(8,128)S(1)}, u32[]{:S(2)}, u32[]{:S(2)}) collective-permute-start(f32[200,512]{1,0:T(8,128)S(1)} %get-tuple-element.82), channel_id=1, source_target_pairs={{0,1},{1,0},{2,3},{3,2},{4,5},{5,4},{6,7},{7,6},{8,9},{9,8},{10,11... | collective-permute-start | bytes 1228808 | tf_op jit(solution)/shard_map/ppermute | solution.py:275
  36.3 4.7 %collective-permute-start.12 = (f32[192,512]{1,0:T(8,128)S(1)}, f32[192,512]{1,0:T(8,128)S(1)}, u32[]{:S(2)}, u32[]{:S(2)}) collective-permute-start(f32[192,512]{1,0:T(8,128)S(1)} %get-tuple-element.78), channel_id=1, source_target_pairs={{0,1},{1,0},{2,3},{3,2},{4,5},{5,4},{6,7},{7,6},{8,9},{9,8},{10,11... | collective-permute-start | bytes 1179656 | tf_op jit(solution)/shard_map/ppermute | solution.py:275
  38.1 7.4 %collective-permute-start.14 = (f32[104,512]{1,0:T(8,128)S(1)}, f32[104,512]{1,0:T(8,128)S(1)}, u32[]{:S(2)}, u32[]{:S(2)}) collective-permute-start(f32[104,512]{1,0:T(8,128)S(1)} %get-tuple-element.83), channel_id=1, source_target_pairs={{0,2},{2,0},{4,6},{6,4},{8,10},{10,8},{12,14},{14,12},{1,3},{3,1},... | collective-permute-start | bytes 638984 | tf_op jit(solution)/shard_map/ppermute | solution.py:275
  38.8 16.0 %collective-permute-start.18 = (f32[2,128,256]{2,1,0:T(8,128)S(1)}, f32[2,128,256]{2,1,0:T(8,128)S(1)}, u32[]{:S(2)}, u32[]{:S(2)}) collective-permute-start(f32[2,128,256]{2,1,0:T(8,128)S(1)} %get-tuple-element.90), channel_id=1, source_target_pairs={{0,8},{2,10},{4,12},{6,14},{8,0},{10,2},{12,4},{14,6},{1,9},{3,11}... | collective-permute-start | bytes 786440 | tf_op jit(solution)/shard_map/ppermute | solution.py:275
  45.5 11.7 %collective-permute-start.15 = (f32[96,512]{1,0:T(8,128)S(1)}, f32[96,512]{1,0:T(8,128)S(1)}, u32[]{:S(2)}, u32[]{:S(2)}) collective-permute-start(f32[96,512]{1,0:T(8,128)S(1)} %get-tuple-element.84), channel_id=1, source_target_pairs={{0,2},{2,0},{4,6},{6,4},{8,10},{10,8},{12,14},{14,12},{1,3},{3,1},... | collective-permute-start | bytes 589832 | tf_op jit(solution)/shard_map/ppermute | solution.py:275
  46.1 8.7 %collective-permute-start.17 = (f32[56,512]{1,0:T(8,128)S(1)}, f32[56,512]{1,0:T(8,128)S(1)}, u32[]{:S(2)}, u32[]{:S(2)}) collective-permute-start(f32[56,512]{1,0:T(8,128)S(1)} %get-tuple-element.89), channel_id=1, source_target_pairs={{0,4},{2,6},{4,0},{6,2},{8,12},{10,14},{12,8},{14,10},{1,5},{3,7},... | collective-permute-start | bytes 344072 | tf_op jit(solution)/shard_map/ppermute | solution.py:275
  54.8 8.2 %collective-permute-start.19 = (f32[56,512]{1,0:T(8,128)S(1)}, f32[56,512]{1,0:T(8,128)S(1)}, u32[]{:S(2)}, u32[]{:S(2)}) collective-permute-start(f32[56,512]{1,0:T(8,128)S(1)} %far_z.1.beyond), channel_id=1, source_target_pairs={{0,8},{2,10},{4,12},{6,14},{8,0},{10,2},{12,4},{14,6},{1,9},{3,11}... | collective-permute-start | bytes 344072 | tf_op jit(solution)/shard_map/ppermute | solution.py:275
  57.2 5.7 %collective-permute-start.16 = (f32[48,512]{1,0:T(8,128)S(1)}, f32[48,512]{1,0:T(8,128)S(1)}, u32[]{:S(2)}, u32[]{:S(2)}) collective-permute-start(f32[48,512]{1,0:T(8,128)S(1)} %get-tuple-element.86), channel_id=1, source_target_pairs={{0,4},{2,6},{4,0},{6,2},{8,12},{10,14},{12,8},{14,10},{1,5},{3,7},... | collective-permute-start | bytes 294920 | tf_op jit(solution)/shard_map/ppermute | solution.py:275
  62.9 0.9 %copy-start.3 = (f32[2,16384]{1,0:T(2,128)S(1)}, f32[2,16384]{1,0:T(2,128)}, u32[]{:S(2)}) copy-start(f32[2,16384]{1,0:T(2,128)} %second_mom.1) | copy-start | bytes 393220
  62.9 0.9 %copy-start.5 = (f32[2,8192]{1,0:T(2,128)S(1)}, f32[2,8192]{1,0:T(2,128)}, u32[]{:S(2)}) copy-start(f32[2,8192]{1,0:T(2,128)} %first_mom.1) | copy-start | bytes 196612
  62.9 0.9 %copy-start.7 = (f32[2,3,512]{2,0,1:T(2,128)S(1)}, f32[2,3,512]{2,0,1:T(2,128)}, u32[]{:S(2)}) copy-start(f32[2,3,512]{2,0,1:T(2,128)} %param.19) | copy-start | bytes 36868

commit v3 on v2

--- a/solution.py
+++ b/solution.py
@@ -195,7 +195,8 @@
         leave[rows:, :] = end
 
 
-def sum_kernel(a, b, out):
+def sum_kernel(a, b, *rest):
+    out = rest[-1]
     out[...] = a[...] + b[...]
 
 
@@ -307,18 +308,22 @@
             pltpu.VMEM(counts.shape, jnp.int32), pltpu.VMEM(struct_ids.shape, jnp.int32), pltpu.VMEM((1, structs), F32),
             pltpu.SemaphoreType.DMA((4,)),
         ],
-        compiler_params=pltpu.CompilerParams(vmem_limit_bytes=60 * 1024 * 1024),
+        compiler_params=pltpu.CompilerParams(vmem_limit_bytes=4 * 1024 * 1024),
         name="message",
     )(descriptors, counts, struct_ids, ref_energy.reshape(1, structs))
     message = to[4](message)
-    own_came = [to[delta](own) for delta in (1, 2, 3)]
-    got = after(got, message, *own_came)
+    own_z = to[2](own)
+    own_x = to[1](jnp.concatenate([own, own_z]))
+    own_came = [own_x[:rows], own_z, own_x[rows:]]
+    got = after(got, own)
     direct = message[:atoms]
     far_meta = message[atoms:]
     shared = to_chain(direct)
     own_set = jnp.concatenate(lax.optimization_barrier((own, *own_came, got))[:4], axis=0)
     own_across = to_core(own_set)
-    got_set = jnp.concatenate([got] + [to[delta](got) for delta in (1, 2, 3)], axis=0)
+    got_z = to[2](got)
+    got_x = to[1](jnp.concatenate([got, got_z]))
+    got_set = jnp.concatenate([got, got_x[:rows], got_z, got_x[rows:]], axis=0)
     got_across = to_core(after(got_set, shared))
 
     work = slots * atoms
@@ -373,8 +378,10 @@
     near_came = to[1](after(near_leave, far_came))
     far_came = to[2](far_leave)
     near_stay, near_leave = halve(near_stay, near_came, 0, "near_x")
-    (beyond_sum,) = call(sum_kernel, [((rows + tail, hidden),)], (far_stay, far_came), size=400 * 1024, name="far_z")
-    came = to[4](after(beyond_sum, force_came))
+    token = force_came[0, 0:8, 0:128]
+    token = to_core(token)
+    (beyond_sum,) = call(sum_kernel, [((rows + tail, hidden),)], (far_stay, far_came, token), name="far_z")
+    came = to[4](beyond_sum)
     (mine_sum,) = call(sum_kernel, [((rows, hidden),)], (near_stay, to[2](near_leave)), size=400 * 1024, name="near_z")
     shape = lambda x: jax.ShapeDtypeStruct(x.shape, F32)
     vec_mom = vector_momentum.transpose(1, 0, 2)

time: 65.5 us -> 61.4 us (0.937)
  waiting for transfers between devices: 29.9 us -> 25.4 us
  starting transfers between devices: 26.3 us -> 28 us
  Pallas kernels: 7.11 us -> 5.68 us
    ppermute x20 -> x19, waiting for transfers between devices: 29.9 us -> 25.4 us  [flip(): lax.ppermute(x, axis, [(i, i ^ delta) for i in range(size)])]
    ppermute x20 -> x19, starting transfers between devices: 26.3 us -> 28 us  [flip(): lax.ppermute(x, axis, [(i, i ^ delta) for i in range(size)])]
    pallas_call x1, Pallas kernels: 1.69 us -> 0.24 us  [halves(): pl.pallas_call(message_kernel, out_shape=[jax.ShapeDtypeStruct((atoms + 8...]
  transfers between devices with their start and end apart: 20 -> 19, of which waited for: 10 -> 11; matrix products, arithmetic and copies ran while one was open for 0% -> 0% of each run, Pallas kernels for 2% -> 3%
where the time goes in v3:
time: 61.4 us; the launch traced here: 61.2 us
  starting transfers between devices  28 us (46%)
  waiting for transfers between devices  25.4 us (41%)
  Pallas kernels  5.68 us (9%)
  local copies, waits for them, and re-layouts  1.1 us (2%)
  between operations  0.95 us (2%)
    ppermute x19, starting transfers between devices, flip(): lax.ppermute(x, axis, [(i, i ^ delta) for i in range(size)])  28 us
    ppermute x19, waiting for transfers between devices, flip(): lax.ppermute(x, axis, [(i, i ^ delta) for i in range(size)])  25.4 us
    pallas_call x10, Pallas kernels, call(): pl.pallas_call(kernel, out_shape=[jax.ShapeDtypeStruct(shape, kind) for s...  3.86 us
    pallas_call x1, Pallas kernels, halves(): pl.pallas_call(final_kernel, out_shape=[shape(first_layer), shape(second_...  1.58 us
  transfers between devices with their start and end apart: 19, of which 11 were waited for; matrix products, arithmetic and copies ran while one was open for 0% of the time, Pallas kernels for 3%

profile of v3, /device:TPU:0, one launch (start us, length us, event | category | flops | bytes accessed | tf_op | source)
XLA Modules:
  0.0 61.2 jit_solution(2824884157964273673)
XLA Ops:
  0.6 0.0 copy-start.1
  0.6 0.0 copy-start
  0.7 0.9 %bitcast_dynamic-update-slice_fusion.1 = f32[2,48,512]{2,1,0:T(8,128)S(1)} fusion(f32[1,2,16,512]{3,1,2,0:T(2,128)} %bitcast.22), kind=kLoop, calls=%fused_computation.6 | loop fusion | bytes 131072
  1.6 0.0 copy-done.1
  1.7 0.0 copy-start.7
  1.7 4.1 %collective-permute-start.4 = (f32[48,512]{1,0:T(8,128)S(1)}, f32[48,512]{1,0:T(8,128)S(1)}, u32[]{:S(2)}, u32[]{:S(2)}) collective-permute-start(f32[48,512]{1,0:T(8,128)S(1)} %get-tuple-element.102), channel_id=1, source_target_pairs={{0,8},{2,10},{4,12},{6,14},{8,0},{10,2},{12,4},{14,6},{1,9},{3,11}... | collective-permute-start | bytes 294920 | tf_op jit(solution)/shard_map/ppermute | solution.py:276
  5.8 0.0 copy-start.8
  5.8 0.0 copy-start.9
  5.8 1.6 %collective-permute-start.2 = (f32[48,512]{1,0:T(8,128)S(1)}, f32[48,512]{1,0:T(8,128)S(1)}, u32[]{:S(2)}, u32[]{:S(2)}) collective-permute-start(f32[48,512]{1,0:T(8,128)S(1)} %get-tuple-element.57), channel_id=1, source_target_pairs={{0,4},{2,6},{4,0},{6,2},{8,12},{10,14},{12,8},{14,10},{1,5},{3,7},... | collective-permute-start | bytes 294920 | tf_op jit(solution)/shard_map/ppermute | solution.py:276
  7.4 0.0 copy-done
  7.4 0.0 copy-done.7
  7.4 0.0 copy-done.8
  7.4 0.0 copy-done.9
  7.4 0.2 message.1
  7.6 0.4 collective-permute-start
  8.0 2.6 %collective-permute-done.4 = f32[48,512]{1,0:T(8,128)S(1)} collective-permute-done((f32[48,512]{1,0:T(8,128)S(1)}, f32[48,512]{1,0:T(8,128)S(1)}, u32[]{:S(2)}, u32[]{:S(2)}) %collective-permute-start.4) | collective-permute-done | bytes 98336 | tf_op jit(solution)/shard_map/ppermute | solution.py:276
  10.6 1.5 %collective-permute-start.6 = (f32[48,512]{1,0:T(8,128)S(1)}, f32[48,512]{1,0:T(8,128)S(1)}, u32[]{:S(2)}, u32[]{:S(2)}) collective-permute-start(f32[48,512]{1,0:T(8,128)S(1)} %collective-permute-done.4), channel_id=1, source_target_pairs={{0,4},{2,6},{4,0},{6,2},{8,12},{10,14},{12,8},{14,10},{1,5},{3,7},... | collective-permute-start | bytes 294920 | tf_op jit(solution)/shard_map/ppermute | solution.py:276
  12.1 0.0 collective-permute-done.2
  12.1 1.6 %collective-permute-start.3 = (f32[96,512]{1,0:T(8,128)S(1)}, f32[96,512]{1,0:T(8,128)S(1)}, u32[]{:S(2)}, u32[]{:S(2)}) collective-permute-start(f32[96,512]{1,0:T(8,128)S(1)} %pad_maximum_fusion.1), channel_id=1, source_target_pairs={{0,2},{2,0},{4,6},{6,4},{8,10},{10,8},{12,14},{14,12},{1,3},{3,1},... | collective-permute-start | bytes 589832 | tf_op jit(solution)/shard_map/ppermute | solution.py:276
  13.7 3.1 %collective-permute-done = f32[136,256]{1,0:T(8,128)S(1)} collective-permute-done((f32[136,256]{1,0:T(8,128)S(1)}, f32[136,256]{1,0:T(8,128)S(1)}, u32[]{:S(2)}, u32[]{:S(2)}) %collective-permute-start) | collective-permute-done | bytes 139296 | tf_op jit(solution)/shard_map/ppermute | solution.py:276
  16.8 1.6 %collective-permute-start.1 = (f32[128,256]{1,0:T(8,128)S(1)}, f32[128,256]{1,0:T(8,128)S(1)}, u32[]{:S(2)}, u32[]{:S(2)}) collective-permute-start(f32[128,256]{1,0:T(8,128)S(1)} %slice.41.first_far), channel_id=1, source_target_pairs={{0,16},{16,0},{1,17},{17,1},{2,18},{18,2},{3,19},{19,3},{4,20},{20... | collective-permute-start | bytes 393224 | tf_op jit(solution)/shard_map/ppermute | solution.py:276
  18.4 0.0 collective-permute-done.6
  18.4 1.6 %collective-permute-start.7 = (f32[96,512]{1,0:T(8,128)S(1)}, f32[96,512]{1,0:T(8,128)S(1)}, u32[]{:S(2)}, u32[]{:S(2)}) collective-permute-start(f32[96,512]{1,0:T(8,128)S(1)} %pad_maximum_fusion.2), channel_id=1, source_target_pairs={{0,2},{2,0},{4,6},{6,4},{8,10},{10,8},{12,14},{14,12},{1,3},{3,1},... | collective-permute-start | bytes 589832 | tf_op jit(solution)/shard_map/ppermute | solution.py:276
  20.0 0.0 collective-permute-done.3
  20.1 0.1 collective-permute-start.5
  20.2 4.1 %collective-permute-done.7 = f32[96,512]{1,0:T(8,128)S(1)} collective-permute-done((f32[96,512]{1,0:T(8,128)S(1)}, f32[96,512]{1,0:T(8,128)S(1)}, u32[]{:S(2)}, u32[]{:S(2)}) %collective-permute-start.7) | collective-permute-done | bytes 196640 | tf_op jit(solution)/shard_map/ppermute | solution.py:276
  24.3 0.0 copy-start.4
  24.3 0.0 collective-permute-done.1.second_far
  24.3 0.1 collective-permute-start.8
  24.4 0.0 collective-permute-done.5.own1
  24.4 1.7 %collective-permute-done.8.rec1 = f32[192,512]{1,0:T(8,128)S(1)} collective-permute-done((f32[192,512]{1,0:T(8,128)S(1)}, f32[192,512]{1,0:T(8,128)S(1)}, u32[]{:S(2)}, u32[]{:S(2)}) %collective-permute-start.8) | collective-permute-done | bytes 393248 | tf_op jit(solution)/shard_map/ppermute | solution.py:276
  26.1 0.0 copy-done.4
  26.1 1.3 %forward.1 = (f32[256,512]{1,0:T(8,128)S(1)}, f32[256,512]{1,0:T(8,128)S(1)}, f32[256,256]{1,0:T(8,128)S(1)}, f32[256,128]{1,0:T(8,128)S(1)}, f32[8,128]{1,0:T(8...) custom-call(f32[2,2,128,256]{3,2,1,0:T(8,128)S(1)} %copy-done, ...), custom_call_target="tpu_custom_call" | custom-call | flops 1 | bytes 1 | tf_op jit(solution)/shard_map/forward/pallas_call | solution.py:32
  27.4 2.8 %collective-permute-start.9 = (f32[8,128]{1,0:T(8,128)S(1)}, f32[8,128]{1,0:T(8,128)S(1)}, u32[]{:S(2)}, u32[]{:S(2)}) collective-permute-start(f32[8,128]{1,0:T(8,128)S(1)} %get-tuple-element.62.mine), channel_id=1, source_target_pairs={{0,8},{2,10},{4,12},{6,14},{8,0},{10,2},{12,4},{14,6},{1,9},{3,11}... | collective-permute-start | bytes 12296 | tf_op jit(solution)/shard_map/ppermute | solution.py:276
  30.2 0.1 bitcast_maximum_fusion.refs
  30.3 1.2 %backward.1 = (f32[256,512]{1,0:T(8,128)S(1)}, f32[256,512]{1,0:T(8,128)S(1)}, f32[256,256]{1,0:T(8,128)S(1)}) custom-call(f32[256,512]{1,0:T(8,128)S(1)} %get-tuple-element.64.h1_ref, f32[256,512]{1,0:T(8,128)S(1)} %get-tuple-element.65.h2_ref, f32[3,2,512]{2,1,0:T(2,128)S(1)} %bitcast.24, bf16[256,512]{1,0:T(8,128)(2,1)S(1)} %get-tuple-element.66.w1h, ...), custom_call_target="tpu_custom_call" | custom-call | flops 1 | bytes 1 | tf_op jit(solution)/shard_map/backward/pallas_call | solution.py:32
  31.4 0.5 collective-permute-done.9.theirs
  32.0 0.2 force.1
  32.2 1.0 %gradient.1 = (f32[200,512]{1,0:T(8,128)S(1)}, f32[200,512]{1,0:T(8,128)S(1)}, f32[192,512]{1,0:T(8,128)S(1)}, f32[192,512]{1,0:T(8,128)S(1)}) custom-call(f32[256,128]{1,0:T(8,128)S(1)} %get-tuple-element.71.adj_ref, f32[8,128]{1,0:T(8,128)S(1)} %get-tuple-element.72.pot_ref, f32[256,512]{1,0:T(8,128)S(1)} %get-tuple-element.64.h1_ref, ...), custom_call_target="tpu_custom_call" | custom-call | flops 1 | bytes 1 | tf_op jit(solution)/shard_map/gradient/pallas_call | solution.py:32
  33.2 0.1 collective-permute-start.11
  33.3 0.5 collective-permute-start.10
  33.8 2.7 %collective-permute-start.16 = (f32[2,128,256]{2,1,0:T(8,128)S(1)}, f32[2,128,256]{2,1,0:T(8,128)S(1)}, u32[]{:S(2)}, u32[]{:S(2)}) collective-permute-start(f32[2,128,256]{2,1,0:T(8,128)S(1)} %get-tuple-element.89), channel_id=1, source_target_pairs={{0,8},{2,10},{4,12},{6,14},{8,0},{10,2},{12,4},{14,6},{1,9},{3,11}... | collective-permute-start | bytes 786440 | tf_op jit(solution)/shard_map/ppermute | solution.py:276
  36.5 0.0 collective-permute-done.11.came
  36.6 1.6 %collective-permute-start.12 = (f32[104,512]{1,0:T(8,128)S(1)}, f32[104,512]{1,0:T(8,128)S(1)}, u32[]{:S(2)}, u32[]{:S(2)}) collective-permute-start(f32[104,512]{1,0:T(8,128)S(1)} %get-tuple-element.82), channel_id=1, source_target_pairs={{0,2},{2,0},{4,6},{6,4},{8,10},{10,8},{12,14},{14,12},{1,3},{3,1},... | collective-permute-start | bytes 638984 | tf_op jit(solution)/shard_map/ppermute | solution.py:276
  38.1 0.0 collective-permute-done.10.came
  38.2 5.4 %collective-permute-done.12.came = f32[104,512]{1,0:T(8,128)S(1)} collective-permute-done((f32[104,512]{1,0:T(8,128)S(1)}, f32[104,512]{1,0:T(8,128)S(1)}, u32[]{:S(2)}, u32[]{:S(2)}) %collective-permute-start.12) | collective-permute-done | bytes 213024 | tf_op jit(solution)/shard_map/ppermute | solution.py:276
  43.6 2.2 %collective-permute-start.15 = (f32[56,512]{1,0:T(8,128)S(1)}, f32[56,512]{1,0:T(8,128)S(1)}, u32[]{:S(2)}, u32[]{:S(2)}) collective-permute-start(f32[56,512]{1,0:T(8,128)S(1)} %get-tuple-element.88), channel_id=1, source_target_pairs={{0,4},{2,6},{4,0},{6,2},{8,12},{10,14},{12,8},{14,10},{1,5},{3,7},... | collective-permute-start | bytes 344072 | tf_op jit(solution)/shard_map/ppermute | solution.py:276
  45.8 1.5 %collective-permute-start.13 = (f32[96,512]{1,0:T(8,128)S(1)}, f32[96,512]{1,0:T(8,128)S(1)}, u32[]{:S(2)}, u32[]{:S(2)}) collective-permute-start(f32[96,512]{1,0:T(8,128)S(1)} %get-tuple-element.83), channel_id=1, source_target_pairs={{0,2},{2,0},{4,6},{6,4},{8,10},{10,8},{12,14},{14,12},{1,3},{3,1},... | collective-permute-start | bytes 589832 | tf_op jit(solution)/shard_map/ppermute | solution.py:276
  47.3 1.5 %collective-permute-done.16.force_came = f32[2,128,256]{2,1,0:T(8,128)S(1)} collective-permute-done((f32[2,128,256]{2,1,0:T(8,128)S(1)}, f32[2,128,256]{2,1,0:T(8,128)S(1)}, u32[]{:S(2)}, u32[]{:S(2)}) %collective-permute-start.16) | collective-permute-done | bytes 262176 | tf_op jit(solution)/shard_map/ppermute | solution.py:276
  48.8 0.0 collective-permute-start.17
  48.8 1.2 %collective-permute-done.17.rest_0_ = f32[8,128]{1,0:T(8,128)S(1)} collective-permute-done((f32[8,128]{1,0:T(8,128)S(1)}, f32[8,128]{1,0:T(8,128)S(1)}, u32[]{:S(2)}, u32[]{:S(2)}) %collective-permute-start.17) | collective-permute-done | bytes 4128 | tf_op jit(solution)/shard_map/ppermute | solution.py:276
  50.0 1.2 %collective-permute-done.15.b = f32[56,512]{1,0:T(8,128)S(1)} collective-permute-done((f32[56,512]{1,0:T(8,128)S(1)}, f32[56,512]{1,0:T(8,128)S(1)}, u32[]{:S(2)}, u32[]{:S(2)}) %collective-permute-start.15) | collective-permute-done | bytes 114720 | tf_op jit(solution)/shard_map/ppermute | solution.py:276
  51.2 1.7 %collective-permute-start.18 = (f32[56,512]{1,0:T(8,128)S(1)}, f32[56,512]{1,0:T(8,128)S(1)}, u32[]{:S(2)}, u32[]{:S(2)}) collective-permute-start(f32[56,512]{1,0:T(8,128)S(1)} %far_z.1.beyond), channel_id=1, source_target_pairs={{0,8},{2,10},{4,12},{6,14},{8,0},{10,2},{12,4},{14,6},{1,9},{3,11}... | collective-permute-start | bytes 344072 | tf_op jit(solution)/shard_map/ppermute | solution.py:276
  52.8 0.0 collective-permute-done.13.came
  52.9 2.5 %collective-permute-start.14 = (f32[48,512]{1,0:T(8,128)S(1)}, f32[48,512]{1,0:T(8,128)S(1)}, u32[]{:S(2)}, u32[]{:S(2)}) collective-permute-start(f32[48,512]{1,0:T(8,128)S(1)} %get-tuple-element.85), channel_id=1, source_target_pairs={{0,4},{2,6},{4,0},{6,2},{8,12},{10,14},{12,8},{14,10},{1,5},{3,7},... | collective-permute-start | bytes 294920 | tf_op jit(solution)/shard_map/ppermute | solution.py:276
  55.4 3.2 %collective-permute-done.14.b = f32[48,512]{1,0:T(8,128)S(1)} collective-permute-done((f32[48,512]{1,0:T(8,128)S(1)}, f32[48,512]{1,0:T(8,128)S(1)}, u32[]{:S(2)}, u32[]{:S(2)}) %collective-permute-start.14) | collective-permute-done | bytes 98336 | tf_op jit(solution)/shard_map/ppermute | solution.py:276
  58.6 0.0 copy-start.2
  58.6 0.0 copy-start.3
  58.6 1.0 %collective-permute-done.18.came = f32[56,512]{1,0:T(8,128)S(1)} collective-permute-done((f32[56,512]{1,0:T(8,128)S(1)}, f32[56,512]{1,0:T(8,128)S(1)}, u32[]{:S(2)}, u32[]{:S(2)}) %collective-permute-start.18) | collective-permute-done | bytes 114720 | tf_op jit(solution)/shard_map/ppermute | solution.py:276
  59.6 0.0 copy-done.2
  59.6 0.0 copy-done.3
  59.7 0.0 copy-done.5
  59.7 0.0 copy-done.6
  59.7 1.6 %final.1 = (f32[2,8192]{1,0:T(2,128)}, f32[2,16384]{1,0:T(2,128)}, f32[3,2,512]{2,1,0:T(2,128)}, f32[2,8192]{1,0:T(2,128)}, f32[2,16384]{1,0:T(2,128)}, /*index=...) custom-call(f32[48,512]{1,0:T(8,128)S(1)} %near_z.1.mine, f32[56,512]{1,0:T(8,128)S(1)} %far_z.1.beyond, ...), custom_call_target="tpu_custom_call" | custom-call | tf_op jit(solution)/shard_map/final/pallas_call | solution.py:390
  (25 shorter events, 0.4 us)
Async XLA Ops:
  0.6 1.0 %copy-start.1 = (f32[2,16384]{1,0:T(2,128)S(1)}, f32[2,16384]{1,0:T(2,128)}, u32[]{:S(2)}) copy-start(f32[2,16384]{1,0:T(2,128)} %second.1) | copy-start | bytes 393220
  0.6 6.7 %copy-start = (f32[2,2,128,256]{3,2,1,0:T(8,128)S(1)}, f32[2,2,128,256]{3,2,1,0:T(8,128)}, u32[]{:S(2)}) copy-start(f32[2,2,128,256]{3,2,1,0:T(8,128)} %desc_ref.1) | copy-start | bytes 1572868
  1.7 5.7 %copy-start.7 = (s32[2,2,128]{2,1,0:T(2,128)S(1)}, s32[2,2,128]{2,1,0:T(2,128)}, u32[]{:S(2)}) copy-start(s32[2,2,128]{2,1,0:T(2,128)} %ids_hbm.1) | copy-start | bytes 6148
  1.7 8.9 %collective-permute-start.4 = (f32[48,512]{1,0:T(8,128)S(1)}, f32[48,512]{1,0:T(8,128)S(1)}, u32[]{:S(2)}, u32[]{:S(2)}) collective-permute-start(f32[48,512]{1,0:T(8,128)S(1)} %get-tuple-element.102), channel_id=1, source_target_pairs={{0,8},{2,10},{4,12},{6,14},{8,0},{10,2},{12,4},{14,6},{1,9},{3,11}... | collective-permute-start | bytes 294920 | tf_op jit(solution)/shard_map/ppermute | solution.py:276
  5.8 1.6 %copy-start.8 = (s32[2,2]{1,0:T(2,128)S(1)}, s32[2,2]{1,0:T(2,128)}, u32[]{:S(2)}) copy-start(s32[2,2]{1,0:T(2,128)} %counts_hbm.1) | copy-start | bytes 52
  5.8 1.6 %copy-start.9 = (f32[32]{0:T(128)S(1)}, f32[32]{0:T(128)}, u32[]{:S(2)}) copy-start(f32[32]{0:T(128)} %param.13) | copy-start | bytes 388
  5.8 6.3 %collective-permute-start.2 = (f32[48,512]{1,0:T(8,128)S(1)}, f32[48,512]{1,0:T(8,128)S(1)}, u32[]{:S(2)}, u32[]{:S(2)}) collective-permute-start(f32[48,512]{1,0:T(8,128)S(1)} %get-tuple-element.57), channel_id=1, source_target_pairs={{0,4},{2,6},{4,0},{6,2},{8,12},{10,14},{12,8},{14,10},{1,5},{3,7},... | collective-permute-start | bytes 294920 | tf_op jit(solution)/shard_map/ppermute | solution.py:276
  7.6 9.1 %collective-permute-start = (f32[136,256]{1,0:T(8,128)S(1)}, f32[136,256]{1,0:T(8,128)S(1)}, u32[]{:S(2)}, u32[]{:S(2)}) collective-permute-start(f32[136,256]{1,0:T(8,128)S(1)} %get-tuple-element.55), channel_id=1, source_target_pairs={{0,8},{2,10},{4,12},{6,14},{8,0},{10,2},{12,4},{14,6},{1,9},{3,11}... | collective-permute-start | bytes 417800 | tf_op jit(solution)/shard_map/ppermute | solution.py:276
  10.6 7.8 %collective-permute-start.6 = (f32[48,512]{1,0:T(8,128)S(1)}, f32[48,512]{1,0:T(8,128)S(1)}, u32[]{:S(2)}, u32[]{:S(2)}) collective-permute-start(f32[48,512]{1,0:T(8,128)S(1)} %collective-permute-done.4), channel_id=1, source_target_pairs={{0,4},{2,6},{4,0},{6,2},{8,12},{10,14},{12,8},{14,10},{1,5},{3,7},... | collective-permute-start | bytes 294920 | tf_op jit(solution)/shard_map/ppermute | solution.py:276
  12.1 7.9 %collective-permute-start.3 = (f32[96,512]{1,0:T(8,128)S(1)}, f32[96,512]{1,0:T(8,128)S(1)}, u32[]{:S(2)}, u32[]{:S(2)}) collective-permute-start(f32[96,512]{1,0:T(8,128)S(1)} %pad_maximum_fusion.1), channel_id=1, source_target_pairs={{0,2},{2,0},{4,6},{6,4},{8,10},{10,8},{12,14},{14,12},{1,3},{3,1},... | collective-permute-start | bytes 589832 | tf_op jit(solution)/shard_map/ppermute | solution.py:276
  16.8 7.5 %collective-permute-start.1 = (f32[128,256]{1,0:T(8,128)S(1)}, f32[128,256]{1,0:T(8,128)S(1)}, u32[]{:S(2)}, u32[]{:S(2)}) collective-permute-start(f32[128,256]{1,0:T(8,128)S(1)} %slice.41.first_far), channel_id=1, source_target_pairs={{0,16},{16,0},{1,17},{17,1},{2,18},{18,2},{3,19},{19,3},{4,20},{20... | collective-permute-start | bytes 393224 | tf_op jit(solution)/shard_map/ppermute | solution.py:276
  18.4 5.8 %collective-permute-start.7 = (f32[96,512]{1,0:T(8,128)S(1)}, f32[96,512]{1,0:T(8,128)S(1)}, u32[]{:S(2)}, u32[]{:S(2)}) collective-permute-start(f32[96,512]{1,0:T(8,128)S(1)} %pad_maximum_fusion.2), channel_id=1, source_target_pairs={{0,2},{2,0},{4,6},{6,4},{8,10},{10,8},{12,14},{14,12},{1,3},{3,1},... | collective-permute-start | bytes 589832 | tf_op jit(solution)/shard_map/ppermute | solution.py:276
  20.1 4.3 %collective-permute-start.5 = (f32[192,512]{1,0:T(8,128)S(1)}, f32[192,512]{1,0:T(8,128)S(1)}, u32[]{:S(2)}, u32[]{:S(2)}) collective-permute-start(f32[192,512]{1,0:T(8,128)S(1)} %constant_dynamic-update-slice_fusion.own0), channel_id=1, source_target_pairs={{0,1},{1,0},{2,3},{3,2},{4,5},{5,4},{6,7},{7,6},{8,9},{9,8},{10,11... | collective-permute-start | bytes 1179656 | tf_op jit(solution)/shard_map/ppermute | solution.py:276
  24.3 1.8 %copy-start.4 = (f32[2,3,512]{2,0,1:T(2,128)S(1)}, f32[2,3,512]{2,0,1:T(2,128)}, u32[]{:S(2)}) copy-start(f32[2,3,512]{2,0,1:T(2,128)} %param.16) | copy-start | bytes 36868
  24.3 1.8 %collective-permute-start.8 = (f32[192,512]{1,0:T(8,128)S(1)}, f32[192,512]{1,0:T(8,128)S(1)}, u32[]{:S(2)}, u32[]{:S(2)}) collective-permute-start(f32[192,512]{1,0:T(8,128)S(1)} %pad_maximum_fusion.rec0), channel_id=1, source_target_pairs={{0,1},{1,0},{2,3},{3,2},{4,5},{5,4},{6,7},{7,6},{8,9},{9,8},{10,11... | collective-permute-start | bytes 1179656 | tf_op jit(solution)/shard_map/ppermute | solution.py:276
  27.4 4.6 %collective-permute-start.9 = (f32[8,128]{1,0:T(8,128)S(1)}, f32[8,128]{1,0:T(8,128)S(1)}, u32[]{:S(2)}, u32[]{:S(2)}) collective-permute-start(f32[8,128]{1,0:T(8,128)S(1)} %get-tuple-element.62.mine), channel_id=1, source_target_pairs={{0,8},{2,10},{4,12},{6,14},{8,0},{10,2},{12,4},{14,6},{1,9},{3,11}... | collective-permute-start | bytes 12296 | tf_op jit(solution)/shard_map/ppermute | solution.py:276
  33.2 3.3 %collective-permute-start.11 = (f32[200,512]{1,0:T(8,128)S(1)}, f32[200,512]{1,0:T(8,128)S(1)}, u32[]{:S(2)}, u32[]{:S(2)}) collective-permute-start(f32[200,512]{1,0:T(8,128)S(1)} %get-tuple-element.81), channel_id=1, source_target_pairs={{0,1},{1,0},{2,3},{3,2},{4,5},{5,4},{6,7},{7,6},{8,9},{9,8},{10,11... | collective-permute-start | bytes 1228808 | tf_op jit(solution)/shard_map/ppermute | solution.py:276
  33.3 4.8 %collective-permute-start.10 = (f32[192,512]{1,0:T(8,128)S(1)}, f32[192,512]{1,0:T(8,128)S(1)}, u32[]{:S(2)}, u32[]{:S(2)}) collective-permute-start(f32[192,512]{1,0:T(8,128)S(1)} %get-tuple-element.77), channel_id=1, source_target_pairs={{0,1},{1,0},{2,3},{3,2},{4,5},{5,4},{6,7},{7,6},{8,9},{9,8},{10,11... | collective-permute-start | bytes 1179656 | tf_op jit(solution)/shard_map/ppermute | solution.py:276
  33.8 15.0 %collective-permute-start.16 = (f32[2,128,256]{2,1,0:T(8,128)S(1)}, f32[2,128,256]{2,1,0:T(8,128)S(1)}, u32[]{:S(2)}, u32[]{:S(2)}) collective-permute-start(f32[2,128,256]{2,1,0:T(8,128)S(1)} %get-tuple-element.89), channel_id=1, source_target_pairs={{0,8},{2,10},{4,12},{6,14},{8,0},{10,2},{12,4},{14,6},{1,9},{3,11}... | collective-permute-start | bytes 786440 | tf_op jit(solution)/shard_map/ppermute | solution.py:276
  36.6 7.0 %collective-permute-start.12 = (f32[104,512]{1,0:T(8,128)S(1)}, f32[104,512]{1,0:T(8,128)S(1)}, u32[]{:S(2)}, u32[]{:S(2)}) collective-permute-start(f32[104,512]{1,0:T(8,128)S(1)} %get-tuple-element.82), channel_id=1, source_target_pairs={{0,2},{2,0},{4,6},{6,4},{8,10},{10,8},{12,14},{14,12},{1,3},{3,1},... | collective-permute-start | bytes 638984 | tf_op jit(solution)/shard_map/ppermute | solution.py:276
  43.6 7.5 %collective-permute-start.15 = (f32[56,512]{1,0:T(8,128)S(1)}, f32[56,512]{1,0:T(8,128)S(1)}, u32[]{:S(2)}, u32[]{:S(2)}) collective-permute-start(f32[56,512]{1,0:T(8,128)S(1)} %get-tuple-element.88), channel_id=1, source_target_pairs={{0,4},{2,6},{4,0},{6,2},{8,12},{10,14},{12,8},{14,10},{1,5},{3,7},... | collective-permute-start | bytes 344072 | tf_op jit(solution)/shard_map/ppermute | solution.py:276
  45.8 7.1 %collective-permute-start.13 = (f32[96,512]{1,0:T(8,128)S(1)}, f32[96,512]{1,0:T(8,128)S(1)}, u32[]{:S(2)}, u32[]{:S(2)}) collective-permute-start(f32[96,512]{1,0:T(8,128)S(1)} %get-tuple-element.83), channel_id=1, source_target_pairs={{0,2},{2,0},{4,6},{6,4},{8,10},{10,8},{12,14},{14,12},{1,3},{3,1},... | collective-permute-start | bytes 589832 | tf_op jit(solution)/shard_map/ppermute | solution.py:276
  48.8 1.2 %collective-permute-start.17 = (f32[8,128]{1,0:T(8,128)S(1)}, f32[8,128]{1,0:T(8,128)S(1)}, u32[]{:S(2)}, u32[]{:S(2)}) collective-permute-start(f32[8,128]{1,0:T(8,128)S(1)} %slice_bitcast_fusion), channel_id=1, source_target_pairs={{0,1},{1,0},{2,3},{3,2},{4,5},{5,4},{6,7},{7,6},{8,9},{9,8},{10,11... | collective-permute-start | bytes 12296 | tf_op jit(solution)/shard_map/ppermute | solution.py:276
  51.2 8.5 %collective-permute-start.18 = (f32[56,512]{1,0:T(8,128)S(1)}, f32[56,512]{1,0:T(8,128)S(1)}, u32[]{:S(2)}, u32[]{:S(2)}) collective-permute-start(f32[56,512]{1,0:T(8,128)S(1)} %far_z.1.beyond), channel_id=1, source_target_pairs={{0,8},{2,10},{4,12},{6,14},{8,0},{10,2},{12,4},{14,6},{1,9},{3,11}... | collective-permute-start | bytes 344072 | tf_op jit(solution)/shard_map/ppermute | solution.py:276
  52.9 5.7 %collective-permute-start.14 = (f32[48,512]{1,0:T(8,128)S(1)}, f32[48,512]{1,0:T(8,128)S(1)}, u32[]{:S(2)}, u32[]{:S(2)}) collective-permute-start(f32[48,512]{1,0:T(8,128)S(1)} %get-tuple-element.85), channel_id=1, source_target_pairs={{0,4},{2,6},{4,0},{6,2},{8,12},{10,14},{12,8},{14,10},{1,5},{3,7},... | collective-permute-start | bytes 294920 | tf_op jit(solution)/shard_map/ppermute | solution.py:276
  58.6 1.0 %copy-start.2 = (f32[2,8192]{1,0:T(2,128)S(1)}, f32[2,8192]{1,0:T(2,128)}, u32[]{:S(2)}) copy-start(f32[2,8192]{1,0:T(2,128)} %first.1) | copy-start | bytes 196612
  58.6 1.0 %copy-start.3 = (f32[2,16384]{1,0:T(2,128)S(1)}, f32[2,16384]{1,0:T(2,128)}, u32[]{:S(2)}) copy-start(f32[2,16384]{1,0:T(2,128)} %second_mom.1) | copy-start | bytes 393220
  58.6 1.0 %copy-start.5 = (f32[2,8192]{1,0:T(2,128)S(1)}, f32[2,8192]{1,0:T(2,128)}, u32[]{:S(2)}) copy-start(f32[2,8192]{1,0:T(2,128)} %first_mom.1) | copy-start | bytes 196612
  58.6 1.0 %copy-start.6 = (f32[2,3,512]{2,0,1:T(2,128)S(1)}, f32[2,3,512]{2,0,1:T(2,128)}, u32[]{:S(2)}) copy-start(f32[2,3,512]{2,0,1:T(2,128)} %param.19) | copy-start | bytes 36868

commit v4 on v3

--- a/solution.py
+++ b/solution.py
@@ -228,25 +228,40 @@
         out[base + 2 : base + 3, 0 : refs.shape[1]] = refs[...]
 
 
-def final_kernel(
-    mine, beyond, came, first, second, vec, first_mom, second_mom, vec_mom, force_near, force_came,
-    new_first, new_second, new_vec, new_first_mom, new_second_mom, new_vec_mom, potential, forces,
-    flat_first, flat_second, sems,
-):
+def near_kernel(a, b, force_near, force_came, mine_first, mine_second, forces, total, sems):
     spot, core, half, chain = place()
     near_copy = pltpu.make_async_copy(force_near, forces.at[half], sems.at[0])
     far_copy = pltpu.make_async_copy(force_came, forces.at[1 - half], sems.at[1])
     near_copy.start()
     far_copy.start()
-    hidden = mine.shape[1]
+    total[...] = a[...] + b[...]
+    hidden = total.shape[1]
+    rows1 = mine_first.shape[1] // hidden
+    rows2 = mine_second.shape[1] // hidden
+    for row in range(rows1):
+        mine_first[:, row * hidden : (row + 1) * hidden] = total[row : row + 1, :]
+    for row in range(rows2):
+        mine_second[:, row * hidden : (row + 1) * hidden] = total[rows1 + row : rows1 + row + 1, :]
+    near_copy.wait()
+    far_copy.wait()
+
+
+def final_kernel(
+    mine_first, mine_second, beyond, came, first, second, vec, first_mom, second_mom, vec_mom,
+    new_first, new_second, new_vec, new_first_mom, new_second_mom, new_vec_mom, potential,
+    flat_first, flat_second,
+):
+    spot, core, half, chain = place()
+    hidden = came.shape[1]
     rows1 = flat_first.shape[1] // hidden
     rows2 = flat_second.shape[1] // hidden
     rows = rows1 + rows2
-    for source, element in ((mine, half), (came, 1 - half)):
-        for row in range(rows1):
-            flat_first[pl.ds(element, 1), row * hidden : (row + 1) * hidden] = source[row : row + 1, :]
-        for row in range(rows2):
-            flat_second[pl.ds(element, 1), row * hidden : (row + 1) * hidden] = source[rows1 + row : rows1 + row + 1, :]
+    flat_first[pl.ds(half, 1), :] = mine_first[...]
+    flat_second[pl.ds(half, 1), :] = mine_second[...]
+    for row in range(rows1):
+        flat_first[pl.ds(1 - half, 1), row * hidden : (row + 1) * hidden] = came[row : row + 1, :]
+    for row in range(rows2):
+        flat_second[pl.ds(1 - half, 1), row * hidden : (row + 1) * hidden] = came[rows1 + row : rows1 + row + 1, :]
     for grad, value, momentum, new_value, new_momentum in (
         (flat_first, first, first_mom, new_first, new_first_mom),
         (flat_second, second, second_mom, new_second, new_second_mom),
@@ -264,8 +279,6 @@
             new_vec_mom[kind, element : element + 1, :] = moved
             new_vec[kind, element : element + 1, :] = vec[kind, element : element + 1, :] + STEP_SIZE * moved
     potential[...] = beyond[rows + 3 : rows + 4, 0:128] * (1.0 / 512.0)
-    near_copy.wait()
-    far_copy.wait()
 
 
 def after(value, *others):
@@ -382,27 +395,38 @@
     token = to_core(token)
     (beyond_sum,) = call(sum_kernel, [((rows + tail, hidden),)], (far_stay, far_came, token), name="far_z")
     came = to[4](beyond_sum)
-    (mine_sum,) = call(sum_kernel, [((rows, hidden),)], (near_stay, to[2](near_leave)), size=400 * 1024, name="near_z")
+    last_came = to[2](near_leave)
     shape = lambda x: jax.ShapeDtypeStruct(x.shape, F32)
     vec_mom = vector_momentum.transpose(1, 0, 2)
+    mine_first, mine_second, force_partials = pl.pallas_call(
+        near_kernel,
+        out_shape=[
+            jax.ShapeDtypeStruct((1, first_layer.shape[1]), F32), jax.ShapeDtypeStruct((1, second_layer.shape[1]), F32),
+            shape(descriptors),
+        ],
+        in_specs=[vmem] * 4,
+        out_specs=[vmem] * 2 + [any_space],
+        scratch_shapes=[pltpu.VMEM((rows, hidden), F32), pltpu.SemaphoreType.DMA((2,))],
+        compiler_params=pltpu.CompilerParams(vmem_limit_bytes=8 * 1024 * 1024),
+        cost_estimate=pl.CostEstimate(flops=1, bytes_accessed=1, transcendentals=0),
+        name="near_z",
+    )(near_stay, last_came, force_near, force_came)
     (
-        new_first, new_second, new_vec, new_first_mom, new_second_mom, new_vec_mom, potential, force_partials,
+        new_first, new_second, new_vec, new_first_mom, new_second_mom, new_vec_mom, potential,
     ) = pl.pallas_call(
         final_kernel,
         out_shape=[
             shape(first_layer), shape(second_layer), shape(vec), shape(first_layer), shape(second_layer), shape(vec),
-            jax.ShapeDtypeStruct((1, 128), F32), shape(descriptors),
+            jax.ShapeDtypeStruct((1, 128), F32),
         ],
-        in_specs=[vmem] * 11,
-        out_specs=[vmem] * 7 + [any_space],
-        scratch_shapes=[
-            pltpu.VMEM(first_layer.shape, F32), pltpu.VMEM(second_layer.shape, F32), pltpu.SemaphoreType.DMA((2,)),
-        ],
+        in_specs=[vmem] * 10,
+        out_specs=[vmem] * 7,
+        scratch_shapes=[pltpu.VMEM(first_layer.shape, F32), pltpu.VMEM(second_layer.shape, F32)],
         compiler_params=pltpu.CompilerParams(vmem_limit_bytes=8 * 1024 * 1024),
+        cost_estimate=pl.CostEstimate(flops=1, bytes_accessed=1, transcendentals=0),
         name="final",
     )(
-        mine_sum, beyond_sum, came, first_layer, second_layer, vec, first_momentum, second_momentum, vec_mom,
-        force_near, after(force_came, came, mine_sum),
+        mine_first, mine_second, beyond_sum, came, first_layer, second_layer, vec, first_momentum, second_momentum, vec_mom,
     )
     return (
         new_first, new_second, new_vec.transpose(1, 0, 2), new_first_mom, new_second_mom,

time: 61.4 us -> 60.7 us (0.989)
  waiting for transfers between devices: 25.4 us -> 24.6 us
    pallas_call x0 -> x1, Pallas kernels: none -> 0.83 us  [halves(): pl.pallas_call(near_kernel, out_shape=[jax.ShapeDtypeStruct((1, first_lay...]
    ppermute x19, waiting for transfers between devices: 25.4 us -> 24.6 us  [flip(): lax.ppermute(x, axis, [(i, i ^ delta) for i in range(size)])]
    pallas_call x1, Pallas kernels: 1.58 us -> 0.82 us  [halves(): pl.pallas_call(final_kernel, out_shape=[shape(first_layer), shape(second_...]
    pallas_call x10 -> x9, Pallas kernels: 3.86 us -> 3.85 us  [call(): pl.pallas_call(kernel, out_shape=[jax.ShapeDtypeStruct(shape, kind) for s...]
  transfers between devices with their start and end apart: 19 -> 19, of which waited for: 11 -> 11; matrix products, arithmetic and copies ran while one was open for 0% -> 0% of each run, Pallas kernels for 3% -> 4%
where the time goes in v4:
time: 60.7 us; the launch traced here: 60.6 us
  starting transfers between devices  28 us (46%)
  waiting for transfers between devices  24.6 us (41%)
  Pallas kernels  5.73 us (9%)
  local copies, waits for them, and re-layouts  1.17 us (2%)
  between operations  0.94 us (2%)
    ppermute x19, starting transfers between devices, flip(): lax.ppermute(x, axis, [(i, i ^ delta) for i in range(size)])  28 us
    ppermute x19, waiting for transfers between devices, flip(): lax.ppermute(x, axis, [(i, i ^ delta) for i in range(size)])  24.6 us
    pallas_call x9, Pallas kernels, call(): pl.pallas_call(kernel, out_shape=[jax.ShapeDtypeStruct(shape, kind) for s...  3.85 us
  transfers between devices with their start and end apart: 19, of which 11 were waited for; matrix products, arithmetic and copies ran while one was open for 0% of the time, Pallas kernels for 4%

profile of v4, /device:TPU:0, one launch (start us, length us, event | category | flops | bytes accessed | tf_op | source)
XLA Modules:
  0.0 60.6 jit_solution(4606463850575845444)
XLA Ops:
  0.6 0.0 copy-start.1
  0.6 0.0 copy-start
  0.7 0.9 %bitcast_dynamic-update-slice_fusion.1 = f32[2,48,512]{2,1,0:T(8,128)S(1)} fusion(f32[1,2,16,512]{3,1,2,0:T(2,128)} %bitcast.22), kind=kLoop, calls=%fused_computation.6 | loop fusion | bytes 131072
  1.6 0.0 copy-done.1
  1.7 0.0 copy-start.7
  1.7 4.1 %collective-permute-start.4 = (f32[48,512]{1,0:T(8,128)S(1)}, f32[48,512]{1,0:T(8,128)S(1)}, u32[]{:S(2)}, u32[]{:S(2)}) collective-permute-start(f32[48,512]{1,0:T(8,128)S(1)} %get-tuple-element.104), channel_id=1, source_target_pairs={{0,8},{2,10},{4,12},{6,14},{8,0},{10,2},{12,4},{14,6},{1,9},{3,11}... | collective-permute-start | bytes 294920 | tf_op jit(solution)/shard_map/ppermute | solution.py:289
  5.8 0.0 copy-start.8
  5.8 1.6 %collective-permute-start.2 = (f32[48,512]{1,0:T(8,128)S(1)}, f32[48,512]{1,0:T(8,128)S(1)}, u32[]{:S(2)}, u32[]{:S(2)}) collective-permute-start(f32[48,512]{1,0:T(8,128)S(1)} %get-tuple-element.58), channel_id=1, source_target_pairs={{0,4},{2,6},{4,0},{6,2},{8,12},{10,14},{12,8},{14,10},{1,5},{3,7},... | collective-permute-start | bytes 294920 | tf_op jit(solution)/shard_map/ppermute | solution.py:289
  7.4 0.0 copy-done
  7.4 0.0 copy-done.7
  7.4 0.0 copy-done.8
  7.4 0.0 copy-done.9
  7.4 0.2 message.1
  7.6 0.4 collective-permute-start
  8.0 2.6 %collective-permute-done.4 = f32[48,512]{1,0:T(8,128)S(1)} collective-permute-done((f32[48,512]{1,0:T(8,128)S(1)}, f32[48,512]{1,0:T(8,128)S(1)}, u32[]{:S(2)}, u32[]{:S(2)}) %collective-permute-start.4) | collective-permute-done | bytes 98336 | tf_op jit(solution)/shard_map/ppermute | solution.py:289
  10.6 1.5 %collective-permute-start.6 = (f32[48,512]{1,0:T(8,128)S(1)}, f32[48,512]{1,0:T(8,128)S(1)}, u32[]{:S(2)}, u32[]{:S(2)}) collective-permute-start(f32[48,512]{1,0:T(8,128)S(1)} %collective-permute-done.4), channel_id=1, source_target_pairs={{0,4},{2,6},{4,0},{6,2},{8,12},{10,14},{12,8},{14,10},{1,5},{3,7},... | collective-permute-start | bytes 294920 | tf_op jit(solution)/shard_map/ppermute | solution.py:289
  12.1 0.0 collective-permute-done.2
  12.1 1.6 %collective-permute-start.3 = (f32[96,512]{1,0:T(8,128)S(1)}, f32[96,512]{1,0:T(8,128)S(1)}, u32[]{:S(2)}, u32[]{:S(2)}) collective-permute-start(f32[96,512]{1,0:T(8,128)S(1)} %pad_maximum_fusion.1), channel_id=1, source_target_pairs={{0,2},{2,0},{4,6},{6,4},{8,10},{10,8},{12,14},{14,12},{1,3},{3,1},... | collective-permute-start | bytes 589832 | tf_op jit(solution)/shard_map/ppermute | solution.py:289
  13.7 3.1 %collective-permute-done = f32[136,256]{1,0:T(8,128)S(1)} collective-permute-done((f32[136,256]{1,0:T(8,128)S(1)}, f32[136,256]{1,0:T(8,128)S(1)}, u32[]{:S(2)}, u32[]{:S(2)}) %collective-permute-start) | collective-permute-done | bytes 139296 | tf_op jit(solution)/shard_map/ppermute | solution.py:289
  16.8 1.6 %collective-permute-start.1 = (f32[128,256]{1,0:T(8,128)S(1)}, f32[128,256]{1,0:T(8,128)S(1)}, u32[]{:S(2)}, u32[]{:S(2)}) collective-permute-start(f32[128,256]{1,0:T(8,128)S(1)} %slice.41.first_far), channel_id=1, source_target_pairs={{0,16},{16,0},{1,17},{17,1},{2,18},{18,2},{3,19},{19,3},{4,20},{20... | collective-permute-start | bytes 393224 | tf_op jit(solution)/shard_map/ppermute | solution.py:289
  18.4 0.0 collective-permute-done.6
  18.4 1.6 %collective-permute-start.7 = (f32[96,512]{1,0:T(8,128)S(1)}, f32[96,512]{1,0:T(8,128)S(1)}, u32[]{:S(2)}, u32[]{:S(2)}) collective-permute-start(f32[96,512]{1,0:T(8,128)S(1)} %pad_maximum_fusion.2), channel_id=1, source_target_pairs={{0,2},{2,0},{4,6},{6,4},{8,10},{10,8},{12,14},{14,12},{1,3},{3,1},... | collective-permute-start | bytes 589832 | tf_op jit(solution)/shard_map/ppermute | solution.py:289
  20.0 0.0 collective-permute-done.3
  20.1 0.1 collective-permute-start.5
  20.2 4.1 %collective-permute-done.7 = f32[96,512]{1,0:T(8,128)S(1)} collective-permute-done((f32[96,512]{1,0:T(8,128)S(1)}, f32[96,512]{1,0:T(8,128)S(1)}, u32[]{:S(2)}, u32[]{:S(2)}) %collective-permute-start.7) | collective-permute-done | bytes 196640 | tf_op jit(solution)/shard_map/ppermute | solution.py:289
  24.3 0.0 copy-start.4
  24.3 0.0 collective-permute-done.1.second_far
  24.3 0.1 collective-permute-start.8
  24.4 0.0 collective-permute-done.5.own1
  24.4 1.7 %collective-permute-done.8.rec1 = f32[192,512]{1,0:T(8,128)S(1)} collective-permute-done((f32[192,512]{1,0:T(8,128)S(1)}, f32[192,512]{1,0:T(8,128)S(1)}, u32[]{:S(2)}, u32[]{:S(2)}) %collective-permute-start.8) | collective-permute-done | bytes 393248 | tf_op jit(solution)/shard_map/ppermute | solution.py:289
  26.1 0.0 copy-done.4
  26.1 1.3 %forward.1 = (f32[256,512]{1,0:T(8,128)S(1)}, f32[256,512]{1,0:T(8,128)S(1)}, f32[256,256]{1,0:T(8,128)S(1)}, f32[256,128]{1,0:T(8,128)S(1)}, f32[8,128]{1,0:T(8...) custom-call(f32[2,2,128,256]{3,2,1,0:T(8,128)S(1)} %copy-done, ...), custom_call_target="tpu_custom_call" | custom-call | flops 1 | bytes 1 | tf_op jit(solution)/shard_map/forward/pallas_call | solution.py:32
  27.4 2.8 %collective-permute-start.9 = (f32[8,128]{1,0:T(8,128)S(1)}, f32[8,128]{1,0:T(8,128)S(1)}, u32[]{:S(2)}, u32[]{:S(2)}) collective-permute-start(f32[8,128]{1,0:T(8,128)S(1)} %get-tuple-element.63.mine), channel_id=1, source_target_pairs={{0,8},{2,10},{4,12},{6,14},{8,0},{10,2},{12,4},{14,6},{1,9},{3,11}... | collective-permute-start | bytes 12296 | tf_op jit(solution)/shard_map/ppermute | solution.py:289
  30.2 0.1 bitcast_maximum_fusion.refs
  30.3 1.2 %backward.1 = (f32[256,512]{1,0:T(8,128)S(1)}, f32[256,512]{1,0:T(8,128)S(1)}, f32[256,256]{1,0:T(8,128)S(1)}) custom-call(f32[256,512]{1,0:T(8,128)S(1)} %get-tuple-element.65.h1_ref, f32[256,512]{1,0:T(8,128)S(1)} %get-tuple-element.66.h2_ref, f32[3,2,512]{2,1,0:T(2,128)S(1)} %bitcast.24, bf16[256,512]{1,0:T(8,128)(2,1)S(1)} %get-tuple-element.67.w1h, ...), custom_call_target="tpu_custom_call" | custom-call | flops 1 | bytes 1 | tf_op jit(solution)/shard_map/backward/pallas_call | solution.py:32
  31.5 0.5 collective-permute-done.9.theirs
  32.0 0.3 force.1
  32.2 1.0 %gradient.1 = (f32[200,512]{1,0:T(8,128)S(1)}, f32[200,512]{1,0:T(8,128)S(1)}, f32[192,512]{1,0:T(8,128)S(1)}, f32[192,512]{1,0:T(8,128)S(1)}) custom-call(f32[256,128]{1,0:T(8,128)S(1)} %get-tuple-element.72.adj_ref, f32[8,128]{1,0:T(8,128)S(1)} %get-tuple-element.73.pot_ref, f32[256,512]{1,0:T(8,128)S(1)} %get-tuple-element.65.h1_ref, ...), custom_call_target="tpu_custom_call" | custom-call | flops 1 | bytes 1 | tf_op jit(solution)/shard_map/gradient/pallas_call | solution.py:32
  33.2 0.1 collective-permute-start.11
  33.3 0.5 collective-permute-start.10
  33.8 2.7 %collective-permute-start.15 = (f32[2,128,256]{2,1,0:T(8,128)S(1)}, f32[2,128,256]{2,1,0:T(8,128)S(1)}, u32[]{:S(2)}, u32[]{:S(2)}) collective-permute-start(f32[2,128,256]{2,1,0:T(8,128)S(1)} %get-tuple-element.88), channel_id=1, source_target_pairs={{0,8},{2,10},{4,12},{6,14},{8,0},{10,2},{12,4},{14,6},{1,9},{3,11}... | collective-permute-start | bytes 786440 | tf_op jit(solution)/shard_map/ppermute | solution.py:289
  36.5 0.0 collective-permute-done.11.came
  36.6 1.6 %collective-permute-start.12 = (f32[104,512]{1,0:T(8,128)S(1)}, f32[104,512]{1,0:T(8,128)S(1)}, u32[]{:S(2)}, u32[]{:S(2)}) collective-permute-start(f32[104,512]{1,0:T(8,128)S(1)} %get-tuple-element.83), channel_id=1, source_target_pairs={{0,2},{2,0},{4,6},{6,4},{8,10},{10,8},{12,14},{14,12},{1,3},{3,1},... | collective-permute-start | bytes 638984 | tf_op jit(solution)/shard_map/ppermute | solution.py:289
  38.1 0.0 collective-permute-done.10.came
  38.2 5.4 %collective-permute-done.12.came = f32[104,512]{1,0:T(8,128)S(1)} collective-permute-done((f32[104,512]{1,0:T(8,128)S(1)}, f32[104,512]{1,0:T(8,128)S(1)}, u32[]{:S(2)}, u32[]{:S(2)}) %collective-permute-start.12) | collective-permute-done | bytes 213024 | tf_op jit(solution)/shard_map/ppermute | solution.py:289
  43.6 2.2 %collective-permute-start.16 = (f32[56,512]{1,0:T(8,128)S(1)}, f32[56,512]{1,0:T(8,128)S(1)}, u32[]{:S(2)}, u32[]{:S(2)}) collective-permute-start(f32[56,512]{1,0:T(8,128)S(1)} %get-tuple-element.93), channel_id=1, source_target_pairs={{0,4},{2,6},{4,0},{6,2},{8,12},{10,14},{12,8},{14,10},{1,5},{3,7},... | collective-permute-start | bytes 344072 | tf_op jit(solution)/shard_map/ppermute | solution.py:289
  45.8 1.5 %collective-permute-start.13 = (f32[96,512]{1,0:T(8,128)S(1)}, f32[96,512]{1,0:T(8,128)S(1)}, u32[]{:S(2)}, u32[]{:S(2)}) collective-permute-start(f32[96,512]{1,0:T(8,128)S(1)} %get-tuple-element.84), channel_id=1, source_target_pairs={{0,2},{2,0},{4,6},{6,4},{8,10},{10,8},{12,14},{14,12},{1,3},{3,1},... | collective-permute-start | bytes 589832 | tf_op jit(solution)/shard_map/ppermute | solution.py:289
  47.3 1.5 %collective-permute-done.15.force_came = f32[2,128,256]{2,1,0:T(8,128)S(1)} collective-permute-done((f32[2,128,256]{2,1,0:T(8,128)S(1)}, f32[2,128,256]{2,1,0:T(8,128)S(1)}, u32[]{:S(2)}, u32[]{:S(2)}) %collective-permute-start.15) | collective-permute-done | bytes 262176 | tf_op jit(solution)/shard_map/ppermute | solution.py:289
  48.8 0.0 collective-permute-start.17
  48.8 1.2 %collective-permute-done.17.rest_0_ = f32[8,128]{1,0:T(8,128)S(1)} collective-permute-done((f32[8,128]{1,0:T(8,128)S(1)}, f32[8,128]{1,0:T(8,128)S(1)}, u32[]{:S(2)}, u32[]{:S(2)}) %collective-permute-start.17) | collective-permute-done | bytes 4128 | tf_op jit(solution)/shard_map/ppermute | solution.py:289
  50.0 1.2 %collective-permute-done.16.b = f32[56,512]{1,0:T(8,128)S(1)} collective-permute-done((f32[56,512]{1,0:T(8,128)S(1)}, f32[56,512]{1,0:T(8,128)S(1)}, u32[]{:S(2)}, u32[]{:S(2)}) %collective-permute-start.16) | collective-permute-done | bytes 114720 | tf_op jit(solution)/shard_map/ppermute | solution.py:289
  51.2 1.7 %collective-permute-start.18 = (f32[56,512]{1,0:T(8,128)S(1)}, f32[56,512]{1,0:T(8,128)S(1)}, u32[]{:S(2)}, u32[]{:S(2)}) collective-permute-start(f32[56,512]{1,0:T(8,128)S(1)} %far_z.1.beyond), channel_id=1, source_target_pairs={{0,8},{2,10},{4,12},{6,14},{8,0},{10,2},{12,4},{14,6},{1,9},{3,11}... | collective-permute-start | bytes 344072 | tf_op jit(solution)/shard_map/ppermute | solution.py:289
  52.9 0.0 collective-permute-done.13.came
  52.9 2.5 %collective-permute-start.14 = (f32[48,512]{1,0:T(8,128)S(1)}, f32[48,512]{1,0:T(8,128)S(1)}, u32[]{:S(2)}, u32[]{:S(2)}) collective-permute-start(f32[48,512]{1,0:T(8,128)S(1)} %get-tuple-element.86), channel_id=1, source_target_pairs={{0,4},{2,6},{4,0},{6,2},{8,12},{10,14},{12,8},{14,10},{1,5},{3,7},... | collective-permute-start | bytes 294920 | tf_op jit(solution)/shard_map/ppermute | solution.py:289
  55.4 3.2 %collective-permute-done.14.b = f32[48,512]{1,0:T(8,128)S(1)} collective-permute-done((f32[48,512]{1,0:T(8,128)S(1)}, f32[48,512]{1,0:T(8,128)S(1)}, u32[]{:S(2)}, u32[]{:S(2)}) %collective-permute-start.14) | collective-permute-done | bytes 98336 | tf_op jit(solution)/shard_map/ppermute | solution.py:289
  58.6 0.0 copy-start.2
  58.6 0.0 copy-start.3
  58.6 0.8 %near_z.1 = (f32[1,8192]{1,0:T(1,128)S(1)}, f32[1,16384]{1,0:T(1,128)S(1)}, f32[2,2,128,256]{3,2,1,0:T(8,128)}) custom-call(f32[48,512]{1,0:T(8,128)S(1)} %get-tuple-element.85.a, f32[48,512]{1,0:T(8,128)S(1)} %collective-permute-done.14.b, f32[2,128,256]{2,1,0:T(8,128)S(1)} %get-tuple-element.87.force_near, ...), custom_call_target="tpu_custom_call" | custom-call | flops 1 | bytes 1 | tf_op jit(solution)/shard_map/near_z/pallas_call | solution.py:401
  59.5 0.2 collective-permute-done.18.came
  59.7 0.0 copy-done.2
  59.7 0.0 copy-done.3
  59.7 0.1 copy-done.5
  59.7 0.0 copy-done.6
  59.7 0.8 %final.1 = (f32[2,8192]{1,0:T(2,128)}, f32[2,16384]{1,0:T(2,128)}, f32[3,2,512]{2,1,0:T(2,128)}, f32[2,8192]{1,0:T(2,128)}, f32[2,16384]{1,0:T(2,128)}, /*index=5*/f32[3,2,512]{2,1,0:T(2,128)}, f32[1,128]{1,0:T(1,128)}) custom-call(f32[1,8192]{1,0:T(1,128)S(1)} %get-tuple-element.89.mine_first, f32[1,16384]{1,0:T(1,128)S(1)} %get-tuple-element.90.mine_second, ...), custom_call_target="tpu_custom_call" | custom-call | flops 1 | bytes 1 | tf_op jit(solution)/shard_map/final/pallas_call | solution.py:416
  (25 shorter events, 0.3 us)
Async XLA Ops:
  0.6 1.0 %copy-start.1 = (f32[2,16384]{1,0:T(2,128)S(1)}, f32[2,16384]{1,0:T(2,128)}, u32[]{:S(2)}) copy-start(f32[2,16384]{1,0:T(2,128)} %second.1) | copy-start | bytes 393220
  0.6 6.7 %copy-start = (f32[2,2,128,256]{3,2,1,0:T(8,128)S(1)}, f32[2,2,128,256]{3,2,1,0:T(8,128)}, u32[]{:S(2)}) copy-start(f32[2,2,128,256]{3,2,1,0:T(8,128)} %desc_ref.1) | copy-start | bytes 1572868
  1.7 5.7 %copy-start.7 = (s32[2,2,128]{2,1,0:T(2,128)S(1)}, s32[2,2,128]{2,1,0:T(2,128)}, u32[]{:S(2)}) copy-start(s32[2,2,128]{2,1,0:T(2,128)} %ids_hbm.1) | copy-start | bytes 6148
  1.7 8.9 %collective-permute-start.4 = (f32[48,512]{1,0:T(8,128)S(1)}, f32[48,512]{1,0:T(8,128)S(1)}, u32[]{:S(2)}, u32[]{:S(2)}) collective-permute-start(f32[48,512]{1,0:T(8,128)S(1)} %get-tuple-element.104), channel_id=1, source_target_pairs={{0,8},{2,10},{4,12},{6,14},{8,0},{10,2},{12,4},{14,6},{1,9},{3,11}... | collective-permute-start | bytes 294920 | tf_op jit(solution)/shard_map/ppermute | solution.py:289
  5.8 1.6 %copy-start.8 = (s32[2,2]{1,0:T(2,128)S(1)}, s32[2,2]{1,0:T(2,128)}, u32[]{:S(2)}) copy-start(s32[2,2]{1,0:T(2,128)} %counts_hbm.1) | copy-start | bytes 52
  5.8 1.6 %copy-start.9 = (f32[32]{0:T(128)S(1)}, f32[32]{0:T(128)}, u32[]{:S(2)}) copy-start(f32[32]{0:T(128)} %param.13) | copy-start | bytes 388
  5.8 6.3 %collective-permute-start.2 = (f32[48,512]{1,0:T(8,128)S(1)}, f32[48,512]{1,0:T(8,128)S(1)}, u32[]{:S(2)}, u32[]{:S(2)}) collective-permute-start(f32[48,512]{1,0:T(8,128)S(1)} %get-tuple-element.58), channel_id=1, source_target_pairs={{0,4},{2,6},{4,0},{6,2},{8,12},{10,14},{12,8},{14,10},{1,5},{3,7},... | collective-permute-start | bytes 294920 | tf_op jit(solution)/shard_map/ppermute | solution.py:289
  7.6 9.1 %collective-permute-start = (f32[136,256]{1,0:T(8,128)S(1)}, f32[136,256]{1,0:T(8,128)S(1)}, u32[]{:S(2)}, u32[]{:S(2)}) collective-permute-start(f32[136,256]{1,0:T(8,128)S(1)} %get-tuple-element.56), channel_id=1, source_target_pairs={{0,8},{2,10},{4,12},{6,14},{8,0},{10,2},{12,4},{14,6},{1,9},{3,11}... | collective-permute-start | bytes 417800 | tf_op jit(solution)/shard_map/ppermute | solution.py:289
  10.6 7.8 %collective-permute-start.6 = (f32[48,512]{1,0:T(8,128)S(1)}, f32[48,512]{1,0:T(8,128)S(1)}, u32[]{:S(2)}, u32[]{:S(2)}) collective-permute-start(f32[48,512]{1,0:T(8,128)S(1)} %collective-permute-done.4), channel_id=1, source_target_pairs={{0,4},{2,6},{4,0},{6,2},{8,12},{10,14},{12,8},{14,10},{1,5},{3,7},... | collective-permute-start | bytes 294920 | tf_op jit(solution)/shard_map/ppermute | solution.py:289
  12.1 7.9 %collective-permute-start.3 = (f32[96,512]{1,0:T(8,128)S(1)}, f32[96,512]{1,0:T(8,128)S(1)}, u32[]{:S(2)}, u32[]{:S(2)}) collective-permute-start(f32[96,512]{1,0:T(8,128)S(1)} %pad_maximum_fusion.1), channel_id=1, source_target_pairs={{0,2},{2,0},{4,6},{6,4},{8,10},{10,8},{12,14},{14,12},{1,3},{3,1},... | collective-permute-start | bytes 589832 | tf_op jit(solution)/shard_map/ppermute | solution.py:289
  16.8 7.5 %collective-permute-start.1 = (f32[128,256]{1,0:T(8,128)S(1)}, f32[128,256]{1,0:T(8,128)S(1)}, u32[]{:S(2)}, u32[]{:S(2)}) collective-permute-start(f32[128,256]{1,0:T(8,128)S(1)} %slice.41.first_far), channel_id=1, source_target_pairs={{0,16},{16,0},{1,17},{17,1},{2,18},{18,2},{3,19},{19,3},{4,20},{20... | collective-permute-start | bytes 393224 | tf_op jit(solution)/shard_map/ppermute | solution.py:289
  18.4 5.8 %collective-permute-start.7 = (f32[96,512]{1,0:T(8,128)S(1)}, f32[96,512]{1,0:T(8,128)S(1)}, u32[]{:S(2)}, u32[]{:S(2)}) collective-permute-start(f32[96,512]{1,0:T(8,128)S(1)} %pad_maximum_fusion.2), channel_id=1, source_target_pairs={{0,2},{2,0},{4,6},{6,4},{8,10},{10,8},{12,14},{14,12},{1,3},{3,1},... | collective-permute-start | bytes 589832 | tf_op jit(solution)/shard_map/ppermute | solution.py:289
  20.1 4.3 %collective-permute-start.5 = (f32[192,512]{1,0:T(8,128)S(1)}, f32[192,512]{1,0:T(8,128)S(1)}, u32[]{:S(2)}, u32[]{:S(2)}) collective-permute-start(f32[192,512]{1,0:T(8,128)S(1)} %constant_dynamic-update-slice_fusion.own0), channel_id=1, source_target_pairs={{0,1},{1,0},{2,3},{3,2},{4,5},{5,4},{6,7},{7,6},{8,9},{9,8},{10,11... | collective-permute-start | bytes 1179656 | tf_op jit(solution)/shard_map/ppermute | solution.py:289
  24.3 1.8 %copy-start.4 = (f32[2,3,512]{2,0,1:T(2,128)S(1)}, f32[2,3,512]{2,0,1:T(2,128)}, u32[]{:S(2)}) copy-start(f32[2,3,512]{2,0,1:T(2,128)} %param.16) | copy-start | bytes 36868
  24.3 1.8 %collective-permute-start.8 = (f32[192,512]{1,0:T(8,128)S(1)}, f32[192,512]{1,0:T(8,128)S(1)}, u32[]{:S(2)}, u32[]{:S(2)}) collective-permute-start(f32[192,512]{1,0:T(8,128)S(1)} %pad_maximum_fusion.rec0), channel_id=1, source_target_pairs={{0,1},{1,0},{2,3},{3,2},{4,5},{5,4},{6,7},{7,6},{8,9},{9,8},{10,11... | collective-permute-start | bytes 1179656 | tf_op jit(solution)/shard_map/ppermute | solution.py:289
  27.4 4.6 %collective-permute-start.9 = (f32[8,128]{1,0:T(8,128)S(1)}, f32[8,128]{1,0:T(8,128)S(1)}, u32[]{:S(2)}, u32[]{:S(2)}) collective-permute-start(f32[8,128]{1,0:T(8,128)S(1)} %get-tuple-element.63.mine), channel_id=1, source_target_pairs={{0,8},{2,10},{4,12},{6,14},{8,0},{10,2},{12,4},{14,6},{1,9},{3,11}... | collective-permute-start | bytes 12296 | tf_op jit(solution)/shard_map/ppermute | solution.py:289
  33.2 3.3 %collective-permute-start.11 = (f32[200,512]{1,0:T(8,128)S(1)}, f32[200,512]{1,0:T(8,128)S(1)}, u32[]{:S(2)}, u32[]{:S(2)}) collective-permute-start(f32[200,512]{1,0:T(8,128)S(1)} %get-tuple-element.82), channel_id=1, source_target_pairs={{0,1},{1,0},{2,3},{3,2},{4,5},{5,4},{6,7},{7,6},{8,9},{9,8},{10,11... | collective-permute-start | bytes 1228808 | tf_op jit(solution)/shard_map/ppermute | solution.py:289
  33.3 4.8 %collective-permute-start.10 = (f32[192,512]{1,0:T(8,128)S(1)}, f32[192,512]{1,0:T(8,128)S(1)}, u32[]{:S(2)}, u32[]{:S(2)}) collective-permute-start(f32[192,512]{1,0:T(8,128)S(1)} %get-tuple-element.78), channel_id=1, source_target_pairs={{0,1},{1,0},{2,3},{3,2},{4,5},{5,4},{6,7},{7,6},{8,9},{9,8},{10,11... | collective-permute-start | bytes 1179656 | tf_op jit(solution)/shard_map/ppermute | solution.py:289
  33.8 15.0 %collective-permute-start.15 = (f32[2,128,256]{2,1,0:T(8,128)S(1)}, f32[2,128,256]{2,1,0:T(8,128)S(1)}, u32[]{:S(2)}, u32[]{:S(2)}) collective-permute-start(f32[2,128,256]{2,1,0:T(8,128)S(1)} %get-tuple-element.88), channel_id=1, source_target_pairs={{0,8},{2,10},{4,12},{6,14},{8,0},{10,2},{12,4},{14,6},{1,9},{3,11}... | collective-permute-start | bytes 786440 | tf_op jit(solution)/shard_map/ppermute | solution.py:289
  36.6 7.0 %collective-permute-start.12 = (f32[104,512]{1,0:T(8,128)S(1)}, f32[104,512]{1,0:T(8,128)S(1)}, u32[]{:S(2)}, u32[]{:S(2)}) collective-permute-start(f32[104,512]{1,0:T(8,128)S(1)} %get-tuple-element.83), channel_id=1, source_target_pairs={{0,2},{2,0},{4,6},{6,4},{8,10},{10,8},{12,14},{14,12},{1,3},{3,1},... | collective-permute-start | bytes 638984 | tf_op jit(solution)/shard_map/ppermute | solution.py:289
  43.6 7.5 %collective-permute-start.16 = (f32[56,512]{1,0:T(8,128)S(1)}, f32[56,512]{1,0:T(8,128)S(1)}, u32[]{:S(2)}, u32[]{:S(2)}) collective-permute-start(f32[56,512]{1,0:T(8,128)S(1)} %get-tuple-element.93), channel_id=1, source_target_pairs={{0,4},{2,6},{4,0},{6,2},{8,12},{10,14},{12,8},{14,10},{1,5},{3,7},... | collective-permute-start | bytes 344072 | tf_op jit(solution)/shard_map/ppermute | solution.py:289
  45.8 7.1 %collective-permute-start.13 = (f32[96,512]{1,0:T(8,128)S(1)}, f32[96,512]{1,0:T(8,128)S(1)}, u32[]{:S(2)}, u32[]{:S(2)}) collective-permute-start(f32[96,512]{1,0:T(8,128)S(1)} %get-tuple-element.84), channel_id=1, source_target_pairs={{0,2},{2,0},{4,6},{6,4},{8,10},{10,8},{12,14},{14,12},{1,3},{3,1},... | collective-permute-start | bytes 589832 | tf_op jit(solution)/shard_map/ppermute | solution.py:289
  48.8 1.2 %collective-permute-start.17 = (f32[8,128]{1,0:T(8,128)S(1)}, f32[8,128]{1,0:T(8,128)S(1)}, u32[]{:S(2)}, u32[]{:S(2)}) collective-permute-start(f32[8,128]{1,0:T(8,128)S(1)} %slice_bitcast_fusion), channel_id=1, source_target_pairs={{0,1},{1,0},{2,3},{3,2},{4,5},{5,4},{6,7},{7,6},{8,9},{9,8},{10,11... | collective-permute-start | bytes 12296 | tf_op jit(solution)/shard_map/ppermute | solution.py:289
  51.2 8.5 %collective-permute-start.18 = (f32[56,512]{1,0:T(8,128)S(1)}, f32[56,512]{1,0:T(8,128)S(1)}, u32[]{:S(2)}, u32[]{:S(2)}) collective-permute-start(f32[56,512]{1,0:T(8,128)S(1)} %far_z.1.beyond), channel_id=1, source_target_pairs={{0,8},{2,10},{4,12},{6,14},{8,0},{10,2},{12,4},{14,6},{1,9},{3,11}... | collective-permute-start | bytes 344072 | tf_op jit(solution)/shard_map/ppermute | solution.py:289
  52.9 5.7 %collective-permute-start.14 = (f32[48,512]{1,0:T(8,128)S(1)}, f32[48,512]{1,0:T(8,128)S(1)}, u32[]{:S(2)}, u32[]{:S(2)}) collective-permute-start(f32[48,512]{1,0:T(8,128)S(1)} %get-tuple-element.86), channel_id=1, source_target_pairs={{0,4},{2,6},{4,0},{6,2},{8,12},{10,14},{12,8},{14,10},{1,5},{3,7},... | collective-permute-start | bytes 294920 | tf_op jit(solution)/shard_map/ppermute | solution.py:289
  58.6 1.0 %copy-start.2 = (f32[2,8192]{1,0:T(2,128)S(1)}, f32[2,8192]{1,0:T(2,128)}, u32[]{:S(2)}) copy-start(f32[2,8192]{1,0:T(2,128)} %first.1) | copy-start | bytes 196612
  58.6 1.1 %copy-start.3 = (f32[2,16384]{1,0:T(2,128)S(1)}, f32[2,16384]{1,0:T(2,128)}, u32[]{:S(2)}) copy-start(f32[2,16384]{1,0:T(2,128)} %second_mom.1) | copy-start | bytes 393220
  58.6 1.1 %copy-start.5 = (f32[2,8192]{1,0:T(2,128)S(1)}, f32[2,8192]{1,0:T(2,128)}, u32[]{:S(2)}) copy-start(f32[2,8192]{1,0:T(2,128)} %first_mom.1) | copy-start | bytes 196612
  58.6 1.1 %copy-start.6 = (f32[2,3,512]{2,0,1:T(2,128)S(1)}, f32[2,3,512]{2,0,1:T(2,128)}, u32[]{:S(2)}) copy-start(f32[2,3,512]{2,0,1:T(2,128)} %param.19) | copy-start | bytes 36868

commit v5 on v4

--- a/solution.py
+++ b/solution.py
@@ -151,7 +151,7 @@
 
 
 def gradient_kernel(
-    adj_ref, pot_ref, h1_ref, h2_ref, g2_ref, g1_ref, x_ref, keep_far, give_far, keep_near, give_near, dw1, dw2,
+    adj_ref, pot_ref, h1_ref, h2_ref, g2_ref, g1_ref, x_ref, keep_all, give_all, dw1, dw2,
 ):
     spot, core, half, chain = place()
     adj = adj_ref[...][:, 0:1]
@@ -162,6 +162,9 @@
     rows1 = dw1.shape[0] // 16
     rows2 = dw2.shape[0] // 16
     rows = rows1 + rows2
+    middle = 4 * rows + 8
+    keep_far, give_far = [ref.at[pl.ds(0, middle)] for ref in (keep_all, give_all)]
+    keep_near, give_near = [ref.at[pl.ds(middle, 4 * rows)] for ref in (keep_all, give_all)]
     for far, keep, give in ((4, keep_far, give_far), (0, keep_near, give_near)):
         for index, delta in enumerate((0, 2, 1, 3)):
             for out, holder in ((keep, core), (give, 1 - core)):
@@ -193,6 +196,20 @@
         end = keep[2 * rows :, :] + came[2 * rows :, :]
         stay[rows:, :] = end
         leave[rows:, :] = end
+
+
+def core_kernel(keep, came, far_stay, far_leave, near_stay, near_leave):
+    half_rows = near_stay.shape[0]
+    tail = far_stay.shape[0] - half_rows
+    far_rows = 2 * half_rows + tail
+    total = lambda start, rows: keep[start : start + rows, :] + came[start : start + rows, :]
+    far_stay[0:half_rows, :] = total(0, half_rows)
+    far_leave[0:half_rows, :] = total(half_rows, half_rows)
+    end = total(2 * half_rows, tail)
+    far_stay[half_rows:, :] = end
+    far_leave[half_rows:, :] = end
+    near_stay[...] = total(far_rows, half_rows)
+    near_leave[...] = total(far_rows + half_rows, half_rows)
 
 
 def sum_kernel(a, b, *rest):
@@ -370,9 +387,9 @@
     force_came = to[4](force_far)
     tail = 8
     group = 4 * rows
-    keep_far, give_far, keep_near, give_near = call(
+    keep, give = call(
         gradient_kernel,
-        [((group + tail, hidden),)] * 2 + [((group, hidden),)] * 2,
+        [((2 * group + tail, hidden),)] * 2,
         (adj, pot, h1, h2, g2, g1, x),
         scratch=[pltpu.VMEM((width, hidden), F32), pltpu.VMEM((hidden, hidden), F32)],
         flops=6 * work * hidden * (width + hidden),
@@ -384,8 +401,12 @@
         left = (keep.shape[0] - end) // 2 + end
         return call(halving_kernel, [((left, hidden),)] * 2, (keep, came), size=4 * 4 * left * hidden, name=name)
 
-    far_stay, far_leave = halve(keep_far, to_core(give_far), tail, "far_core")
-    near_stay, near_leave = halve(keep_near, to_core(give_near), 0, "near_core")
+    far_stay, far_leave, near_stay, near_leave = call(
+        core_kernel,
+        [((group // 2 + tail, hidden),)] * 2 + [((group // 2, hidden),)] * 2,
+        (keep, to_core(give)),
+        name="core_sum",
+    )
     far_came = to[1](far_leave)
     far_stay, far_leave = halve(far_stay, far_came, tail, "far_x")
     near_came = to[1](after(near_leave, far_came))

time: 60.7 us -> 60.7 us (level)
    ppermute x19 -> x18, starting transfers between devices: 28 us -> 27.6 us  [flip(): lax.ppermute(x, axis, [(i, i ^ delta) for i in range(size)])]
    ppermute x19 -> x18, waiting for transfers between devices: 24.6 us -> 24.9 us  [flip(): lax.ppermute(x, axis, [(i, i ^ delta) for i in range(size)])]
    pallas_call x9 -> x8, Pallas kernels: 3.85 us -> 3.87 us  [call(): pl.pallas_call(kernel, out_shape=[jax.ShapeDtypeStruct(shape, kind) for s...]
  transfers between devices with their start and end apart: 19 -> 18, of which waited for: 11 -> 11; matrix products, arithmetic and copies ran while one was open for 0% -> 0% of each run, Pallas kernels for 4% -> 4%
where the time goes in v5:
time: 60.7 us; the launch traced here: 60.5 us
  starting transfers between devices  27.6 us (45%)
  waiting for transfers between devices  24.9 us (41%)
  Pallas kernels  5.75 us (9%)
  local copies, waits for them, and re-layouts  1.19 us (2%)
  between operations  0.93 us (2%)
    ppermute x18, starting transfers between devices, flip(): lax.ppermute(x, axis, [(i, i ^ delta) for i in range(size)])  27.6 us
    ppermute x18, waiting for transfers between devices, flip(): lax.ppermute(x, axis, [(i, i ^ delta) for i in range(size)])  24.9 us
    pallas_call x8, Pallas kernels, call(): pl.pallas_call(kernel, out_shape=[jax.ShapeDtypeStruct(shape, kind) for s...  3.87 us
  transfers between devices with their start and end apart: 18, of which 11 were waited for; matrix products, arithmetic and copies ran while one was open for 0% of the time, Pallas kernels for 4%

profile of v5, /device:TPU:0, one launch (start us, length us, event | category | flops | bytes accessed | tf_op | source)
XLA Modules:
  0.0 60.5 jit_solution(15358920995372106782)
XLA Ops:
  0.6 0.0 copy-start.1
  0.6 0.0 copy-start
  0.7 0.9 %bitcast_dynamic-update-slice_fusion.1 = f32[2,48,512]{2,1,0:T(8,128)S(1)} fusion(f32[1,2,16,512]{3,1,2,0:T(2,128)} %bitcast.22), kind=kLoop, calls=%fused_computation.6 | loop fusion | bytes 131072
  1.6 0.0 copy-done.1
  1.7 0.0 copy-start.7
  1.7 4.1 %collective-permute-start.4 = (f32[48,512]{1,0:T(8,128)S(1)}, f32[48,512]{1,0:T(8,128)S(1)}, u32[]{:S(2)}, u32[]{:S(2)}) collective-permute-start(f32[48,512]{1,0:T(8,128)S(1)} %get-tuple-element.100), channel_id=1, source_target_pairs={{0,8},{2,10},{4,12},{6,14},{8,0},{10,2},{12,4},{14,6},{1,9},{3,11}... | collective-permute-start | bytes 294920 | tf_op jit(solution)/shard_map/ppermute | solution.py:306
  5.8 0.0 copy-start.8
  5.8 0.0 copy-start.9
  5.8 1.6 %collective-permute-start.2 = (f32[48,512]{1,0:T(8,128)S(1)}, f32[48,512]{1,0:T(8,128)S(1)}, u32[]{:S(2)}, u32[]{:S(2)}) collective-permute-start(f32[48,512]{1,0:T(8,128)S(1)} %get-tuple-element.56), channel_id=1, source_target_pairs={{0,4},{2,6},{4,0},{6,2},{8,12},{10,14},{12,8},{14,10},{1,5},{3,7},... | collective-permute-start | bytes 294920 | tf_op jit(solution)/shard_map/ppermute | solution.py:306
  7.4 0.0 copy-done
  7.4 0.0 copy-done.7
  7.4 0.0 copy-done.8
  7.4 0.0 copy-done.9
  7.4 0.2 message.1
  7.6 0.4 collective-permute-start
  8.0 2.6 %collective-permute-done.4 = f32[48,512]{1,0:T(8,128)S(1)} collective-permute-done((f32[48,512]{1,0:T(8,128)S(1)}, f32[48,512]{1,0:T(8,128)S(1)}, u32[]{:S(2)}, u32[]{:S(2)}) %collective-permute-start.4) | collective-permute-done | bytes 98336 | tf_op jit(solution)/shard_map/ppermute | solution.py:306
  10.6 1.5 %collective-permute-start.6 = (f32[48,512]{1,0:T(8,128)S(1)}, f32[48,512]{1,0:T(8,128)S(1)}, u32[]{:S(2)}, u32[]{:S(2)}) collective-permute-start(f32[48,512]{1,0:T(8,128)S(1)} %collective-permute-done.4), channel_id=1, source_target_pairs={{0,4},{2,6},{4,0},{6,2},{8,12},{10,14},{12,8},{14,10},{1,5},{3,7},... | collective-permute-start | bytes 294920 | tf_op jit(solution)/shard_map/ppermute | solution.py:306
  12.1 0.0 collective-permute-done.2
  12.1 1.6 %collective-permute-start.3 = (f32[96,512]{1,0:T(8,128)S(1)}, f32[96,512]{1,0:T(8,128)S(1)}, u32[]{:S(2)}, u32[]{:S(2)}) collective-permute-start(f32[96,512]{1,0:T(8,128)S(1)} %pad_maximum_fusion.1), channel_id=1, source_target_pairs={{0,2},{2,0},{4,6},{6,4},{8,10},{10,8},{12,14},{14,12},{1,3},{3,1},... | collective-permute-start | bytes 589832 | tf_op jit(solution)/shard_map/ppermute | solution.py:306
  13.7 3.1 %collective-permute-done = f32[136,256]{1,0:T(8,128)S(1)} collective-permute-done((f32[136,256]{1,0:T(8,128)S(1)}, f32[136,256]{1,0:T(8,128)S(1)}, u32[]{:S(2)}, u32[]{:S(2)}) %collective-permute-start) | collective-permute-done | bytes 139296 | tf_op jit(solution)/shard_map/ppermute | solution.py:306
  16.8 1.6 %collective-permute-start.1 = (f32[128,256]{1,0:T(8,128)S(1)}, f32[128,256]{1,0:T(8,128)S(1)}, u32[]{:S(2)}, u32[]{:S(2)}) collective-permute-start(f32[128,256]{1,0:T(8,128)S(1)} %slice.41.first_far), channel_id=1, source_target_pairs={{0,16},{16,0},{1,17},{17,1},{2,18},{18,2},{3,19},{19,3},{4,20},{20... | collective-permute-start | bytes 393224 | tf_op jit(solution)/shard_map/ppermute | solution.py:306
  18.4 0.0 collective-permute-done.6
  18.4 1.6 %collective-permute-start.7 = (f32[96,512]{1,0:T(8,128)S(1)}, f32[96,512]{1,0:T(8,128)S(1)}, u32[]{:S(2)}, u32[]{:S(2)}) collective-permute-start(f32[96,512]{1,0:T(8,128)S(1)} %pad_maximum_fusion.2), channel_id=1, source_target_pairs={{0,2},{2,0},{4,6},{6,4},{8,10},{10,8},{12,14},{14,12},{1,3},{3,1},... | collective-permute-start | bytes 589832 | tf_op jit(solution)/shard_map/ppermute | solution.py:306
  20.0 0.0 collective-permute-done.3
  20.1 0.1 collective-permute-start.5
  20.2 4.1 %collective-permute-done.7 = f32[96,512]{1,0:T(8,128)S(1)} collective-permute-done((f32[96,512]{1,0:T(8,128)S(1)}, f32[96,512]{1,0:T(8,128)S(1)}, u32[]{:S(2)}, u32[]{:S(2)}) %collective-permute-start.7) | collective-permute-done | bytes 196640 | tf_op jit(solution)/shard_map/ppermute | solution.py:306
  24.3 0.0 copy-start.4
  24.3 0.0 collective-permute-done.1.second_far
  24.3 0.1 collective-permute-start.8
  24.4 0.0 collective-permute-done.5.own1
  24.4 1.7 %collective-permute-done.8.rec1 = f32[192,512]{1,0:T(8,128)S(1)} collective-permute-done((f32[192,512]{1,0:T(8,128)S(1)}, f32[192,512]{1,0:T(8,128)S(1)}, u32[]{:S(2)}, u32[]{:S(2)}) %collective-permute-start.8) | collective-permute-done | bytes 393248 | tf_op jit(solution)/shard_map/ppermute | solution.py:306
  26.1 0.0 copy-done.4
  26.1 1.3 %forward.1 = (f32[256,512]{1,0:T(8,128)S(1)}, f32[256,512]{1,0:T(8,128)S(1)}, f32[256,256]{1,0:T(8,128)S(1)}, f32[256,128]{1,0:T(8,128)S(1)}, f32[8,128]{1,0:T(8...) custom-call(f32[2,2,128,256]{3,2,1,0:T(8,128)S(1)} %copy-done, ...), custom_call_target="tpu_custom_call" | custom-call | flops 1 | bytes 1 | tf_op jit(solution)/shard_map/forward/pallas_call | solution.py:32
  27.4 2.8 %collective-permute-start.9 = (f32[8,128]{1,0:T(8,128)S(1)}, f32[8,128]{1,0:T(8,128)S(1)}, u32[]{:S(2)}, u32[]{:S(2)}) collective-permute-start(f32[8,128]{1,0:T(8,128)S(1)} %get-tuple-element.61.mine), channel_id=1, source_target_pairs={{0,8},{2,10},{4,12},{6,14},{8,0},{10,2},{12,4},{14,6},{1,9},{3,11}... | collective-permute-start | bytes 12296 | tf_op jit(solution)/shard_map/ppermute | solution.py:306
  30.2 0.1 bitcast_maximum_fusion.refs
  30.3 1.2 %backward.1 = (f32[256,512]{1,0:T(8,128)S(1)}, f32[256,512]{1,0:T(8,128)S(1)}, f32[256,256]{1,0:T(8,128)S(1)}) custom-call(f32[256,512]{1,0:T(8,128)S(1)} %get-tuple-element.63.h1_ref, f32[256,512]{1,0:T(8,128)S(1)} %get-tuple-element.64.h2_ref, f32[3,2,512]{2,1,0:T(2,128)S(1)} %bitcast.24, bf16[256,512]{1,0:T(8,128)(2,1)S(1)} %get-tuple-element.65.w1h, ...), custom_call_target="tpu_custom_call" | custom-call | flops 1 | bytes 1 | tf_op jit(solution)/shard_map/backward/pallas_call | solution.py:32
  31.5 0.5 collective-permute-done.9.theirs
  32.0 0.3 force.1
  32.2 1.0 %gradient.1 = (f32[392,512]{1,0:T(8,128)S(1)}, f32[392,512]{1,0:T(8,128)S(1)}) custom-call(f32[256,128]{1,0:T(8,128)S(1)} %get-tuple-element.70.adj_ref, f32[8,128]{1,0:T(8,128)S(1)} %get-tuple-element.71.pot_ref, f32[256,512]{1,0:T(8,128)S(1)} %get-tuple-element.63.h1_ref, f32[256,512]{1,0:T(8,128)S(1)} %get-tuple-element.64.h2_ref, ...), custom_call_target="tpu_custom_call" | custom-call | flops 1 | bytes 1 | tf_op jit(solution)/shard_map/gradient/pallas_call | solution.py:32
  33.2 0.1 collective-permute-start.10
  33.3 2.8 %collective-permute-start.14 = (f32[2,128,256]{2,1,0:T(8,128)S(1)}, f32[2,128,256]{2,1,0:T(8,128)S(1)}, u32[]{:S(2)}, u32[]{:S(2)}) collective-permute-start(f32[2,128,256]{2,1,0:T(8,128)S(1)} %get-tuple-element.84), channel_id=1, source_target_pairs={{0,8},{2,10},{4,12},{6,14},{8,0},{10,2},{12,4},{14,6},{1,9},{3,11}... | collective-permute-start | bytes 786440 | tf_op jit(solution)/shard_map/ppermute | solution.py:306
  36.1 0.0 collective-permute-done.10.came
  36.1 0.1 core_sum.1
  36.2 1.6 %collective-permute-start.11 = (f32[104,512]{1,0:T(8,128)S(1)}, f32[104,512]{1,0:T(8,128)S(1)}, u32[]{:S(2)}, u32[]{:S(2)}) collective-permute-start(f32[104,512]{1,0:T(8,128)S(1)} %get-tuple-element.79), channel_id=1, source_target_pairs={{0,2},{2,0},{4,6},{6,4},{8,10},{10,8},{12,14},{14,12},{1,3},{3,1},... | collective-permute-start | bytes 638984 | tf_op jit(solution)/shard_map/ppermute | solution.py:306
  37.7 5.8 %collective-permute-done.11.came = f32[104,512]{1,0:T(8,128)S(1)} collective-permute-done((f32[104,512]{1,0:T(8,128)S(1)}, f32[104,512]{1,0:T(8,128)S(1)}, u32[]{:S(2)}, u32[]{:S(2)}) %collective-permute-start.11) | collective-permute-done | bytes 213024 | tf_op jit(solution)/shard_map/ppermute | solution.py:306
  43.6 2.2 %collective-permute-start.15 = (f32[56,512]{1,0:T(8,128)S(1)}, f32[56,512]{1,0:T(8,128)S(1)}, u32[]{:S(2)}, u32[]{:S(2)}) collective-permute-start(f32[56,512]{1,0:T(8,128)S(1)} %get-tuple-element.89), channel_id=1, source_target_pairs={{0,4},{2,6},{4,0},{6,2},{8,12},{10,14},{12,8},{14,10},{1,5},{3,7},... | collective-permute-start | bytes 344072 | tf_op jit(solution)/shard_map/ppermute | solution.py:306
  45.8 1.5 %collective-permute-start.12 = (f32[96,512]{1,0:T(8,128)S(1)}, f32[96,512]{1,0:T(8,128)S(1)}, u32[]{:S(2)}, u32[]{:S(2)}) collective-permute-start(f32[96,512]{1,0:T(8,128)S(1)} %get-tuple-element.80), channel_id=1, source_target_pairs={{0,2},{2,0},{4,6},{6,4},{8,10},{10,8},{12,14},{14,12},{1,3},{3,1},... | collective-permute-start | bytes 589832 | tf_op jit(solution)/shard_map/ppermute | solution.py:306
  47.3 1.4 %collective-permute-done.14.force_came = f32[2,128,256]{2,1,0:T(8,128)S(1)} collective-permute-done((f32[2,128,256]{2,1,0:T(8,128)S(1)}, f32[2,128,256]{2,1,0:T(8,128)S(1)}, u32[]{:S(2)}, u32[]{:S(2)}) %collective-permute-start.14) | collective-permute-done | bytes 262176 | tf_op jit(solution)/shard_map/ppermute | solution.py:306
  48.7 0.0 collective-permute-start.16
  48.7 1.2 %collective-permute-done.16.rest_0_ = f32[8,128]{1,0:T(8,128)S(1)} collective-permute-done((f32[8,128]{1,0:T(8,128)S(1)}, f32[8,128]{1,0:T(8,128)S(1)}, u32[]{:S(2)}, u32[]{:S(2)}) %collective-permute-start.16) | collective-permute-done | bytes 4128 | tf_op jit(solution)/shard_map/ppermute | solution.py:306
  49.9 1.2 %collective-permute-done.15.b = f32[56,512]{1,0:T(8,128)S(1)} collective-permute-done((f32[56,512]{1,0:T(8,128)S(1)}, f32[56,512]{1,0:T(8,128)S(1)}, u32[]{:S(2)}, u32[]{:S(2)}) %collective-permute-start.15) | collective-permute-done | bytes 114720 | tf_op jit(solution)/shard_map/ppermute | solution.py:306
  51.1 1.7 %collective-permute-start.17 = (f32[56,512]{1,0:T(8,128)S(1)}, f32[56,512]{1,0:T(8,128)S(1)}, u32[]{:S(2)}, u32[]{:S(2)}) collective-permute-start(f32[56,512]{1,0:T(8,128)S(1)} %far_z.1.beyond), channel_id=1, source_target_pairs={{0,8},{2,10},{4,12},{6,14},{8,0},{10,2},{12,4},{14,6},{1,9},{3,11}... | collective-permute-start | bytes 344072 | tf_op jit(solution)/shard_map/ppermute | solution.py:306
  52.8 0.0 collective-permute-done.12.came
  52.8 2.5 %collective-permute-start.13 = (f32[48,512]{1,0:T(8,128)S(1)}, f32[48,512]{1,0:T(8,128)S(1)}, u32[]{:S(2)}, u32[]{:S(2)}) collective-permute-start(f32[48,512]{1,0:T(8,128)S(1)} %get-tuple-element.82), channel_id=1, source_target_pairs={{0,4},{2,6},{4,0},{6,2},{8,12},{10,14},{12,8},{14,10},{1,5},{3,7},... | collective-permute-start | bytes 294920 | tf_op jit(solution)/shard_map/ppermute | solution.py:306
  55.4 3.2 %collective-permute-done.13.b = f32[48,512]{1,0:T(8,128)S(1)} collective-permute-done((f32[48,512]{1,0:T(8,128)S(1)}, f32[48,512]{1,0:T(8,128)S(1)}, u32[]{:S(2)}, u32[]{:S(2)}) %collective-permute-start.13) | collective-permute-done | bytes 98336 | tf_op jit(solution)/shard_map/ppermute | solution.py:306
  58.6 0.0 copy-start.2
  58.6 0.0 copy-start.5
  58.6 0.8 %near_z.1 = (f32[1,8192]{1,0:T(1,128)S(1)}, f32[1,16384]{1,0:T(1,128)S(1)}, f32[2,2,128,256]{3,2,1,0:T(8,128)}) custom-call(f32[48,512]{1,0:T(8,128)S(1)} %get-tuple-element.81.a, f32[48,512]{1,0:T(8,128)S(1)} %collective-permute-done.13.b, f32[2,128,256]{2,1,0:T(8,128)S(1)} %get-tuple-element.83.force_near, ...), custom_call_target="tpu_custom_call" | custom-call | flops 1 | bytes 1 | tf_op jit(solution)/shard_map/near_z/pallas_call | solution.py:422
  59.4 0.2 collective-permute-done.17.came
  59.6 0.0 copy-done.2
  59.6 0.0 copy-done.3
  59.6 0.1 copy-done.5
  59.7 0.0 copy-done.6
  59.7 0.8 %final.1 = (f32[2,8192]{1,0:T(2,128)}, f32[2,16384]{1,0:T(2,128)}, f32[3,2,512]{2,1,0:T(2,128)}, f32[2,8192]{1,0:T(2,128)}, f32[2,16384]{1,0:T(2,128)}, /*index=5*/f32[3,2,512]{2,1,0:T(2,128)}, f32[1,128]{1,0:T(1,128)}) custom-call(f32[1,8192]{1,0:T(1,128)S(1)} %get-tuple-element.85.mine_first, f32[1,16384]{1,0:T(1,128)S(1)} %get-tuple-element.86.mine_second, ...), custom_call_target="tpu_custom_call" | custom-call | flops 1 | bytes 1 | tf_op jit(solution)/shard_map/final/pallas_call | solution.py:437
  (22 shorter events, 0.3 us)
Async XLA Ops:
  0.6 1.0 %copy-start.1 = (f32[2,16384]{1,0:T(2,128)S(1)}, f32[2,16384]{1,0:T(2,128)}, u32[]{:S(2)}) copy-start(f32[2,16384]{1,0:T(2,128)} %second.1) | copy-start | bytes 393220
  0.6 6.7 %copy-start = (f32[2,2,128,256]{3,2,1,0:T(8,128)S(1)}, f32[2,2,128,256]{3,2,1,0:T(8,128)}, u32[]{:S(2)}) copy-start(f32[2,2,128,256]{3,2,1,0:T(8,128)} %desc_ref.1) | copy-start | bytes 1572868
  1.7 5.7 %copy-start.7 = (s32[2,2,128]{2,1,0:T(2,128)S(1)}, s32[2,2,128]{2,1,0:T(2,128)}, u32[]{:S(2)}) copy-start(s32[2,2,128]{2,1,0:T(2,128)} %ids_hbm.1) | copy-start | bytes 6148
  1.7 8.9 %collective-permute-start.4 = (f32[48,512]{1,0:T(8,128)S(1)}, f32[48,512]{1,0:T(8,128)S(1)}, u32[]{:S(2)}, u32[]{:S(2)}) collective-permute-start(f32[48,512]{1,0:T(8,128)S(1)} %get-tuple-element.100), channel_id=1, source_target_pairs={{0,8},{2,10},{4,12},{6,14},{8,0},{10,2},{12,4},{14,6},{1,9},{3,11}... | collective-permute-start | bytes 294920 | tf_op jit(solution)/shard_map/ppermute | solution.py:306
  5.8 1.6 %copy-start.8 = (s32[2,2]{1,0:T(2,128)S(1)}, s32[2,2]{1,0:T(2,128)}, u32[]{:S(2)}) copy-start(s32[2,2]{1,0:T(2,128)} %counts_hbm.1) | copy-start | bytes 52
  5.8 1.6 %copy-start.9 = (f32[32]{0:T(128)S(1)}, f32[32]{0:T(128)}, u32[]{:S(2)}) copy-start(f32[32]{0:T(128)} %param.13) | copy-start | bytes 388
  5.8 6.3 %collective-permute-start.2 = (f32[48,512]{1,0:T(8,128)S(1)}, f32[48,512]{1,0:T(8,128)S(1)}, u32[]{:S(2)}, u32[]{:S(2)}) collective-permute-start(f32[48,512]{1,0:T(8,128)S(1)} %get-tuple-element.56), channel_id=1, source_target_pairs={{0,4},{2,6},{4,0},{6,2},{8,12},{10,14},{12,8},{14,10},{1,5},{3,7},... | collective-permute-start | bytes 294920 | tf_op jit(solution)/shard_map/ppermute | solution.py:306
  7.6 9.1 %collective-permute-start = (f32[136,256]{1,0:T(8,128)S(1)}, f32[136,256]{1,0:T(8,128)S(1)}, u32[]{:S(2)}, u32[]{:S(2)}) collective-permute-start(f32[136,256]{1,0:T(8,128)S(1)} %get-tuple-element.54), channel_id=1, source_target_pairs={{0,8},{2,10},{4,12},{6,14},{8,0},{10,2},{12,4},{14,6},{1,9},{3,11}... | collective-permute-start | bytes 417800 | tf_op jit(solution)/shard_map/ppermute | solution.py:306
  10.6 7.8 %collective-permute-start.6 = (f32[48,512]{1,0:T(8,128)S(1)}, f32[48,512]{1,0:T(8,128)S(1)}, u32[]{:S(2)}, u32[]{:S(2)}) collective-permute-start(f32[48,512]{1,0:T(8,128)S(1)} %collective-permute-done.4), channel_id=1, source_target_pairs={{0,4},{2,6},{4,0},{6,2},{8,12},{10,14},{12,8},{14,10},{1,5},{3,7},... | collective-permute-start | bytes 294920 | tf_op jit(solution)/shard_map/ppermute | solution.py:306
  12.1 7.9 %collective-permute-start.3 = (f32[96,512]{1,0:T(8,128)S(1)}, f32[96,512]{1,0:T(8,128)S(1)}, u32[]{:S(2)}, u32[]{:S(2)}) collective-permute-start(f32[96,512]{1,0:T(8,128)S(1)} %pad_maximum_fusion.1), channel_id=1, source_target_pairs={{0,2},{2,0},{4,6},{6,4},{8,10},{10,8},{12,14},{14,12},{1,3},{3,1},... | collective-permute-start | bytes 589832 | tf_op jit(solution)/shard_map/ppermute | solution.py:306
  16.8 7.5 %collective-permute-start.1 = (f32[128,256]{1,0:T(8,128)S(1)}, f32[128,256]{1,0:T(8,128)S(1)}, u32[]{:S(2)}, u32[]{:S(2)}) collective-permute-start(f32[128,256]{1,0:T(8,128)S(1)} %slice.41.first_far), channel_id=1, source_target_pairs={{0,16},{16,0},{1,17},{17,1},{2,18},{18,2},{3,19},{19,3},{4,20},{20... | collective-permute-start | bytes 393224 | tf_op jit(solution)/shard_map/ppermute | solution.py:306
  18.4 5.8 %collective-permute-start.7 = (f32[96,512]{1,0:T(8,128)S(1)}, f32[96,512]{1,0:T(8,128)S(1)}, u32[]{:S(2)}, u32[]{:S(2)}) collective-permute-start(f32[96,512]{1,0:T(8,128)S(1)} %pad_maximum_fusion.2), channel_id=1, source_target_pairs={{0,2},{2,0},{4,6},{6,4},{8,10},{10,8},{12,14},{14,12},{1,3},{3,1},... | collective-permute-start | bytes 589832 | tf_op jit(solution)/shard_map/ppermute | solution.py:306
  20.1 4.3 %collective-permute-start.5 = (f32[192,512]{1,0:T(8,128)S(1)}, f32[192,512]{1,0:T(8,128)S(1)}, u32[]{:S(2)}, u32[]{:S(2)}) collective-permute-start(f32[192,512]{1,0:T(8,128)S(1)} %constant_dynamic-update-slice_fusion.own0), channel_id=1, source_target_pairs={{0,1},{1,0},{2,3},{3,2},{4,5},{5,4},{6,7},{7,6},{8,9},{9,8},{10,11... | collective-permute-start | bytes 1179656 | tf_op jit(solution)/shard_map/ppermute | solution.py:306
  24.3 1.8 %copy-start.4 = (f32[2,3,512]{2,0,1:T(2,128)S(1)}, f32[2,3,512]{2,0,1:T(2,128)}, u32[]{:S(2)}) copy-start(f32[2,3,512]{2,0,1:T(2,128)} %param.16) | copy-start | bytes 36868
  24.3 1.8 %collective-permute-start.8 = (f32[192,512]{1,0:T(8,128)S(1)}, f32[192,512]{1,0:T(8,128)S(1)}, u32[]{:S(2)}, u32[]{:S(2)}) collective-permute-start(f32[192,512]{1,0:T(8,128)S(1)} %pad_maximum_fusion.rec0), channel_id=1, source_target_pairs={{0,1},{1,0},{2,3},{3,2},{4,5},{5,4},{6,7},{7,6},{8,9},{9,8},{10,11... | collective-permute-start | bytes 1179656 | tf_op jit(solution)/shard_map/ppermute | solution.py:306
  27.4 4.6 %collective-permute-start.9 = (f32[8,128]{1,0:T(8,128)S(1)}, f32[8,128]{1,0:T(8,128)S(1)}, u32[]{:S(2)}, u32[]{:S(2)}) collective-permute-start(f32[8,128]{1,0:T(8,128)S(1)} %get-tuple-element.61.mine), channel_id=1, source_target_pairs={{0,8},{2,10},{4,12},{6,14},{8,0},{10,2},{12,4},{14,6},{1,9},{3,11}... | collective-permute-start | bytes 12296 | tf_op jit(solution)/shard_map/ppermute | solution.py:306
  33.2 2.9 %collective-permute-start.10 = (f32[392,512]{1,0:T(8,128)S(1)}, f32[392,512]{1,0:T(8,128)S(1)}, u32[]{:S(2)}, u32[]{:S(2)}) collective-permute-start(f32[392,512]{1,0:T(8,128)S(1)} %get-tuple-element.76), channel_id=1, source_target_pairs={{0,1},{1,0},{2,3},{3,2},{4,5},{5,4},{6,7},{7,6},{8,9},{9,8},{10,11... | collective-permute-start | bytes 2408456 | tf_op jit(solution)/shard_map/ppermute | solution.py:306
  33.3 15.4 %collective-permute-start.14 = (f32[2,128,256]{2,1,0:T(8,128)S(1)}, f32[2,128,256]{2,1,0:T(8,128)S(1)}, u32[]{:S(2)}, u32[]{:S(2)}) collective-permute-start(f32[2,128,256]{2,1,0:T(8,128)S(1)} %get-tuple-element.84), channel_id=1, source_target_pairs={{0,8},{2,10},{4,12},{6,14},{8,0},{10,2},{12,4},{14,6},{1,9},{3,11}... | collective-permute-start | bytes 786440 | tf_op jit(solution)/shard_map/ppermute | solution.py:306
  36.2 7.4 %collective-permute-start.11 = (f32[104,512]{1,0:T(8,128)S(1)}, f32[104,512]{1,0:T(8,128)S(1)}, u32[]{:S(2)}, u32[]{:S(2)}) collective-permute-start(f32[104,512]{1,0:T(8,128)S(1)} %get-tuple-element.79), channel_id=1, source_target_pairs={{0,2},{2,0},{4,6},{6,4},{8,10},{10,8},{12,14},{14,12},{1,3},{3,1},... | collective-permute-start | bytes 638984 | tf_op jit(solution)/shard_map/ppermute | solution.py:306
  43.6 7.5 %collective-permute-start.15 = (f32[56,512]{1,0:T(8,128)S(1)}, f32[56,512]{1,0:T(8,128)S(1)}, u32[]{:S(2)}, u32[]{:S(2)}) collective-permute-start(f32[56,512]{1,0:T(8,128)S(1)} %get-tuple-element.89), channel_id=1, source_target_pairs={{0,4},{2,6},{4,0},{6,2},{8,12},{10,14},{12,8},{14,10},{1,5},{3,7},... | collective-permute-start | bytes 344072 | tf_op jit(solution)/shard_map/ppermute | solution.py:306
  45.8 7.0 %collective-permute-start.12 = (f32[96,512]{1,0:T(8,128)S(1)}, f32[96,512]{1,0:T(8,128)S(1)}, u32[]{:S(2)}, u32[]{:S(2)}) collective-permute-start(f32[96,512]{1,0:T(8,128)S(1)} %get-tuple-element.80), channel_id=1, source_target_pairs={{0,2},{2,0},{4,6},{6,4},{8,10},{10,8},{12,14},{14,12},{1,3},{3,1},... | collective-permute-start | bytes 589832 | tf_op jit(solution)/shard_map/ppermute | solution.py:306
  48.7 1.2 %collective-permute-start.16 = (f32[8,128]{1,0:T(8,128)S(1)}, f32[8,128]{1,0:T(8,128)S(1)}, u32[]{:S(2)}, u32[]{:S(2)}) collective-permute-start(f32[8,128]{1,0:T(8,128)S(1)} %slice_bitcast_fusion), channel_id=1, source_target_pairs={{0,1},{1,0},{2,3},{3,2},{4,5},{5,4},{6,7},{7,6},{8,9},{9,8},{10,11... | collective-permute-start | bytes 12296 | tf_op jit(solution)/shard_map/ppermute | solution.py:306
  51.1 8.5 %collective-permute-start.17 = (f32[56,512]{1,0:T(8,128)S(1)}, f32[56,512]{1,0:T(8,128)S(1)}, u32[]{:S(2)}, u32[]{:S(2)}) collective-permute-start(f32[56,512]{1,0:T(8,128)S(1)} %far_z.1.beyond), channel_id=1, source_target_pairs={{0,8},{2,10},{4,12},{6,14},{8,0},{10,2},{12,4},{14,6},{1,9},{3,11}... | collective-permute-start | bytes 344072 | tf_op jit(solution)/shard_map/ppermute | solution.py:306
  52.8 5.7 %collective-permute-start.13 = (f32[48,512]{1,0:T(8,128)S(1)}, f32[48,512]{1,0:T(8,128)S(1)}, u32[]{:S(2)}, u32[]{:S(2)}) collective-permute-start(f32[48,512]{1,0:T(8,128)S(1)} %get-tuple-element.82), channel_id=1, source_target_pairs={{0,4},{2,6},{4,0},{6,2},{8,12},{10,14},{12,8},{14,10},{1,5},{3,7},... | collective-permute-start | bytes 294920 | tf_op jit(solution)/shard_map/ppermute | solution.py:306
  58.6 1.0 %copy-start.2 = (f32[2,8192]{1,0:T(2,128)S(1)}, f32[2,8192]{1,0:T(2,128)}, u32[]{:S(2)}) copy-start(f32[2,8192]{1,0:T(2,128)} %first.1) | copy-start | bytes 196612
  58.6 1.1 %copy-start.3 = (f32[2,16384]{1,0:T(2,128)S(1)}, f32[2,16384]{1,0:T(2,128)}, u32[]{:S(2)}) copy-start(f32[2,16384]{1,0:T(2,128)} %second_mom.1) | copy-start | bytes 393220
  58.6 1.1 %copy-start.5 = (f32[2,8192]{1,0:T(2,128)S(1)}, f32[2,8192]{1,0:T(2,128)}, u32[]{:S(2)}) copy-start(f32[2,8192]{1,0:T(2,128)} %first_mom.1) | copy-start | bytes 196612
  58.6 1.1 %copy-start.6 = (f32[2,3,512]{2,0,1:T(2,128)S(1)}, f32[2,3,512]{2,0,1:T(2,128)}, u32[]{:S(2)}) copy-start(f32[2,3,512]{2,0,1:T(2,128)} %param.19) | copy-start | bytes 36868

commit v6 on v5

--- a/solution.py
+++ b/solution.py
@@ -217,7 +217,9 @@
     out[...] = a[...] + b[...]
 
 
-def message_kernel(desc_hbm, counts_hbm, ids_hbm, refs_hbm, message, near, counts, ids, refs, sems):
+def message_kernel(
+    desc_hbm, counts_hbm, ids_hbm, refs_hbm, vec_hbm, message, near, vec, counts, ids, refs, sems,
+):
     spot, core, half, chain = place()
     atoms = message.shape[0] - 8
     loads = [
@@ -227,6 +229,7 @@
                 (counts_hbm, counts),
                 (ids_hbm, ids),
                 (refs_hbm, refs),
+                (vec_hbm, vec),
                 (desc_hbm.at[1 - half, chain], message.at[pl.ds(0, atoms)]),
             )
         )
@@ -329,18 +332,20 @@
 
     any_space = pl.BlockSpec(memory_space=pl.ANY)
     vmem = pl.BlockSpec(memory_space=VMEM)
-    message, meta = pl.pallas_call(
+    message, meta, vec = pl.pallas_call(
         message_kernel,
-        out_shape=[jax.ShapeDtypeStruct((atoms + 8, width), F32), jax.ShapeDtypeStruct((8, width), F32)],
-        in_specs=[pl.BlockSpec(memory_space=pltpu.HBM)] * 4,
-        out_specs=[vmem] * 2,
+        out_shape=[jax.ShapeDtypeStruct((atoms + 8, width), F32), jax.ShapeDtypeStruct((8, width), F32),
+            jax.ShapeDtypeStruct((3, nelem, hidden), F32),
+        ],
+        in_specs=[pl.BlockSpec(memory_space=pltpu.HBM)] * 5,
+        out_specs=[vmem] * 3,
         scratch_shapes=[
             pltpu.VMEM(counts.shape, jnp.int32), pltpu.VMEM(struct_ids.shape, jnp.int32), pltpu.VMEM((1, structs), F32),
-            pltpu.SemaphoreType.DMA((4,)),
+            pltpu.SemaphoreType.DMA((5,)),
         ],
         compiler_params=pltpu.CompilerParams(vmem_limit_bytes=4 * 1024 * 1024),
         name="message",
-    )(descriptors, counts, struct_ids, ref_energy.reshape(1, structs))
+    )(descriptors, counts, struct_ids, ref_energy.reshape(1, structs), vectors.transpose(1, 0, 2))
     message = to[4](message)
     own_z = to[2](own)
     own_x = to[1](jnp.concatenate([own, own_z]))
@@ -350,14 +355,15 @@
     far_meta = message[atoms:]
     shared = to_chain(direct)
     own_set = jnp.concatenate(lax.optimization_barrier((own, *own_came, got))[:4], axis=0)
-    own_across = to_core(own_set)
+    own_across = to_core(after(own_set, message))
     got_z = to[2](got)
     got_x = to[1](jnp.concatenate([got, got_z]))
     got_set = jnp.concatenate([got, got_x[:rows], got_z, got_x[rows:]], axis=0)
-    got_across = to_core(after(got_set, shared))
+    near_across = to_core(after(jnp.concatenate([got, got_z]), message))
+    last_across = to_core(after(got_x, shared))
+    got_across = jnp.concatenate([near_across[:rows], last_across[:rows], near_across[rows:], last_across[rows:]], axis=0)
 
     work = slots * atoms
-    vec = vectors.transpose(1, 0, 2)
     h1, h2, x, member, sums, *weights = call(
         forward_kernel,
         [((work, hidden),)] * 2 + [((work, width),), ((work, 128),), ((8, 128),)]
@@ -409,7 +415,7 @@
     )
     far_came = to[1](far_leave)
     far_stay, far_leave = halve(far_stay, far_came, tail, "far_x")
-    near_came = to[1](after(near_leave, far_came))
+    near_came = to[1](near_leave)
     far_came = to[2](far_leave)
     near_stay, near_leave = halve(near_stay, near_came, 0, "near_x")
     token = force_came[0, 0:8, 0:128]

time: 60.7 us -> 60.7 us (level)
  starting transfers between devices: 27.6 us -> 25.5 us
  waiting for transfers between devices: 24.9 us -> 26.3 us
    ppermute x18 -> x19, starting transfers between devices: 27.6 us -> 25.5 us  [flip(): lax.ppermute(x, axis, [(i, i ^ delta) for i in range(size)])]
    ppermute x18 -> x19, waiting for transfers between devices: 24.9 us -> 26.3 us  [flip(): lax.ppermute(x, axis, [(i, i ^ delta) for i in range(size)])]
    unnamed x24 -> x25, local copies, waits for them, and re-layouts: 1.08 us -> 1.65 us
  transfers between devices with their start and end apart: 18 -> 19, of which waited for: 11 -> 12; matrix products, arithmetic and copies ran while one was open for 0% -> 0% of each run, Pallas kernels for 4% -> 4%
where the time goes in v6:
time: 60.7 us; the launch traced here: 60.5 us
  waiting for transfers between devices  26.3 us (43%)
  starting transfers between devices  25.5 us (42%)
  Pallas kernels  5.76 us (9%)
  local copies, waits for them, and re-layouts  1.79 us (3%)
  between operations  0.93 us (2%)
    ppermute x19, waiting for transfers between devices, flip(): lax.ppermute(x, axis, [(i, i ^ delta) for i in range(size)])  26.3 us
    ppermute x19, starting transfers between devices, flip(): lax.ppermute(x, axis, [(i, i ^ delta) for i in range(size)])  25.5 us
    pallas_call x8, Pallas kernels, call(): pl.pallas_call(kernel, out_shape=[jax.ShapeDtypeStruct(shape, kind) for s...  3.87 us
    unnamed x25, local copies, waits for them, and re-layouts  1.65 us
  transfers between devices with their start and end apart: 19, of which 12 were waited for; matrix products, arithmetic and copies ran while one was open for 0% of the time, Pallas kernels for 4%

profile of v6, /device:TPU:0, one launch (start us, length us, event | category | flops | bytes accessed | tf_op | source)
XLA Modules:
  0.0 60.5 jit_solution(8151827109956918187)
XLA Ops:
  0.6 0.0 copy-start.1
  0.6 0.0 copy-start
  0.7 0.9 %bitcast_dynamic-update-slice_fusion.1 = f32[2,48,512]{2,1,0:T(8,128)S(1)} fusion(f32[1,2,16,512]{3,1,2,0:T(2,128)} %bitcast.22), kind=kLoop, calls=%fused_computation.6 | loop fusion | bytes 131072
  1.6 0.0 copy-done.1
  1.6 0.0 copy-start.5
  1.7 4.1 %collective-permute-start.4 = (f32[48,512]{1,0:T(8,128)S(1)}, f32[48,512]{1,0:T(8,128)S(1)}, u32[]{:S(2)}, u32[]{:S(2)}) collective-permute-start(f32[48,512]{1,0:T(8,128)S(1)} %get-tuple-element.108), channel_id=1, source_target_pairs={{0,8},{2,10},{4,12},{6,14},{8,0},{10,2},{12,4},{14,6},{1,9},{3,11}... | collective-permute-start | bytes 294920 | tf_op jit(solution)/shard_map/ppermute | solution.py:309
  5.8 0.0 copy-start.7
  5.8 1.6 %collective-permute-start.2 = (f32[48,512]{1,0:T(8,128)S(1)}, f32[48,512]{1,0:T(8,128)S(1)}, u32[]{:S(2)}, u32[]{:S(2)}) collective-permute-start(f32[48,512]{1,0:T(8,128)S(1)} %get-tuple-element.59), channel_id=1, source_target_pairs={{0,4},{2,6},{4,0},{6,2},{8,12},{10,14},{12,8},{14,10},{1,5},{3,7},... | collective-permute-start | bytes 294920 | tf_op jit(solution)/shard_map/ppermute | solution.py:309
  7.4 0.0 copy-start.8
  7.4 0.0 copy-start.9
  7.4 0.0 copy-done
  7.4 0.0 copy-done.5
  7.4 0.0 copy-done.7
  7.4 0.7 %copy-done.8 = s32[2,2]{1,0:T(2,128)S(1)} copy-done((s32[2,2]{1,0:T(2,128)S(1)}, s32[2,2]{1,0:T(2,128)}, u32[]{:S(2)}) %copy-start.8) | copy-done | bytes 40
  8.1 0.0 copy-done.9
  8.1 0.2 message.1
  8.3 0.4 collective-permute-start
  8.7 1.9 %collective-permute-done.4 = f32[48,512]{1,0:T(8,128)S(1)} collective-permute-done((f32[48,512]{1,0:T(8,128)S(1)}, f32[48,512]{1,0:T(8,128)S(1)}, u32[]{:S(2)}, u32[]{:S(2)}) %collective-permute-start.4) | collective-permute-done | bytes 98336 | tf_op jit(solution)/shard_map/ppermute | solution.py:309
  10.6 1.5 %collective-permute-start.6 = (f32[48,512]{1,0:T(8,128)S(1)}, f32[48,512]{1,0:T(8,128)S(1)}, u32[]{:S(2)}, u32[]{:S(2)}) collective-permute-start(f32[48,512]{1,0:T(8,128)S(1)} %collective-permute-done.4), channel_id=1, source_target_pairs={{0,4},{2,6},{4,0},{6,2},{8,12},{10,14},{12,8},{14,10},{1,5},{3,7},... | collective-permute-start | bytes 294920 | tf_op jit(solution)/shard_map/ppermute | solution.py:309
  12.1 0.0 collective-permute-done.2
  12.1 1.6 %collective-permute-start.3 = (f32[96,512]{1,0:T(8,128)S(1)}, f32[96,512]{1,0:T(8,128)S(1)}, u32[]{:S(2)}, u32[]{:S(2)}) collective-permute-start(f32[96,512]{1,0:T(8,128)S(1)} %pad_maximum_fusion.2), channel_id=1, source_target_pairs={{0,2},{2,0},{4,6},{6,4},{8,10},{10,8},{12,14},{14,12},{1,3},{3,1},... | collective-permute-start | bytes 589832 | tf_op jit(solution)/shard_map/ppermute | solution.py:309
  13.7 3.5 %collective-permute-done = f32[136,256]{1,0:T(8,128)S(1)} collective-permute-done((f32[136,256]{1,0:T(8,128)S(1)}, f32[136,256]{1,0:T(8,128)S(1)}, u32[]{:S(2)}, u32[]{:S(2)}) %collective-permute-start) | collective-permute-done | bytes 139296 | tf_op jit(solution)/shard_map/ppermute | solution.py:309
  17.2 1.6 %collective-permute-start.1 = (f32[128,256]{1,0:T(8,128)S(1)}, f32[128,256]{1,0:T(8,128)S(1)}, u32[]{:S(2)}, u32[]{:S(2)}) collective-permute-start(f32[128,256]{1,0:T(8,128)S(1)} %slice.57.first_far), channel_id=1, source_target_pairs={{0,16},{16,0},{1,17},{17,1},{2,18},{18,2},{3,19},{19,3},{4,20},{20... | collective-permute-start | bytes 393224 | tf_op jit(solution)/shard_map/ppermute | solution.py:309
  18.8 0.0 collective-permute-done.6
  18.8 1.6 %collective-permute-start.7 = (f32[96,512]{1,0:T(8,128)S(1)}, f32[96,512]{1,0:T(8,128)S(1)}, u32[]{:S(2)}, u32[]{:S(2)}) collective-permute-start(f32[96,512]{1,0:T(8,128)S(1)} %constant_dynamic-update-slice_fusion.4), channel_id=1, source_target_pairs={{0,2},{2,0},{4,6},{6,4},{8,10},{10,8},{12,14},{14,12},{1,3},{3,1},... | collective-permute-start | bytes 589832 | tf_op jit(solution)/shard_map/ppermute | solution.py:309
  20.4 0.0 collective-permute-start.8
  20.4 0.0 collective-permute-done.3
  20.5 0.6 collective-permute-start.5
  21.0 1.2 %collective-permute-done.1.second_far = f32[128,256]{1,0:T(8,128)S(1)} collective-permute-done((f32[128,256]{1,0:T(8,128)S(1)}, f32[128,256]{1,0:T(8,128)S(1)}, u32[]{:S(2)}, u32[]{:S(2)}) %collective-permute-start.1) | collective-permute-done | bytes 131104 | tf_op jit(solution)/shard_map/ppermute | solution.py:309
  22.2 2.5 %collective-permute-done.7 = f32[96,512]{1,0:T(8,128)S(1)} collective-permute-done((f32[96,512]{1,0:T(8,128)S(1)}, f32[96,512]{1,0:T(8,128)S(1)}, u32[]{:S(2)}, u32[]{:S(2)}) %collective-permute-start.7) | collective-permute-done | bytes 196640 | tf_op jit(solution)/shard_map/ppermute | solution.py:309
  24.7 0.0 collective-permute-start.9
  24.8 0.0 collective-permute-done.8
  24.8 1.4 %collective-permute-done.9 = f32[96,512]{1,0:T(8,128)S(1)} collective-permute-done((f32[96,512]{1,0:T(8,128)S(1)}, f32[96,512]{1,0:T(8,128)S(1)}, u32[]{:S(2)}, u32[]{:S(2)}) %collective-permute-start.9) | collective-permute-done | bytes 196640 | tf_op jit(solution)/shard_map/ppermute | solution.py:309
  26.2 0.0 collective-permute-done.5.own1
  26.3 1.3 %forward.1 = (f32[256,512]{1,0:T(8,128)S(1)}, f32[256,512]{1,0:T(8,128)S(1)}, f32[256,256]{1,0:T(8,128)S(1)}, f32[256,128]{1,0:T(8,128)S(1)}, f32[8,128]{1,0:T(8...) custom-call(f32[2,2,128,256]{3,2,1,0:T(8,128)S(1)} %copy-done, ...), custom_call_target="tpu_custom_call" | custom-call | flops 1 | bytes 1 | tf_op jit(solution)/shard_map/forward/pallas_call | solution.py:32
  27.5 2.3 %collective-permute-start.10 = (f32[8,128]{1,0:T(8,128)S(1)}, f32[8,128]{1,0:T(8,128)S(1)}, u32[]{:S(2)}, u32[]{:S(2)}) collective-permute-start(f32[8,128]{1,0:T(8,128)S(1)} %get-tuple-element.66.mine), channel_id=1, source_target_pairs={{0,8},{2,10},{4,12},{6,14},{8,0},{10,2},{12,4},{14,6},{1,9},{3,11}... | collective-permute-start | bytes 12296 | tf_op jit(solution)/shard_map/ppermute | solution.py:309
  29.8 0.1 bitcast_maximum_fusion.refs
  29.9 1.2 %backward.1 = (f32[256,512]{1,0:T(8,128)S(1)}, f32[256,512]{1,0:T(8,128)S(1)}, f32[256,256]{1,0:T(8,128)S(1)}) custom-call(f32[256,512]{1,0:T(8,128)S(1)} %get-tuple-element.68.h1_ref, f32[256,512]{1,0:T(8,128)S(1)} %get-tuple-element.69.h2_ref, f32[3,2,512]{2,1,0:T(2,128)S(1)} %get-tuple-element.57.vec_ref.vec, bf16[256,512]{1,0:T(8,128)(2,1)S(1)} %get-tuple-element.70.w1h, ...), custom_call_target="tpu_custom_call" | custom-call | flops 1 | bytes 1 | tf_op jit(solution)/shard_map/backward/pallas_call | solution.py:32
  31.1 1.0 %collective-permute-done.10.theirs = f32[8,128]{1,0:T(8,128)S(1)} collective-permute-done((f32[8,128]{1,0:T(8,128)S(1)}, f32[8,128]{1,0:T(8,128)S(1)}, u32[]{:S(2)}, u32[]{:S(2)}) %collective-permute-start.10) | collective-permute-done | bytes 4128 | tf_op jit(solution)/shard_map/ppermute | solution.py:309
  32.1 0.3 force.1
  32.4 1.0 %gradient.1 = (f32[392,512]{1,0:T(8,128)S(1)}, f32[392,512]{1,0:T(8,128)S(1)}) custom-call(f32[256,128]{1,0:T(8,128)S(1)} %get-tuple-element.75.adj_ref, f32[8,128]{1,0:T(8,128)S(1)} %get-tuple-element.76.pot_ref, f32[256,512]{1,0:T(8,128)S(1)} %get-tuple-element.68.h1_ref, f32[256,512]{1,0:T(8,128)S(1)} %get-tuple-element.69.h2_ref, ...), custom_call_target="tpu_custom_call" | custom-call | flops 1 | bytes 1 | tf_op jit(solution)/shard_map/gradient/pallas_call | solution.py:32
  33.4 0.1 collective-permute-start.11
  33.5 2.3 %collective-permute-start.14 = (f32[2,128,256]{2,1,0:T(8,128)S(1)}, f32[2,128,256]{2,1,0:T(8,128)S(1)}, u32[]{:S(2)}, u32[]{:S(2)}) collective-permute-start(f32[2,128,256]{2,1,0:T(8,128)S(1)} %get-tuple-element.87), channel_id=1, source_target_pairs={{0,8},{2,10},{4,12},{6,14},{8,0},{10,2},{12,4},{14,6},{1,9},{3,11}... | collective-permute-start | bytes 786440 | tf_op jit(solution)/shard_map/ppermute | solution.py:309
  35.7 0.0 collective-permute-done.11.came
  35.7 0.1 core_sum.1
  35.8 1.6 %collective-permute-start.15 = (f32[104,512]{1,0:T(8,128)S(1)}, f32[104,512]{1,0:T(8,128)S(1)}, u32[]{:S(2)}, u32[]{:S(2)}) collective-permute-start(f32[104,512]{1,0:T(8,128)S(1)} %get-tuple-element.91), channel_id=1, source_target_pairs={{0,2},{2,0},{4,6},{6,4},{8,10},{10,8},{12,14},{14,12},{1,3},{3,1},... | collective-permute-start | bytes 638984 | tf_op jit(solution)/shard_map/ppermute | solution.py:309
  37.4 0.5 collective-permute-start.12
  37.9 6.1 %collective-permute-done.15.came = f32[104,512]{1,0:T(8,128)S(1)} collective-permute-done((f32[104,512]{1,0:T(8,128)S(1)}, f32[104,512]{1,0:T(8,128)S(1)}, u32[]{:S(2)}, u32[]{:S(2)}) %collective-permute-start.15) | collective-permute-done | bytes 213024 | tf_op jit(solution)/shard_map/ppermute | solution.py:309
  44.0 2.2 %collective-permute-start.16 = (f32[56,512]{1,0:T(8,128)S(1)}, f32[56,512]{1,0:T(8,128)S(1)}, u32[]{:S(2)}, u32[]{:S(2)}) collective-permute-start(f32[56,512]{1,0:T(8,128)S(1)} %get-tuple-element.93), channel_id=1, source_target_pairs={{0,4},{2,6},{4,0},{6,2},{8,12},{10,14},{12,8},{14,10},{1,5},{3,7},... | collective-permute-start | bytes 344072 | tf_op jit(solution)/shard_map/ppermute | solution.py:309
  46.2 2.6 %collective-permute-done.14.force_came = f32[2,128,256]{2,1,0:T(8,128)S(1)} collective-permute-done((f32[2,128,256]{2,1,0:T(8,128)S(1)}, f32[2,128,256]{2,1,0:T(8,128)S(1)}, u32[]{:S(2)}, u32[]{:S(2)}) %collective-permute-start.14) | collective-permute-done | bytes 262176 | tf_op jit(solution)/shard_map/ppermute | solution.py:309
  48.8 0.0 collective-permute-start.17
  48.8 1.2 %collective-permute-done.17.rest_0_ = f32[8,128]{1,0:T(8,128)S(1)} collective-permute-done((f32[8,128]{1,0:T(8,128)S(1)}, f32[8,128]{1,0:T(8,128)S(1)}, u32[]{:S(2)}, u32[]{:S(2)}) %collective-permute-start.17) | collective-permute-done | bytes 4128 | tf_op jit(solution)/shard_map/ppermute | solution.py:309
  50.0 1.2 %collective-permute-done.16.b = f32[56,512]{1,0:T(8,128)S(1)} collective-permute-done((f32[56,512]{1,0:T(8,128)S(1)}, f32[56,512]{1,0:T(8,128)S(1)}, u32[]{:S(2)}, u32[]{:S(2)}) %collective-permute-start.16) | collective-permute-done | bytes 114720 | tf_op jit(solution)/shard_map/ppermute | solution.py:309
  51.2 1.3 %collective-permute-start.18 = (f32[56,512]{1,0:T(8,128)S(1)}, f32[56,512]{1,0:T(8,128)S(1)}, u32[]{:S(2)}, u32[]{:S(2)}) collective-permute-start(f32[56,512]{1,0:T(8,128)S(1)} %far_z.1.beyond), channel_id=1, source_target_pairs={{0,8},{2,10},{4,12},{6,14},{8,0},{10,2},{12,4},{14,6},{1,9},{3,11}... | collective-permute-start | bytes 344072 | tf_op jit(solution)/shard_map/ppermute | solution.py:309
  52.4 0.0 collective-permute-done.12.came
  52.5 2.5 %collective-permute-start.13 = (f32[48,512]{1,0:T(8,128)S(1)}, f32[48,512]{1,0:T(8,128)S(1)}, u32[]{:S(2)}, u32[]{:S(2)}) collective-permute-start(f32[48,512]{1,0:T(8,128)S(1)} %get-tuple-element.85), channel_id=1, source_target_pairs={{0,4},{2,6},{4,0},{6,2},{8,12},{10,14},{12,8},{14,10},{1,5},{3,7},... | collective-permute-start | bytes 294920 | tf_op jit(solution)/shard_map/ppermute | solution.py:309
  55.0 3.2 %collective-permute-done.13.b = f32[48,512]{1,0:T(8,128)S(1)} collective-permute-done((f32[48,512]{1,0:T(8,128)S(1)}, f32[48,512]{1,0:T(8,128)S(1)}, u32[]{:S(2)}, u32[]{:S(2)}) %collective-permute-start.13) | collective-permute-done | bytes 98336 | tf_op jit(solution)/shard_map/ppermute | solution.py:309
  58.2 0.8 %near_z.1 = (f32[1,8192]{1,0:T(1,128)S(1)}, f32[1,16384]{1,0:T(1,128)S(1)}, f32[2,2,128,256]{3,2,1,0:T(8,128)}) custom-call(f32[48,512]{1,0:T(8,128)S(1)} %get-tuple-element.84.a, f32[48,512]{1,0:T(8,128)S(1)} %collective-permute-done.13.b, f32[2,128,256]{2,1,0:T(8,128)S(1)} %get-tuple-element.86.force_near, ...), custom_call_target="tpu_custom_call" | custom-call | flops 1 | bytes 1 | tf_op jit(solution)/shard_map/near_z/pallas_call | solution.py:428
  59.0 0.6 %collective-permute-done.18.came = f32[56,512]{1,0:T(8,128)S(1)} collective-permute-done((f32[56,512]{1,0:T(8,128)S(1)}, f32[56,512]{1,0:T(8,128)S(1)}, u32[]{:S(2)}, u32[]{:S(2)}) %collective-permute-start.18) | collective-permute-done | bytes 114720 | tf_op jit(solution)/shard_map/ppermute | solution.py:309
  59.7 0.0 copy-done.2
  59.7 0.0 copy-done.3
  59.7 0.0 copy-done.4
  59.7 0.0 copy-done.6
  59.7 0.8 %final.1 = (f32[2,8192]{1,0:T(2,128)}, f32[2,16384]{1,0:T(2,128)}, f32[3,2,512]{2,1,0:T(2,128)}, f32[2,8192]{1,0:T(2,128)}, f32[2,16384]{1,0:T(2,128)}, /*index=5*/f32[3,2,512]{2,1,0:T(2,128)}, f32[1,128]{1,0:T(1,128)}) custom-call(f32[1,8192]{1,0:T(1,128)S(1)} %get-tuple-element.88.mine_first, f32[1,16384]{1,0:T(1,128)S(1)} %get-tuple-element.89.mine_second, ...), custom_call_target="tpu_custom_call" | custom-call | flops 1 | bytes 1 | tf_op jit(solution)/shard_map/final/pallas_call | solution.py:443
  (28 shorter events, 0.3 us)
Async XLA Ops:
  0.6 1.0 %copy-start.1 = (f32[2,16384]{1,0:T(2,128)S(1)}, f32[2,16384]{1,0:T(2,128)}, u32[]{:S(2)}) copy-start(f32[2,16384]{1,0:T(2,128)} %second.1) | copy-start | bytes 393220
  0.6 6.7 %copy-start = (f32[2,2,128,256]{3,2,1,0:T(8,128)S(1)}, f32[2,2,128,256]{3,2,1,0:T(8,128)}, u32[]{:S(2)}) copy-start(f32[2,2,128,256]{3,2,1,0:T(8,128)} %desc_ref.1) | copy-start | bytes 1572868
  1.6 5.7 %copy-start.5 = (f32[2,3,512]{2,0,1:T(2,128)S(1)}, f32[2,3,512]{2,0,1:T(2,128)}, u32[]{:S(2)}) copy-start(f32[2,3,512]{2,0,1:T(2,128)} %param.16) | copy-start | bytes 36868
  1.7 8.9 %collective-permute-start.4 = (f32[48,512]{1,0:T(8,128)S(1)}, f32[48,512]{1,0:T(8,128)S(1)}, u32[]{:S(2)}, u32[]{:S(2)}) collective-permute-start(f32[48,512]{1,0:T(8,128)S(1)} %get-tuple-element.108), channel_id=1, source_target_pairs={{0,8},{2,10},{4,12},{6,14},{8,0},{10,2},{12,4},{14,6},{1,9},{3,11}... | collective-permute-start | bytes 294920 | tf_op jit(solution)/shard_map/ppermute | solution.py:309
  5.8 1.6 %copy-start.7 = (s32[2,2,128]{2,1,0:T(2,128)S(1)}, s32[2,2,128]{2,1,0:T(2,128)}, u32[]{:S(2)}) copy-start(s32[2,2,128]{2,1,0:T(2,128)} %ids_hbm.1) | copy-start | bytes 6148
  5.8 6.3 %collective-permute-start.2 = (f32[48,512]{1,0:T(8,128)S(1)}, f32[48,512]{1,0:T(8,128)S(1)}, u32[]{:S(2)}, u32[]{:S(2)}) collective-permute-start(f32[48,512]{1,0:T(8,128)S(1)} %get-tuple-element.59), channel_id=1, source_target_pairs={{0,4},{2,6},{4,0},{6,2},{8,12},{10,14},{12,8},{14,10},{1,5},{3,7},... | collective-permute-start | bytes 294920 | tf_op jit(solution)/shard_map/ppermute | solution.py:309
  7.4 0.7 %copy-start.8 = (s32[2,2]{1,0:T(2,128)S(1)}, s32[2,2]{1,0:T(2,128)}, u32[]{:S(2)}) copy-start(s32[2,2]{1,0:T(2,128)} %counts_hbm.1) | copy-start | bytes 52
  7.4 0.7 %copy-start.9 = (f32[32]{0:T(128)S(1)}, f32[32]{0:T(128)}, u32[]{:S(2)}) copy-start(f32[32]{0:T(128)} %param.13) | copy-start | bytes 388
  8.3 8.9 %collective-permute-start = (f32[136,256]{1,0:T(8,128)S(1)}, f32[136,256]{1,0:T(8,128)S(1)}, u32[]{:S(2)}, u32[]{:S(2)}) collective-permute-start(f32[136,256]{1,0:T(8,128)S(1)} %get-tuple-element.56), channel_id=1, source_target_pairs={{0,8},{2,10},{4,12},{6,14},{8,0},{10,2},{12,4},{14,6},{1,9},{3,11}... | collective-permute-start | bytes 417800 | tf_op jit(solution)/shard_map/ppermute | solution.py:309
  10.6 8.2 %collective-permute-start.6 = (f32[48,512]{1,0:T(8,128)S(1)}, f32[48,512]{1,0:T(8,128)S(1)}, u32[]{:S(2)}, u32[]{:S(2)}) collective-permute-start(f32[48,512]{1,0:T(8,128)S(1)} %collective-permute-done.4), channel_id=1, source_target_pairs={{0,4},{2,6},{4,0},{6,2},{8,12},{10,14},{12,8},{14,10},{1,5},{3,7},... | collective-permute-start | bytes 294920 | tf_op jit(solution)/shard_map/ppermute | solution.py:309
  12.1 8.3 %collective-permute-start.3 = (f32[96,512]{1,0:T(8,128)S(1)}, f32[96,512]{1,0:T(8,128)S(1)}, u32[]{:S(2)}, u32[]{:S(2)}) collective-permute-start(f32[96,512]{1,0:T(8,128)S(1)} %pad_maximum_fusion.2), channel_id=1, source_target_pairs={{0,2},{2,0},{4,6},{6,4},{8,10},{10,8},{12,14},{14,12},{1,3},{3,1},... | collective-permute-start | bytes 589832 | tf_op jit(solution)/shard_map/ppermute | solution.py:309
  17.2 5.0 %collective-permute-start.1 = (f32[128,256]{1,0:T(8,128)S(1)}, f32[128,256]{1,0:T(8,128)S(1)}, u32[]{:S(2)}, u32[]{:S(2)}) collective-permute-start(f32[128,256]{1,0:T(8,128)S(1)} %slice.57.first_far), channel_id=1, source_target_pairs={{0,16},{16,0},{1,17},{17,1},{2,18},{18,2},{3,19},{19,3},{4,20},{20... | collective-permute-start | bytes 393224 | tf_op jit(solution)/shard_map/ppermute | solution.py:309
  18.8 5.9 %collective-permute-start.7 = (f32[96,512]{1,0:T(8,128)S(1)}, f32[96,512]{1,0:T(8,128)S(1)}, u32[]{:S(2)}, u32[]{:S(2)}) collective-permute-start(f32[96,512]{1,0:T(8,128)S(1)} %constant_dynamic-update-slice_fusion.4), channel_id=1, source_target_pairs={{0,2},{2,0},{4,6},{6,4},{8,10},{10,8},{12,14},{14,12},{1,3},{3,1},... | collective-permute-start | bytes 589832 | tf_op jit(solution)/shard_map/ppermute | solution.py:309
  20.4 4.4 %collective-permute-start.8 = (f32[96,512]{1,0:T(8,128)S(1)}, f32[96,512]{1,0:T(8,128)S(1)}, u32[]{:S(2)}, u32[]{:S(2)}) collective-permute-start(f32[96,512]{1,0:T(8,128)S(1)} %constant_dynamic-update-slice_fusion.4), channel_id=1, source_target_pairs={{0,1},{1,0},{2,3},{3,2},{4,5},{5,4},{6,7},{7,6},{8,9},{9,8},{10,11... | collective-permute-start | bytes 589832 | tf_op jit(solution)/shard_map/ppermute | solution.py:309
  20.5 5.8 %collective-permute-start.5 = (f32[192,512]{1,0:T(8,128)S(1)}, f32[192,512]{1,0:T(8,128)S(1)}, u32[]{:S(2)}, u32[]{:S(2)}) collective-permute-start(f32[192,512]{1,0:T(8,128)S(1)} %constant_dynamic-update-slice_fusion.own0), channel_id=1, source_target_pairs={{0,1},{1,0},{2,3},{3,2},{4,5},{5,4},{6,7},{7,6},{8,9},{9,8},{10,11... | collective-permute-start | bytes 1179656 | tf_op jit(solution)/shard_map/ppermute | solution.py:309
  24.7 1.4 %collective-permute-start.9 = (f32[96,512]{1,0:T(8,128)S(1)}, f32[96,512]{1,0:T(8,128)S(1)}, u32[]{:S(2)}, u32[]{:S(2)}) collective-permute-start(f32[96,512]{1,0:T(8,128)S(1)} %collective-permute-done.7), channel_id=1, source_target_pairs={{0,1},{1,0},{2,3},{3,2},{4,5},{5,4},{6,7},{7,6},{8,9},{9,8},{10,11... | collective-permute-start | bytes 589832 | tf_op jit(solution)/shard_map/ppermute | solution.py:309
  27.5 4.6 %collective-permute-start.10 = (f32[8,128]{1,0:T(8,128)S(1)}, f32[8,128]{1,0:T(8,128)S(1)}, u32[]{:S(2)}, u32[]{:S(2)}) collective-permute-start(f32[8,128]{1,0:T(8,128)S(1)} %get-tuple-element.66.mine), channel_id=1, source_target_pairs={{0,8},{2,10},{4,12},{6,14},{8,0},{10,2},{12,4},{14,6},{1,9},{3,11}... | collective-permute-start | bytes 12296 | tf_op jit(solution)/shard_map/ppermute | solution.py:309
  33.4 2.4 %collective-permute-start.11 = (f32[392,512]{1,0:T(8,128)S(1)}, f32[392,512]{1,0:T(8,128)S(1)}, u32[]{:S(2)}, u32[]{:S(2)}) collective-permute-start(f32[392,512]{1,0:T(8,128)S(1)} %get-tuple-element.81), channel_id=1, source_target_pairs={{0,1},{1,0},{2,3},{3,2},{4,5},{5,4},{6,7},{7,6},{8,9},{9,8},{10,11... | collective-permute-start | bytes 2408456 | tf_op jit(solution)/shard_map/ppermute | solution.py:309
  33.5 15.3 %collective-permute-start.14 = (f32[2,128,256]{2,1,0:T(8,128)S(1)}, f32[2,128,256]{2,1,0:T(8,128)S(1)}, u32[]{:S(2)}, u32[]{:S(2)}) collective-permute-start(f32[2,128,256]{2,1,0:T(8,128)S(1)} %get-tuple-element.87), channel_id=1, source_target_pairs={{0,8},{2,10},{4,12},{6,14},{8,0},{10,2},{12,4},{14,6},{1,9},{3,11}... | collective-permute-start | bytes 786440 | tf_op jit(solution)/shard_map/ppermute | solution.py:309
  35.8 8.2 %collective-permute-start.15 = (f32[104,512]{1,0:T(8,128)S(1)}, f32[104,512]{1,0:T(8,128)S(1)}, u32[]{:S(2)}, u32[]{:S(2)}) collective-permute-start(f32[104,512]{1,0:T(8,128)S(1)} %get-tuple-element.91), channel_id=1, source_target_pairs={{0,2},{2,0},{4,6},{6,4},{8,10},{10,8},{12,14},{14,12},{1,3},{3,1},... | collective-permute-start | bytes 638984 | tf_op jit(solution)/shard_map/ppermute | solution.py:309
  37.4 15.0 %collective-permute-start.12 = (f32[96,512]{1,0:T(8,128)S(1)}, f32[96,512]{1,0:T(8,128)S(1)}, u32[]{:S(2)}, u32[]{:S(2)}) collective-permute-start(f32[96,512]{1,0:T(8,128)S(1)} %get-tuple-element.83), channel_id=1, source_target_pairs={{0,2},{2,0},{4,6},{6,4},{8,10},{10,8},{12,14},{14,12},{1,3},{3,1},... | collective-permute-start | bytes 589832 | tf_op jit(solution)/shard_map/ppermute | solution.py:309
  44.0 7.1 %collective-permute-start.16 = (f32[56,512]{1,0:T(8,128)S(1)}, f32[56,512]{1,0:T(8,128)S(1)}, u32[]{:S(2)}, u32[]{:S(2)}) collective-permute-start(f32[56,512]{1,0:T(8,128)S(1)} %get-tuple-element.93), channel_id=1, source_target_pairs={{0,4},{2,6},{4,0},{6,2},{8,12},{10,14},{12,8},{14,10},{1,5},{3,7},... | collective-permute-start | bytes 344072 | tf_op jit(solution)/shard_map/ppermute | solution.py:309
  48.8 1.2 %collective-permute-start.17 = (f32[8,128]{1,0:T(8,128)S(1)}, f32[8,128]{1,0:T(8,128)S(1)}, u32[]{:S(2)}, u32[]{:S(2)}) collective-permute-start(f32[8,128]{1,0:T(8,128)S(1)} %slice_bitcast_fusion), channel_id=1, source_target_pairs={{0,1},{1,0},{2,3},{3,2},{4,5},{5,4},{6,7},{7,6},{8,9},{9,8},{10,11... | collective-permute-start | bytes 12296 | tf_op jit(solution)/shard_map/ppermute | solution.py:309
  51.2 8.5 %collective-permute-start.18 = (f32[56,512]{1,0:T(8,128)S(1)}, f32[56,512]{1,0:T(8,128)S(1)}, u32[]{:S(2)}, u32[]{:S(2)}) collective-permute-start(f32[56,512]{1,0:T(8,128)S(1)} %far_z.1.beyond), channel_id=1, source_target_pairs={{0,8},{2,10},{4,12},{6,14},{8,0},{10,2},{12,4},{14,6},{1,9},{3,11}... | collective-permute-start | bytes 344072 | tf_op jit(solution)/shard_map/ppermute | solution.py:309
  52.5 5.7 %collective-permute-start.13 = (f32[48,512]{1,0:T(8,128)S(1)}, f32[48,512]{1,0:T(8,128)S(1)}, u32[]{:S(2)}, u32[]{:S(2)}) collective-permute-start(f32[48,512]{1,0:T(8,128)S(1)} %get-tuple-element.85), channel_id=1, source_target_pairs={{0,4},{2,6},{4,0},{6,2},{8,12},{10,14},{12,8},{14,10},{1,5},{3,7},... | collective-permute-start | bytes 294920 | tf_op jit(solution)/shard_map/ppermute | solution.py:309
  58.2 1.5 %copy-start.2 = (f32[2,8192]{1,0:T(2,128)S(1)}, f32[2,8192]{1,0:T(2,128)}, u32[]{:S(2)}) copy-start(f32[2,8192]{1,0:T(2,128)} %first.1) | copy-start | bytes 196612
  58.2 1.5 %copy-start.3 = (f32[2,16384]{1,0:T(2,128)S(1)}, f32[2,16384]{1,0:T(2,128)}, u32[]{:S(2)}) copy-start(f32[2,16384]{1,0:T(2,128)} %second_mom.1) | copy-start | bytes 393220
  58.2 1.5 %copy-start.4 = (f32[2,8192]{1,0:T(2,128)S(1)}, f32[2,8192]{1,0:T(2,128)}, u32[]{:S(2)}) copy-start(f32[2,8192]{1,0:T(2,128)} %first_mom.1) | copy-start | bytes 196612
  58.2 1.5 %copy-start.6 = (f32[2,3,512]{2,0,1:T(2,128)S(1)}, f32[2,3,512]{2,0,1:T(2,128)}, u32[]{:S(2)}) copy-start(f32[2,3,512]{2,0,1:T(2,128)} %param.19) | copy-start | bytes 36868

commit v7 on v6

--- a/solution.py
+++ b/solution.py
@@ -347,7 +347,7 @@
         name="message",
     )(descriptors, counts, struct_ids, ref_energy.reshape(1, structs), vectors.transpose(1, 0, 2))
     message = to[4](message)
-    own_z = to[2](own)
+    own_z = to[2](after(own, meta))
     own_x = to[1](jnp.concatenate([own, own_z]))
     own_came = [own_x[:rows], own_z, own_x[rows:]]
     got = after(got, own)

time: 60.7 us -> 60.7 us (level)
  starting transfers between devices: 25.5 us -> 27.8 us
  waiting for transfers between devices: 26.3 us -> 24 us
    ppermute x19, waiting for transfers between devices: 26.3 us -> 24 us  [flip(): lax.ppermute(x, axis, [(i, i ^ delta) for i in range(size)])]
    ppermute x19, starting transfers between devices: 25.5 us -> 27.8 us  [flip(): lax.ppermute(x, axis, [(i, i ^ delta) for i in range(size)])]
where the time goes in v7:
time: 60.7 us; the launch traced here: 60.5 us
  starting transfers between devices  27.8 us (46%)
  waiting for transfers between devices  24 us (40%)
  Pallas kernels  5.75 us (9%)
  local copies, waits for them, and re-layouts  1.89 us (3%)
  between operations  0.93 us (2%)
    ppermute x19, starting transfers between devices, flip(): lax.ppermute(x, axis, [(i, i ^ delta) for i in range(size)])  27.8 us
    ppermute x19, waiting for transfers between devices, flip(): lax.ppermute(x, axis, [(i, i ^ delta) for i in range(size)])  24 us
    pallas_call x8, Pallas kernels, call(): pl.pallas_call(kernel, out_shape=[jax.ShapeDtypeStruct(shape, kind) for s...  3.87 us
    unnamed x25, local copies, waits for them, and re-layouts  1.74 us
  transfers between devices with their start and end apart: 19, of which 12 were waited for; matrix products, arithmetic and copies ran while one was open for 0% of the time, Pallas kernels for 4%

profile of v7, /device:TPU:0, one launch (start us, length us, event | category | flops | bytes accessed | tf_op | source)
XLA Modules:
  0.0 60.5 jit_solution(16566484318630198676)
XLA Ops:
  0.6 0.0 copy-start.1
  0.6 0.0 copy-start
  0.7 0.9 %bitcast_dynamic-update-slice_fusion.1 = f32[2,48,512]{2,1,0:T(8,128)S(1)} fusion(f32[1,2,16,512]{3,1,2,0:T(2,128)} %bitcast.22), kind=kLoop, calls=%fused_computation.6 | loop fusion | bytes 131072
  1.6 0.0 copy-done.1
  1.6 0.0 copy-start.5
  1.7 0.0 copy-start.7
  1.7 4.1 %collective-permute-start.4 = (f32[48,512]{1,0:T(8,128)S(1)}, f32[48,512]{1,0:T(8,128)S(1)}, u32[]{:S(2)}, u32[]{:S(2)}) collective-permute-start(f32[48,512]{1,0:T(8,128)S(1)} %get-tuple-element.110), channel_id=1, source_target_pairs={{0,8},{2,10},{4,12},{6,14},{8,0},{10,2},{12,4},{14,6},{1,9},{3,11}... | collective-permute-start | bytes 294920 | tf_op jit(solution)/shard_map/ppermute | solution.py:309
  5.8 0.0 copy-start.8
  5.8 0.0 copy-start.9
  5.8 0.0 copy-done
  5.8 0.0 copy-done.5
  5.8 0.0 copy-done.7
  5.8 0.7 %copy-done.8 = s32[2,2]{1,0:T(2,128)S(1)} copy-done((s32[2,2]{1,0:T(2,128)S(1)}, s32[2,2]{1,0:T(2,128)}, u32[]{:S(2)}) %copy-start.8) | copy-done | bytes 40
  6.5 0.0 copy-done.9
  6.5 0.2 message.1
  6.7 1.6 %collective-permute-start.2 = (f32[48,512]{1,0:T(8,128)S(1)}, f32[48,512]{1,0:T(8,128)S(1)}, u32[]{:S(2)}, u32[]{:S(2)}) collective-permute-start(f32[48,512]{1,0:T(8,128)S(1)} %get-tuple-element.61), channel_id=1, source_target_pairs={{0,4},{2,6},{4,0},{6,2},{8,12},{10,14},{12,8},{14,10},{1,5},{3,7},... | collective-permute-start | bytes 294920 | tf_op jit(solution)/shard_map/ppermute | solution.py:309
  8.4 0.3 collective-permute-start
  8.7 1.9 %collective-permute-done.4 = f32[48,512]{1,0:T(8,128)S(1)} collective-permute-done((f32[48,512]{1,0:T(8,128)S(1)}, f32[48,512]{1,0:T(8,128)S(1)}, u32[]{:S(2)}, u32[]{:S(2)}) %collective-permute-start.4) | collective-permute-done | bytes 98336 | tf_op jit(solution)/shard_map/ppermute | solution.py:309
  10.6 2.0 %collective-permute-start.6 = (f32[48,512]{1,0:T(8,128)S(1)}, f32[48,512]{1,0:T(8,128)S(1)}, u32[]{:S(2)}, u32[]{:S(2)}) collective-permute-start(f32[48,512]{1,0:T(8,128)S(1)} %collective-permute-done.4), channel_id=1, source_target_pairs={{0,4},{2,6},{4,0},{6,2},{8,12},{10,14},{12,8},{14,10},{1,5},{3,7},... | collective-permute-start | bytes 294920 | tf_op jit(solution)/shard_map/ppermute | solution.py:309
  12.7 0.0 collective-permute-done.2
  12.7 1.6 %collective-permute-start.3 = (f32[96,512]{1,0:T(8,128)S(1)}, f32[96,512]{1,0:T(8,128)S(1)}, u32[]{:S(2)}, u32[]{:S(2)}) collective-permute-start(f32[96,512]{1,0:T(8,128)S(1)} %pad_maximum_fusion.2), channel_id=1, source_target_pairs={{0,2},{2,0},{4,6},{6,4},{8,10},{10,8},{12,14},{14,12},{1,3},{3,1},... | collective-permute-start | bytes 589832 | tf_op jit(solution)/shard_map/ppermute | solution.py:309
  14.3 2.9 %collective-permute-done = f32[136,256]{1,0:T(8,128)S(1)} collective-permute-done((f32[136,256]{1,0:T(8,128)S(1)}, f32[136,256]{1,0:T(8,128)S(1)}, u32[]{:S(2)}, u32[]{:S(2)}) %collective-permute-start) | collective-permute-done | bytes 139296 | tf_op jit(solution)/shard_map/ppermute | solution.py:309
  17.2 1.6 %collective-permute-start.1 = (f32[128,256]{1,0:T(8,128)S(1)}, f32[128,256]{1,0:T(8,128)S(1)}, u32[]{:S(2)}, u32[]{:S(2)}) collective-permute-start(f32[128,256]{1,0:T(8,128)S(1)} %slice.57.first_far), channel_id=1, source_target_pairs={{0,16},{16,0},{1,17},{17,1},{2,18},{18,2},{3,19},{19,3},{4,20},{20... | collective-permute-start | bytes 393224 | tf_op jit(solution)/shard_map/ppermute | solution.py:309
  18.8 0.0 collective-permute-done.6
  18.8 1.6 %collective-permute-start.7 = (f32[96,512]{1,0:T(8,128)S(1)}, f32[96,512]{1,0:T(8,128)S(1)}, u32[]{:S(2)}, u32[]{:S(2)}) collective-permute-start(f32[96,512]{1,0:T(8,128)S(1)} %constant_dynamic-update-slice_fusion.4), channel_id=1, source_target_pairs={{0,2},{2,0},{4,6},{6,4},{8,10},{10,8},{12,14},{14,12},{1,3},{3,1},... | collective-permute-start | bytes 589832 | tf_op jit(solution)/shard_map/ppermute | solution.py:309
  20.4 0.0 collective-permute-start.8
  20.4 0.0 collective-permute-done.3
  20.5 0.6 collective-permute-start.5
  21.0 1.2 %collective-permute-done.1.second_far = f32[128,256]{1,0:T(8,128)S(1)} collective-permute-done((f32[128,256]{1,0:T(8,128)S(1)}, f32[128,256]{1,0:T(8,128)S(1)}, u32[]{:S(2)}, u32[]{:S(2)}) %collective-permute-start.1) | collective-permute-done | bytes 131104 | tf_op jit(solution)/shard_map/ppermute | solution.py:309
  22.2 2.4 %collective-permute-done.7 = f32[96,512]{1,0:T(8,128)S(1)} collective-permute-done((f32[96,512]{1,0:T(8,128)S(1)}, f32[96,512]{1,0:T(8,128)S(1)}, u32[]{:S(2)}, u32[]{:S(2)}) %collective-permute-start.7) | collective-permute-done | bytes 196640 | tf_op jit(solution)/shard_map/ppermute | solution.py:309
  24.7 0.0 collective-permute-start.9
  24.7 0.0 collective-permute-done.8
  24.8 1.4 %collective-permute-done.9 = f32[96,512]{1,0:T(8,128)S(1)} collective-permute-done((f32[96,512]{1,0:T(8,128)S(1)}, f32[96,512]{1,0:T(8,128)S(1)}, u32[]{:S(2)}, u32[]{:S(2)}) %collective-permute-start.9) | collective-permute-done | bytes 196640 | tf_op jit(solution)/shard_map/ppermute | solution.py:309
  26.2 0.0 collective-permute-done.5.own1
  26.2 1.3 %forward.1 = (f32[256,512]{1,0:T(8,128)S(1)}, f32[256,512]{1,0:T(8,128)S(1)}, f32[256,256]{1,0:T(8,128)S(1)}, f32[256,128]{1,0:T(8,128)S(1)}, f32[8,128]{1,0:T(8...) custom-call(f32[2,2,128,256]{3,2,1,0:T(8,128)S(1)} %copy-done, ...), custom_call_target="tpu_custom_call" | custom-call | flops 1 | bytes 1 | tf_op jit(solution)/shard_map/forward/pallas_call | solution.py:32
  27.4 2.7 %collective-permute-start.10 = (f32[8,128]{1,0:T(8,128)S(1)}, f32[8,128]{1,0:T(8,128)S(1)}, u32[]{:S(2)}, u32[]{:S(2)}) collective-permute-start(f32[8,128]{1,0:T(8,128)S(1)} %get-tuple-element.68.mine), channel_id=1, source_target_pairs={{0,8},{2,10},{4,12},{6,14},{8,0},{10,2},{12,4},{14,6},{1,9},{3,11}... | collective-permute-start | bytes 12296 | tf_op jit(solution)/shard_map/ppermute | solution.py:309
  30.2 0.1 bitcast_maximum_fusion.refs
  30.2 1.2 %backward.1 = (f32[256,512]{1,0:T(8,128)S(1)}, f32[256,512]{1,0:T(8,128)S(1)}, f32[256,256]{1,0:T(8,128)S(1)}) custom-call(f32[256,512]{1,0:T(8,128)S(1)} %get-tuple-element.70.h1_ref, f32[256,512]{1,0:T(8,128)S(1)} %get-tuple-element.71.h2_ref, f32[3,2,512]{2,1,0:T(2,128)S(1)} %get-tuple-element.58.vec_ref.vec, bf16[256,512]{1,0:T(8,128)(2,1)S(1)} %get-tuple-element.72.w1h, ...), custom_call_target="tpu_custom_call" | custom-call | flops 1 | bytes 1 | tf_op jit(solution)/shard_map/backward/pallas_call | solution.py:32
  31.4 0.6 collective-permute-done.10.theirs
  32.0 0.3 force.1
  32.3 1.0 %gradient.1 = (f32[392,512]{1,0:T(8,128)S(1)}, f32[392,512]{1,0:T(8,128)S(1)}) custom-call(f32[256,128]{1,0:T(8,128)S(1)} %get-tuple-element.77.adj_ref, f32[8,128]{1,0:T(8,128)S(1)} %get-tuple-element.78.pot_ref, f32[256,512]{1,0:T(8,128)S(1)} %get-tuple-element.70.h1_ref, f32[256,512]{1,0:T(8,128)S(1)} %get-tuple-element.71.h2_ref, ...), custom_call_target="tpu_custom_call" | custom-call | flops 1 | bytes 1 | tf_op jit(solution)/shard_map/gradient/pallas_call | solution.py:32
  33.3 0.1 collective-permute-start.11
  33.4 2.7 %collective-permute-start.14 = (f32[2,128,256]{2,1,0:T(8,128)S(1)}, f32[2,128,256]{2,1,0:T(8,128)S(1)}, u32[]{:S(2)}, u32[]{:S(2)}) collective-permute-start(f32[2,128,256]{2,1,0:T(8,128)S(1)} %get-tuple-element.89), channel_id=1, source_target_pairs={{0,8},{2,10},{4,12},{6,14},{8,0},{10,2},{12,4},{14,6},{1,9},{3,11}... | collective-permute-start | bytes 786440 | tf_op jit(solution)/shard_map/ppermute | solution.py:309
  36.1 0.0 collective-permute-done.11.came
  36.1 0.1 core_sum.1
  36.2 1.6 %collective-permute-start.15 = (f32[104,512]{1,0:T(8,128)S(1)}, f32[104,512]{1,0:T(8,128)S(1)}, u32[]{:S(2)}, u32[]{:S(2)}) collective-permute-start(f32[104,512]{1,0:T(8,128)S(1)} %get-tuple-element.93), channel_id=1, source_target_pairs={{0,2},{2,0},{4,6},{6,4},{8,10},{10,8},{12,14},{14,12},{1,3},{3,1},... | collective-permute-start | bytes 638984 | tf_op jit(solution)/shard_map/ppermute | solution.py:309
  37.7 0.5 collective-permute-start.12
  38.3 6.1 %collective-permute-done.15.came = f32[104,512]{1,0:T(8,128)S(1)} collective-permute-done((f32[104,512]{1,0:T(8,128)S(1)}, f32[104,512]{1,0:T(8,128)S(1)}, u32[]{:S(2)}, u32[]{:S(2)}) %collective-permute-start.15) | collective-permute-done | bytes 213024 | tf_op jit(solution)/shard_map/ppermute | solution.py:309
  44.4 2.6 %collective-permute-start.16 = (f32[56,512]{1,0:T(8,128)S(1)}, f32[56,512]{1,0:T(8,128)S(1)}, u32[]{:S(2)}, u32[]{:S(2)}) collective-permute-start(f32[56,512]{1,0:T(8,128)S(1)} %get-tuple-element.95), channel_id=1, source_target_pairs={{0,4},{2,6},{4,0},{6,2},{8,12},{10,14},{12,8},{14,10},{1,5},{3,7},... | collective-permute-start | bytes 344072 | tf_op jit(solution)/shard_map/ppermute | solution.py:309
  46.9 1.8 %collective-permute-done.14.force_came = f32[2,128,256]{2,1,0:T(8,128)S(1)} collective-permute-done((f32[2,128,256]{2,1,0:T(8,128)S(1)}, f32[2,128,256]{2,1,0:T(8,128)S(1)}, u32[]{:S(2)}, u32[]{:S(2)}) %collective-permute-start.14) | collective-permute-done | bytes 262176 | tf_op jit(solution)/shard_map/ppermute | solution.py:309
  48.7 0.0 collective-permute-start.17
  48.7 1.2 %collective-permute-done.17.rest_0_ = f32[8,128]{1,0:T(8,128)S(1)} collective-permute-done((f32[8,128]{1,0:T(8,128)S(1)}, f32[8,128]{1,0:T(8,128)S(1)}, u32[]{:S(2)}, u32[]{:S(2)}) %collective-permute-start.17) | collective-permute-done | bytes 4128 | tf_op jit(solution)/shard_map/ppermute | solution.py:309
  49.9 1.2 %collective-permute-done.16.b = f32[56,512]{1,0:T(8,128)S(1)} collective-permute-done((f32[56,512]{1,0:T(8,128)S(1)}, f32[56,512]{1,0:T(8,128)S(1)}, u32[]{:S(2)}, u32[]{:S(2)}) %collective-permute-start.16) | collective-permute-done | bytes 114720 | tf_op jit(solution)/shard_map/ppermute | solution.py:309
  51.1 1.7 %collective-permute-start.18 = (f32[56,512]{1,0:T(8,128)S(1)}, f32[56,512]{1,0:T(8,128)S(1)}, u32[]{:S(2)}, u32[]{:S(2)}) collective-permute-start(f32[56,512]{1,0:T(8,128)S(1)} %far_z.1.beyond), channel_id=1, source_target_pairs={{0,8},{2,10},{4,12},{6,14},{8,0},{10,2},{12,4},{14,6},{1,9},{3,11}... | collective-permute-start | bytes 344072 | tf_op jit(solution)/shard_map/ppermute | solution.py:309
  52.8 0.0 collective-permute-done.12.came
  52.8 2.5 %collective-permute-start.13 = (f32[48,512]{1,0:T(8,128)S(1)}, f32[48,512]{1,0:T(8,128)S(1)}, u32[]{:S(2)}, u32[]{:S(2)}) collective-permute-start(f32[48,512]{1,0:T(8,128)S(1)} %get-tuple-element.87), channel_id=1, source_target_pairs={{0,4},{2,6},{4,0},{6,2},{8,12},{10,14},{12,8},{14,10},{1,5},{3,7},... | collective-permute-start | bytes 294920 | tf_op jit(solution)/shard_map/ppermute | solution.py:309
  55.4 3.2 %collective-permute-done.13.b = f32[48,512]{1,0:T(8,128)S(1)} collective-permute-done((f32[48,512]{1,0:T(8,128)S(1)}, f32[48,512]{1,0:T(8,128)S(1)}, u32[]{:S(2)}, u32[]{:S(2)}) %collective-permute-start.13) | collective-permute-done | bytes 98336 | tf_op jit(solution)/shard_map/ppermute | solution.py:309
  58.6 0.8 %near_z.1 = (f32[1,8192]{1,0:T(1,128)S(1)}, f32[1,16384]{1,0:T(1,128)S(1)}, f32[2,2,128,256]{3,2,1,0:T(8,128)}) custom-call(f32[48,512]{1,0:T(8,128)S(1)} %get-tuple-element.86.a, f32[48,512]{1,0:T(8,128)S(1)} %collective-permute-done.13.b, f32[2,128,256]{2,1,0:T(8,128)S(1)} %get-tuple-element.88.force_near, ...), custom_call_target="tpu_custom_call" | custom-call | flops 1 | bytes 1 | tf_op jit(solution)/shard_map/near_z/pallas_call | solution.py:428
  59.4 0.2 collective-permute-done.18.came
  59.6 0.0 copy-done.2
  59.6 0.0 copy-done.3
  59.6 0.1 copy-done.4
  59.7 0.0 copy-done.6
  59.7 0.8 %final.1 = (f32[2,8192]{1,0:T(2,128)}, f32[2,16384]{1,0:T(2,128)}, f32[3,2,512]{2,1,0:T(2,128)}, f32[2,8192]{1,0:T(2,128)}, f32[2,16384]{1,0:T(2,128)}, /*index=5*/f32[3,2,512]{2,1,0:T(2,128)}, f32[1,128]{1,0:T(1,128)}) custom-call(f32[1,8192]{1,0:T(1,128)S(1)} %get-tuple-element.90.mine_first, f32[1,16384]{1,0:T(1,128)S(1)} %get-tuple-element.91.mine_second, ...), custom_call_target="tpu_custom_call" | custom-call | flops 1 | bytes 1 | tf_op jit(solution)/shard_map/final/pallas_call | solution.py:443
  (28 shorter events, 0.3 us)
Async XLA Ops:
  0.6 1.0 %copy-start.1 = (f32[2,16384]{1,0:T(2,128)S(1)}, f32[2,16384]{1,0:T(2,128)}, u32[]{:S(2)}) copy-start(f32[2,16384]{1,0:T(2,128)} %second.1) | copy-start | bytes 393220
  0.6 5.2 %copy-start = (f32[2,2,128,256]{3,2,1,0:T(8,128)S(1)}, f32[2,2,128,256]{3,2,1,0:T(8,128)}, u32[]{:S(2)}) copy-start(f32[2,2,128,256]{3,2,1,0:T(8,128)} %desc_ref.1) | copy-start | bytes 1572868
  1.6 4.2 %copy-start.5 = (f32[2,3,512]{2,0,1:T(2,128)S(1)}, f32[2,3,512]{2,0,1:T(2,128)}, u32[]{:S(2)}) copy-start(f32[2,3,512]{2,0,1:T(2,128)} %param.16) | copy-start | bytes 36868
  1.7 4.1 %copy-start.7 = (s32[2,2,128]{2,1,0:T(2,128)S(1)}, s32[2,2,128]{2,1,0:T(2,128)}, u32[]{:S(2)}) copy-start(s32[2,2,128]{2,1,0:T(2,128)} %ids_hbm.1) | copy-start | bytes 6148
  1.7 8.9 %collective-permute-start.4 = (f32[48,512]{1,0:T(8,128)S(1)}, f32[48,512]{1,0:T(8,128)S(1)}, u32[]{:S(2)}, u32[]{:S(2)}) collective-permute-start(f32[48,512]{1,0:T(8,128)S(1)} %get-tuple-element.110), channel_id=1, source_target_pairs={{0,8},{2,10},{4,12},{6,14},{8,0},{10,2},{12,4},{14,6},{1,9},{3,11}... | collective-permute-start | bytes 294920 | tf_op jit(solution)/shard_map/ppermute | solution.py:309
  5.8 0.7 %copy-start.8 = (s32[2,2]{1,0:T(2,128)S(1)}, s32[2,2]{1,0:T(2,128)}, u32[]{:S(2)}) copy-start(s32[2,2]{1,0:T(2,128)} %counts_hbm.1) | copy-start | bytes 52
  5.8 0.7 %copy-start.9 = (f32[32]{0:T(128)S(1)}, f32[32]{0:T(128)}, u32[]{:S(2)}) copy-start(f32[32]{0:T(128)} %param.13) | copy-start | bytes 388
  6.7 5.9 %collective-permute-start.2 = (f32[48,512]{1,0:T(8,128)S(1)}, f32[48,512]{1,0:T(8,128)S(1)}, u32[]{:S(2)}, u32[]{:S(2)}) collective-permute-start(f32[48,512]{1,0:T(8,128)S(1)} %get-tuple-element.61), channel_id=1, source_target_pairs={{0,4},{2,6},{4,0},{6,2},{8,12},{10,14},{12,8},{14,10},{1,5},{3,7},... | collective-permute-start | bytes 294920 | tf_op jit(solution)/shard_map/ppermute | solution.py:309
  8.4 8.8 %collective-permute-start = (f32[136,256]{1,0:T(8,128)S(1)}, f32[136,256]{1,0:T(8,128)S(1)}, u32[]{:S(2)}, u32[]{:S(2)}) collective-permute-start(f32[136,256]{1,0:T(8,128)S(1)} %get-tuple-element.57), channel_id=1, source_target_pairs={{0,8},{2,10},{4,12},{6,14},{8,0},{10,2},{12,4},{14,6},{1,9},{3,11}... | collective-permute-start | bytes 417800 | tf_op jit(solution)/shard_map/ppermute | solution.py:309
  10.6 8.2 %collective-permute-start.6 = (f32[48,512]{1,0:T(8,128)S(1)}, f32[48,512]{1,0:T(8,128)S(1)}, u32[]{:S(2)}, u32[]{:S(2)}) collective-permute-start(f32[48,512]{1,0:T(8,128)S(1)} %collective-permute-done.4), channel_id=1, source_target_pairs={{0,4},{2,6},{4,0},{6,2},{8,12},{10,14},{12,8},{14,10},{1,5},{3,7},... | collective-permute-start | bytes 294920 | tf_op jit(solution)/shard_map/ppermute | solution.py:309
  12.7 7.7 %collective-permute-start.3 = (f32[96,512]{1,0:T(8,128)S(1)}, f32[96,512]{1,0:T(8,128)S(1)}, u32[]{:S(2)}, u32[]{:S(2)}) collective-permute-start(f32[96,512]{1,0:T(8,128)S(1)} %pad_maximum_fusion.2), channel_id=1, source_target_pairs={{0,2},{2,0},{4,6},{6,4},{8,10},{10,8},{12,14},{14,12},{1,3},{3,1},... | collective-permute-start | bytes 589832 | tf_op jit(solution)/shard_map/ppermute | solution.py:309
  17.2 5.0 %collective-permute-start.1 = (f32[128,256]{1,0:T(8,128)S(1)}, f32[128,256]{1,0:T(8,128)S(1)}, u32[]{:S(2)}, u32[]{:S(2)}) collective-permute-start(f32[128,256]{1,0:T(8,128)S(1)} %slice.57.first_far), channel_id=1, source_target_pairs={{0,16},{16,0},{1,17},{17,1},{2,18},{18,2},{3,19},{19,3},{4,20},{20... | collective-permute-start | bytes 393224 | tf_op jit(solution)/shard_map/ppermute | solution.py:309
  18.8 5.8 %collective-permute-start.7 = (f32[96,512]{1,0:T(8,128)S(1)}, f32[96,512]{1,0:T(8,128)S(1)}, u32[]{:S(2)}, u32[]{:S(2)}) collective-permute-start(f32[96,512]{1,0:T(8,128)S(1)} %constant_dynamic-update-slice_fusion.4), channel_id=1, source_target_pairs={{0,2},{2,0},{4,6},{6,4},{8,10},{10,8},{12,14},{14,12},{1,3},{3,1},... | collective-permute-start | bytes 589832 | tf_op jit(solution)/shard_map/ppermute | solution.py:309
  20.4 4.3 %collective-permute-start.8 = (f32[96,512]{1,0:T(8,128)S(1)}, f32[96,512]{1,0:T(8,128)S(1)}, u32[]{:S(2)}, u32[]{:S(2)}) collective-permute-start(f32[96,512]{1,0:T(8,128)S(1)} %constant_dynamic-update-slice_fusion.4), channel_id=1, source_target_pairs={{0,1},{1,0},{2,3},{3,2},{4,5},{5,4},{6,7},{7,6},{8,9},{9,8},{10,11... | collective-permute-start | bytes 589832 | tf_op jit(solution)/shard_map/ppermute | solution.py:309
  20.5 5.7 %collective-permute-start.5 = (f32[192,512]{1,0:T(8,128)S(1)}, f32[192,512]{1,0:T(8,128)S(1)}, u32[]{:S(2)}, u32[]{:S(2)}) collective-permute-start(f32[192,512]{1,0:T(8,128)S(1)} %constant_dynamic-update-slice_fusion.own0), channel_id=1, source_target_pairs={{0,1},{1,0},{2,3},{3,2},{4,5},{5,4},{6,7},{7,6},{8,9},{9,8},{10,11... | collective-permute-start | bytes 1179656 | tf_op jit(solution)/shard_map/ppermute | solution.py:309
  24.7 1.4 %collective-permute-start.9 = (f32[96,512]{1,0:T(8,128)S(1)}, f32[96,512]{1,0:T(8,128)S(1)}, u32[]{:S(2)}, u32[]{:S(2)}) collective-permute-start(f32[96,512]{1,0:T(8,128)S(1)} %collective-permute-done.7), channel_id=1, source_target_pairs={{0,1},{1,0},{2,3},{3,2},{4,5},{5,4},{6,7},{7,6},{8,9},{9,8},{10,11... | collective-permute-start | bytes 589832 | tf_op jit(solution)/shard_map/ppermute | solution.py:309
  27.4 4.6 %collective-permute-start.10 = (f32[8,128]{1,0:T(8,128)S(1)}, f32[8,128]{1,0:T(8,128)S(1)}, u32[]{:S(2)}, u32[]{:S(2)}) collective-permute-start(f32[8,128]{1,0:T(8,128)S(1)} %get-tuple-element.68.mine), channel_id=1, source_target_pairs={{0,8},{2,10},{4,12},{6,14},{8,0},{10,2},{12,4},{14,6},{1,9},{3,11}... | collective-permute-start | bytes 12296 | tf_op jit(solution)/shard_map/ppermute | solution.py:309
  33.3 2.8 %collective-permute-start.11 = (f32[392,512]{1,0:T(8,128)S(1)}, f32[392,512]{1,0:T(8,128)S(1)}, u32[]{:S(2)}, u32[]{:S(2)}) collective-permute-start(f32[392,512]{1,0:T(8,128)S(1)} %get-tuple-element.83), channel_id=1, source_target_pairs={{0,1},{1,0},{2,3},{3,2},{4,5},{5,4},{6,7},{7,6},{8,9},{9,8},{10,11... | collective-permute-start | bytes 2408456 | tf_op jit(solution)/shard_map/ppermute | solution.py:309
  33.4 15.3 %collective-permute-start.14 = (f32[2,128,256]{2,1,0:T(8,128)S(1)}, f32[2,128,256]{2,1,0:T(8,128)S(1)}, u32[]{:S(2)}, u32[]{:S(2)}) collective-permute-start(f32[2,128,256]{2,1,0:T(8,128)S(1)} %get-tuple-element.89), channel_id=1, source_target_pairs={{0,8},{2,10},{4,12},{6,14},{8,0},{10,2},{12,4},{14,6},{1,9},{3,11}... | collective-permute-start | bytes 786440 | tf_op jit(solution)/shard_map/ppermute | solution.py:309
  36.2 8.2 %collective-permute-start.15 = (f32[104,512]{1,0:T(8,128)S(1)}, f32[104,512]{1,0:T(8,128)S(1)}, u32[]{:S(2)}, u32[]{:S(2)}) collective-permute-start(f32[104,512]{1,0:T(8,128)S(1)} %get-tuple-element.93), channel_id=1, source_target_pairs={{0,2},{2,0},{4,6},{6,4},{8,10},{10,8},{12,14},{14,12},{1,3},{3,1},... | collective-permute-start | bytes 638984 | tf_op jit(solution)/shard_map/ppermute | solution.py:309
  37.7 15.0 %collective-permute-start.12 = (f32[96,512]{1,0:T(8,128)S(1)}, f32[96,512]{1,0:T(8,128)S(1)}, u32[]{:S(2)}, u32[]{:S(2)}) collective-permute-start(f32[96,512]{1,0:T(8,128)S(1)} %get-tuple-element.85), channel_id=1, source_target_pairs={{0,2},{2,0},{4,6},{6,4},{8,10},{10,8},{12,14},{14,12},{1,3},{3,1},... | collective-permute-start | bytes 589832 | tf_op jit(solution)/shard_map/ppermute | solution.py:309
  44.4 6.7 %collective-permute-start.16 = (f32[56,512]{1,0:T(8,128)S(1)}, f32[56,512]{1,0:T(8,128)S(1)}, u32[]{:S(2)}, u32[]{:S(2)}) collective-permute-start(f32[56,512]{1,0:T(8,128)S(1)} %get-tuple-element.95), channel_id=1, source_target_pairs={{0,4},{2,6},{4,0},{6,2},{8,12},{10,14},{12,8},{14,10},{1,5},{3,7},... | collective-permute-start | bytes 344072 | tf_op jit(solution)/shard_map/ppermute | solution.py:309
  48.7 1.2 %collective-permute-start.17 = (f32[8,128]{1,0:T(8,128)S(1)}, f32[8,128]{1,0:T(8,128)S(1)}, u32[]{:S(2)}, u32[]{:S(2)}) collective-permute-start(f32[8,128]{1,0:T(8,128)S(1)} %slice_bitcast_fusion), channel_id=1, source_target_pairs={{0,1},{1,0},{2,3},{3,2},{4,5},{5,4},{6,7},{7,6},{8,9},{9,8},{10,11... | collective-permute-start | bytes 12296 | tf_op jit(solution)/shard_map/ppermute | solution.py:309
  51.1 8.5 %collective-permute-start.18 = (f32[56,512]{1,0:T(8,128)S(1)}, f32[56,512]{1,0:T(8,128)S(1)}, u32[]{:S(2)}, u32[]{:S(2)}) collective-permute-start(f32[56,512]{1,0:T(8,128)S(1)} %far_z.1.beyond), channel_id=1, source_target_pairs={{0,8},{2,10},{4,12},{6,14},{8,0},{10,2},{12,4},{14,6},{1,9},{3,11}... | collective-permute-start | bytes 344072 | tf_op jit(solution)/shard_map/ppermute | solution.py:309
  52.8 5.7 %collective-permute-start.13 = (f32[48,512]{1,0:T(8,128)S(1)}, f32[48,512]{1,0:T(8,128)S(1)}, u32[]{:S(2)}, u32[]{:S(2)}) collective-permute-start(f32[48,512]{1,0:T(8,128)S(1)} %get-tuple-element.87), channel_id=1, source_target_pairs={{0,4},{2,6},{4,0},{6,2},{8,12},{10,14},{12,8},{14,10},{1,5},{3,7},... | collective-permute-start | bytes 294920 | tf_op jit(solution)/shard_map/ppermute | solution.py:309
  58.5 1.0 %copy-start.2 = (f32[2,8192]{1,0:T(2,128)S(1)}, f32[2,8192]{1,0:T(2,128)}, u32[]{:S(2)}) copy-start(f32[2,8192]{1,0:T(2,128)} %first.1) | copy-start | bytes 196612
  58.5 1.1 %copy-start.3 = (f32[2,16384]{1,0:T(2,128)S(1)}, f32[2,16384]{1,0:T(2,128)}, u32[]{:S(2)}) copy-start(f32[2,16384]{1,0:T(2,128)} %second_mom.1) | copy-start | bytes 393220
  58.5 1.1 %copy-start.4 = (f32[2,8192]{1,0:T(2,128)S(1)}, f32[2,8192]{1,0:T(2,128)}, u32[]{:S(2)}) copy-start(f32[2,8192]{1,0:T(2,128)} %first_mom.1) | copy-start | bytes 196612
  58.5 1.1 %copy-start.6 = (f32[2,3,512]{2,0,1:T(2,128)S(1)}, f32[2,3,512]{2,0,1:T(2,128)}, u32[]{:S(2)}) copy-start(f32[2,3,512]{2,0,1:T(2,128)} %param.19) | copy-start | bytes 36868
